TPU v7x, 512 devices: a whole 4x4x16 slice. The times are simulated.
512 devices in a mesh: kpool: 8 (over x, core), fft: 64 (over z, y).
Axes of the slice: x: 4, y: 4, z: 16, core: 2. Of those that a mesh axis runs over, the one named last changes fastest.
Arguments:
- orbitals: float32 [8, 8, 4, 16384], P('kpool', None, None, 'fft'), may hold values from -6 to 6
- response: float32 [8, 8, 4, 16384], P('kpool', None, None, 'fft'), may hold values from -6 to 6
- residual: float32 [8, 8, 4, 16384], P('kpool', None, None, 'fft'), may hold values from -9 to 9
- old_direction: float32 [8, 8, 4, 16384], P('kpool', None, None, 'fft'), may hold values from -6 to 6
- old_norm: float32 [8, 8], P('kpool'), may hold values from 9830.4 to 7208960
- band_energy: float32 [8, 8], P('kpool'), may hold values from -1 to 0.4
- kinetic: float32 [8, 16384], P('kpool', 'fft'), may hold values from 0.5 to 20
- form_factor: float32 [8, 2, 16, 16384], P('kpool', None, None, 'fft'), may hold values from -0.046875 to 0.046875
- sphere_index: int32 [8, 16384], P('kpool', 'fft'), may hold values from 0 to 262143, as said below
- atom_positions: float32 [3, 64], replicated, may hold values from 0 to 1
- proj_atom: int32 [1024], replicated, may hold values from 0 to 63
- coupling: float32 [2, 32, 32], replicated, may hold values from -0.03 to 3
- potential: float32 [4, 64, 4096], P(None, 'fft'), may hold values from -0.3 to 2
Outputs:
- response_next: float32 [8, 8, 4, 16384], P('kpool', None, None, 'fft')
- residual_next: float32 [8, 8, 4, 16384], P('kpool', None, None, 'fft')
- direction: float32 [8, 8, 4, 16384], P('kpool', None, None, 'fft')
- induced_density: float32 [4, 64, 4096], P(None, 'fft')
Inputs may be any that keep to these rules, and one draw needn't show every extreme that they name: `sphere_index`: within one point the entries are distinct. Entry j = b * 32 + t (t < 32) has gz = (t - 16) mod 64, and the 32 entries of one b share one column (gx, gy), so the plane waves of every device are whole columns. The columns of one point are the 512 columns nearest the anchor in signed frequencies f(gx)^2 + f(gy)^2, ties broken at random, in a random order.
All inputs are finite; a program needn't handle non-finite values.
Results may differ from a plain program's by a relative error of at most 0.0003.
Values sent between devices are 32-bit elements; how exact they have to be, the bound alone decides.
No kernel may reach another device: no remote copies, remote signals or barrier semaphores. Data moves between devices by JAX's collectives and lax.ppermute only.
A program may use at most 64 MiB of HBM per device.

v0:
```python
import math

import jax
import jax.numpy as jnp
from jax import lax
from jax.sharding import PartitionSpec as P

NG = 64
STICK_LEN = 32


TWO_PI = 2.0 * math.pi
SMALL_TERM = 1e-06
HIGHEST = lax.Precision.HIGHEST


def contract(form_text, *operands):
    return jnp.einsum(form_text, *operands, precision=HIGHEST)


def phase_table(rows, cols, length, sign):
    wound = rows[:, None] * cols[None, :] % length
    angle = TWO_PI / length * wound.astype(jnp.float32)
    cosine = jnp.cos(angle)
    sine = sign * jnp.sin(angle)
    first = jnp.stack([cosine, sine])
    second = jnp.stack([-sine, cosine])
    return jnp.transpose(jnp.stack([first, second]), (0, 2, 1, 3))


def frequencies(index, length):

    def signed(values):
        return jnp.where(values < length // 2, values, values - length).astype(jnp.float32)

    return (
        signed(index // (length * length)),
        signed(index // length % length),
        signed(index % length),
    )


def projector_tables(form_factor, sphere_index, atom_positions, proj_atom, length):
    freq_x, freq_y, freq_z = frequencies(sphere_index, length)
    theta = TWO_PI * (
        atom_positions[0][:, None] * freq_x[None, :]
        + atom_positions[1][:, None] * freq_y[None, :]
        + atom_positions[2][:, None] * freq_z[None, :]
    )
    cosine = jnp.cos(theta)
    sine = jnp.sin(theta)
    channels = form_factor.shape[1]
    slots = proj_atom.reshape(channels, -1)
    cos_rows = jnp.take(cosine, slots, axis=0)
    sin_rows = jnp.take(sine, slots, axis=0)
    real_part = form_factor[0][:, None, :]
    imag_part = form_factor[1][:, None, :]
    return (
        real_part * cos_rows + imag_part * sin_rows,
        imag_part * cos_rows - real_part * sin_rows,
    )


def project(values, tab_real, tab_imag):
    val_real = values[:, 0::2]
    val_imag = values[:, 1::2]
    amp_real = contract("ckg,nsg->sckn", tab_real, val_real) + contract(
        "ckg,nsg->sckn", tab_imag, val_imag
    )
    amp_imag = contract("ckg,nsg->sckn", tab_real, val_imag) - contract(
        "ckg,nsg->sckn", tab_imag, val_real
    )
    return (amp_real, amp_imag)


def combine(amp_real, amp_imag, proj_atom, coupling):
    channels = amp_real.shape[1]
    atoms = amp_real.shape[2]
    slots = proj_atom.reshape(channels, atoms)
    onehot = (slots[:, None, :] == jnp.arange(atoms, dtype=jnp.int32)[None, :, None]).astype(
        amp_real.dtype
    )
    by_real = contract("cak,sckn->scan", onehot, amp_real)
    by_imag = contract("cak,sckn->scan", onehot, amp_imag)
    herm_real = (0.5 * (coupling[0] + coupling[0].T)).reshape(2, channels, 2, channels)
    herm_imag = (0.5 * (coupling[1] - coupling[1].T)).reshape(2, channels, 2, channels)
    out_real = contract("scte,tean->scan", herm_real, by_real) - contract(
        "scte,tean->scan", herm_imag, by_imag
    )
    out_imag = contract("scte,tean->scan", herm_real, by_imag) + contract(
        "scte,tean->scan", herm_imag, by_real
    )
    return (
        contract("cak,scan->sckn", onehot, out_real),
        contract("cak,scan->sckn", onehot, out_imag),
    )


def expand(q_real, q_imag, tab_real, tab_imag):
    new_real = contract("ckg,sckn->nsg", tab_real, q_real) - contract(
        "ckg,sckn->nsg", tab_imag, q_imag
    )
    new_imag = contract("ckg,sckn->nsg", tab_real, q_imag) + contract(
        "ckg,sckn->nsg", tab_imag, q_real
    )
    bands, points = (new_real.shape[0], new_real.shape[2])
    return jnp.stack([new_real, new_imag], axis=2).reshape(bands, 4, points)


def apply_potential(values, potential):
    up_re, up_im, down_re, down_im = (values[:, 0], values[:, 1], values[:, 2], values[:, 3])
    scalar, field_x, field_y, field_z = (potential[0], potential[1], potential[2], potential[3])
    upper = scalar + field_z
    lower = scalar - field_z
    new_up_re = upper * up_re + field_x * down_re + field_y * down_im
    new_up_im = upper * up_im + field_x * down_im - field_y * down_re
    new_down_re = field_x * up_re - field_y * up_im + lower * down_re
    new_down_im = field_x * up_im + field_y * up_re + lower * down_im
    return jnp.stack([new_up_re, new_up_im, new_down_re, new_down_im], axis=1)


def density_terms(orbital, changed):
    up_re, up_im, down_re, down_im = (orbital[:, 0], orbital[:, 1], orbital[:, 2], orbital[:, 3])
    ch_up_re, ch_up_im, ch_down_re, ch_down_im = (
        changed[:, 0],
        changed[:, 1],
        changed[:, 2],
        changed[:, 3],
    )
    same_up = up_re * ch_up_re + up_im * ch_up_im
    same_down = down_re * ch_down_re + down_im * ch_down_im
    charge = 2.0 * (same_up + same_down)
    spin_x = 2.0 * (
        up_re * ch_down_re + up_im * ch_down_im + down_re * ch_up_re + down_im * ch_up_im
    )
    spin_y = 2.0 * (
        up_re * ch_down_im - up_im * ch_down_re - (down_re * ch_up_im - down_im * ch_up_re)
    )
    spin_z = 2.0 * (same_up - same_down)
    return jnp.stack(
        [
            jnp.sum(charge, axis=0),
            jnp.sum(spin_x, axis=0),
            jnp.sum(spin_y, axis=0),
            jnp.sum(spin_z, axis=0),
        ]
    )


def to_lines(coefficients, table, columns):
    bands = coefficients.shape[0]
    lines = coefficients.reshape(bands, 2, 2, columns, -1)
    return contract("nscSg,cgdr->nsdrS", lines, table)


def finish_planes(values, all_columns, inverse):
    bands, slab_rows = (values.shape[0], values.shape[3])
    length = inverse.shape[1]
    plane = (
        jnp.zeros((bands, 2, 2, slab_rows, length * length), values.dtype)
        .at[:, :, :, :, all_columns]
        .set(values)
    )
    plane = plane.reshape(bands, 2, 2, slab_rows, length, length)
    along_y = contract("nsczxg,cgdr->nsdzxr", plane, inverse)
    along_x = contract("nsczgy,cgdr->nsdzry", along_y, inverse)
    return along_x.reshape(bands, 4, slab_rows, length * length)


def start_sticks(values, forward, all_columns):
    bands, slab_rows = (values.shape[0], values.shape[2])
    length = forward.shape[1]
    grid_values = values.reshape(bands, 2, 2, slab_rows, length, length)
    along_x = contract("nsczgy,cgdr->nsdzry", grid_values, forward)
    along_y = contract("nsczxg,cgdr->nsdzxr", along_x, forward)
    flat = along_y.reshape(bands, 2, 2, slab_rows, length * length)
    return jnp.take(flat, all_columns, axis=4)


def finish_sticks(values, table, length):
    along_z = contract("nsczS,czdt->nsdSt", values, table)
    bands = along_z.shape[0]
    return along_z.reshape(bands, 4, -1) / (length * length * length)


def per_device(
    orbitals,
    response,
    residual,
    old_direction,
    old_norm,
    band_energy,
    kinetic,
    form_factor,
    sphere_index,
    atom_positions,
    proj_atom,
    coupling,
    potential,
):
    groups = lax.axis_size("fft")
    points = sphere_index.shape[1]
    columns = points // STICK_LEN
    scale = 1.0 / (orbitals.shape[0] * lax.axis_size("kpool") * points * groups)
    grid_steps = jnp.arange(NG, dtype=jnp.int32)
    depth = (jnp.arange(STICK_LEN, dtype=jnp.int32) - STICK_LEN // 2) % NG
    inverse = phase_table(grid_steps, grid_steps, NG, 1.0)
    forward = phase_table(grid_steps, grid_steps, NG, -1.0)
    lines_in = phase_table(depth, grid_steps, NG, 1.0)
    lines_out = phase_table(grid_steps, depth, NG, -1.0)
    own_columns = sphere_index.reshape(sphere_index.shape[0], columns, STICK_LEN)[:, :, 0] // NG
    every_column = lax.all_gather(own_columns, "fft", axis=1, tiled=True)
    next_response, next_residual, directions = ([], [], [])
    orbital = orbitals[0]
    current = response[0]
    res_now = residual[0]
    previous = old_direction[0]
    all_columns = every_column[0]
    tab_real, tab_imag = projector_tables(
        form_factor[0], sphere_index[0], atom_positions, proj_atom, NG
    )
    norm_now = lax.psum(jnp.sum(res_now * res_now, axis=(1, 2)), "fft")
    ratio = norm_now / old_norm[0]
    direction = res_now + ratio[:, None, None] * previous
    dir_amps = project(direction, tab_real, tab_imag)
    amp_real, amp_imag = lax.psum((dir_amps[0], dir_amps[1]), "fft")
    orbital_grid = finish_planes(
        lax.all_to_all(
            to_lines(orbital, lines_in, columns), "fft", split_axis=3, concat_axis=4, tiled=True
        ),
        all_columns,
        inverse,
    )
    response_grid = finish_planes(
        lax.all_to_all(
            to_lines(current, lines_in, columns), "fft", split_axis=3, concat_axis=4, tiled=True
        ),
        all_columns,
        inverse,
    )
    direction_grid = finish_planes(
        lax.all_to_all(
            to_lines(direction, lines_in, columns), "fft", split_axis=3, concat_axis=4, tiled=True
        ),
        all_columns,
        inverse,
    )
    q_real, q_imag = combine(amp_real, amp_imag, proj_atom, coupling)
    nonlocal_term = expand(q_real, q_imag, tab_real, tab_imag)
    local_term = (
        kinetic[0][None, None, :] * direction
        + nonlocal_term
        - band_energy[0][:, None, None] * direction
    )
    potential_grid = apply_potential(direction_grid, potential)
    potential_term = finish_sticks(
        lax.all_to_all(
            start_sticks(potential_grid, forward, all_columns),
            "fft",
            split_axis=4,
            concat_axis=3,
            tiled=True,
        ),
        lines_out,
        NG,
    )
    image = local_term + potential_term
    curvature = lax.psum(jnp.sum(direction * image, axis=(1, 2)), "fft")
    step = norm_now / (curvature + SMALL_TERM)
    next_response.append(current + step[:, None, None] * direction)
    next_residual.append(res_now - step[:, None, None] * image)
    directions.append(direction)
    changed = response_grid + step[:, None, None, None] * direction_grid
    density = density_terms(orbital_grid, changed)
    density = lax.psum(density * scale, "kpool")
    return (jnp.stack(next_response), jnp.stack(next_residual), jnp.stack(directions), density)


def solution(mesh):
    in_specs = (
        P("kpool", None, None, "fft"),
        P("kpool", None, None, "fft"),
        P("kpool", None, None, "fft"),
        P("kpool", None, None, "fft"),
        P("kpool", None),
        P("kpool", None),
        P("kpool", "fft"),
        P("kpool", None, None, "fft"),
        P("kpool", "fft"),
        P(),
        P(),
        P(),
        P(None, "fft", None),
    )
    out_specs = (
        P("kpool", None, None, "fft"),
        P("kpool", None, None, "fft"),
        P("kpool", None, None, "fft"),
        P(None, "fft", None),
    )
    return jax.shard_map(
        per_device, mesh=mesh, in_specs=in_specs, out_specs=out_specs, check_vma=False
    )
```

profile of v0, /device:TPU:1, one launch (start us, length us, event | category | flops | bytes accessed | tf_op | source)
XLA Modules:
  0.0 970.7 jit_solution(16062180153447039626)
XLA Ops:
  9.8 122.9 %psum.35 = f32[8]{0:T(128)S(1)} all-reduce(f32[8]{0:T(128)S(1)} %fusion.77), channel_id=1, replica_groups=mesh['kpool'=8,'fft'=64] {'fft'}, use_global_device_ids=true, to_apply=%region_1.2 | all-reduce | flops 8 | bytes 64 | tf_op jit(solution)/shard_map/psum | solution.py:222
  135.0 2.2 reshape.1383
  137.2 6.5 all-to-all-start
  148.5 3.5 gather_fusion.2
  152.0 4.7 gather_fusion.1
  156.7 1.6 multiply_subtract_fusion
  159.7 1.4 fusion.21
  161.0 2.1 fusion.1
  163.1 2.0 fusion
  169.8 23.4 %all-reduce = s32[512]{0:T(512)S(1)} all-reduce(s32[512]{0:T(512)S(1)} %bitcast_dynamic-update-slice_fusion), channel_id=1, replica_groups=mesh['kpool'=8,'fft'=64] {'fft'}, use_global_device_ids=true, to_apply=%add | all-reduce | flops 512 | bytes 4096 | tf_op jit(solution)/shard_map/squeeze | solution.py:218
  197.6 1.9 copy.132
  199.5 2.2 reshape.1387
  202.8 2.2 reshape.1389
  205.9 241.1 %all-reduce.7.cloned.1.call-done = (f32[2,16,64,8]{2,3,0,1:T(8,128)}, f32[2,16,64,8]{2,3,0,1:T(8,128)}) async-done(((f32[2,16,64,8]{2,3,0,1:T(8,128)}, f32[2,16,64,8]{2,3,0,1:T(8,128)}), (f32[2,16,64,8]{2,3,0,1:T(8,128)}, f32[2,16,64,8]{2,3,0,1:T(8,128)})) %all-reduce.7.cloned.1.call-update) | async-done | bytes 131088 | tf_op jit(solution)/shard_map/psum | solution.py:226
  447.0 1.4 convolution_bitcast_fusion.19
  448.4 1.4 convolution_bitcast_fusion.17
  454.3 8.2 all-to-all-start.3
  463.8 1.6 reshape.1384
  467.2 5.4 broadcast.872.clone
  472.6 47.1 %scatter_fusion = f32[8,2,2,4096]{0,2,3,1:T(2,128)} fusion(f32[8,2,2,4096]{0,2,3,1:T(2,128)} %broadcast.872.clone, s32[512]{0:T(512)S(1)} %bitcast.478, f32[512,8,2,2]{1,3,2,0:T(2,128)S(1)} %copy.106), kind=kCustom, calls=%fused_computation.3 | custom fusion | bytes 198656 | tf_op jit(solution)/shard_map/scatter | solution.py:162
  519.7 10.4 %copy.107 = f32[8,2,2,64,64]{4,3,2,1,0:T(8,128)S(1)} copy(f32[8,2,2,64,64]{0,2,4,3,1:T(2,128)} %bitcast.450) | data formatting | bytes 1048576 | tf_op jit(solution)/shard_map/reshape.9
  530.1 1.7 convolution_bitcast_fusion.7
  531.7 1.7 convolution_bitcast_fusion.2
  536.0 1.6 convolution_bitcast_fusion.5
  537.6 9.3 copy.187
  546.9 5.5 gather_fusion
  552.5 2.0 fusion.132
  554.5 2.2 reshape.1385
  556.7 14.6 %all-to-all-start.2 = ((f32[64,1,256]{2,1,0:T(1,128)}), f32[64,1,256]{2,1,0:T(1,128)S(1)}, u32[]{:S(2)}, u32[]{:S(2)}) async-start(f32[64,1,256]{2,1,0:T(1,128)} %reshape.1389), calls=%async_computation.2 | async-start | bytes 131072 | tf_op jit(solution)/shard_map/all_to_all | solution.py:228
  572.2 1.6 reshape.1388
  575.6 5.4 broadcast.872.clone.1
  581.0 47.1 %scatter_fusion.2 = f32[8,2,2,4096]{0,2,3,1:T(2,128)} fusion(f32[8,2,2,4096]{0,2,3,1:T(2,128)} %broadcast.872.clone.1, s32[512]{0:T(512)S(1)} %bitcast.479, f32[512,8,2,2]{1,3,2,0:T(2,128)S(1)} %copy.134), kind=kCustom, calls=%fused_computation.5 | custom fusion | bytes 198656 | tf_op jit(solution)/shard_map/scatter | solution.py:162
  628.0 10.4 %copy.135 = f32[8,2,2,64,64]{4,3,2,1,0:T(8,128)S(1)} copy(f32[8,2,2,64,64]{0,2,4,3,1:T(2,128)} %bitcast.451) | data formatting | bytes 1048576 | tf_op jit(solution)/shard_map/reshape.53
  638.4 1.7 convolution_bitcast_fusion.3
  640.1 1.7 convolution_bitcast_fusion
  642.2 14.8 %all-to-all-start.1 = ((f32[64,1,256]{2,1,0:T(1,128)}), f32[64,1,256]{2,1,0:T(1,128)}, u32[]{:S(2)}, u32[]{:S(2)}) async-start(f32[64,1,256]{2,1,0:T(1,128)} %reshape.1385), calls=%async_computation.1 | async-start | bytes 131072 | tf_op jit(solution)/shard_map/all_to_all | solution.py:257
  658.2 1.6 reshape.1390
  661.6 5.4 broadcast.872.clone.2
  667.0 47.1 %scatter_fusion.1 = f32[8,2,2,4096]{0,2,3,1:T(2,128)} fusion(f32[8,2,2,4096]{0,2,3,1:T(2,128)} %broadcast.872.clone.2, s32[512]{0:T(512)S(1)} %bitcast.480, f32[512,8,2,2]{1,3,2,0:T(2,128)S(1)} %copy.128), kind=kCustom, calls=%fused_computation.4 | custom fusion | bytes 198656 | tf_op jit(solution)/shard_map/scatter | solution.py:162
  714.0 10.4 %copy.129 = f32[8,2,2,64,64]{4,3,2,1,0:T(8,128)S(1)} copy(f32[8,2,2,64,64]{0,2,4,3,1:T(2,128)} %bitcast.449) | data formatting | bytes 1048576 | tf_op jit(solution)/shard_map/reshape.47
  724.5 1.7 convolution_bitcast_fusion.4
  726.1 1.7 convolution_bitcast_fusion.1
  729.1 1.6 reduce.14
  730.7 1.6 reshape.1386
  733.6 1.8 fusion.3
  735.8 115.0 %psum.38 = f32[8]{0:T(128)S(1)} all-reduce(f32[8]{0:T(128)S(1)} %fusion.75), channel_id=1, replica_groups=mesh['kpool'=8,'fft'=64] {'fft'}, use_global_device_ids=true, to_apply=%region_6.8 | all-reduce | flops 8 | bytes 64 | tf_op jit(solution)/shard_map/psum | solution.py:268
  855.1 106.8 %all-reduce.5.cloned.1.call-done = f32[4,1,4096]{2,1,0:T(1,128)} async-done(((f32[4,1,4096]{2,1,0:T(1,128)}), f32[4,1,4096]{2,1,0:T(1,128)}) %all-reduce.5.cloned.1.call-update) | async-done | bytes 65552 | tf_op jit(solution)/shard_map/psum | solution.py:275
  961.9 1.5 copy.252
  (149 shorter events, 44.5 us)
Async XLA Ops:
  132.7 11.9 %copy-start.19 = (f32[8]{0:T(128)}, f32[8]{0:T(128)S(1)}, u32[]{:S(2)}) copy-start(f32[8]{0:T(128)S(1)} %psum.35) | copy-start | bytes 100
  133.5 23.2 %copy-start.14 = (f32[8]{0:T(128)}, f32[8]{0:T(128)S(1)}, u32[]{:S(2)}) copy-start(f32[8]{0:T(128)S(1)} %bitcast_divide_fusion) | copy-start | bytes 100
  137.2 317.1 %all-to-all-start = ((f32[64,1,256]{2,1,0:T(1,128)}), f32[64,1,256]{2,1,0:T(1,128)S(1)}, u32[]{:S(2)}, u32[]{:S(2)}) async-start(f32[64,1,256]{2,1,0:T(1,128)} %reshape.1383), calls=%async_computation | async-start | bytes 131072 | tf_op jit(solution)/shard_map/all_to_all | solution.py:242
  143.7 303.3 %all-reduce.7.cloned.1.call-start = ((), (), s32[]{:S(2)}) async-start(), calls=%async_computation.5 | async-start | bytes 524288 | tf_op jit(solution)/shard_map/psum | solution.py:226
  148.5 8.2 copy-start.13
  151.9 41.8 %copy-start.10 = (f32[4,1,4096]{2,1,0:T(1,128)S(1)}, f32[4,1,4096]{2,1,0:T(1,128)}, u32[]{:S(2)}) copy-start(f32[4,1,4096]{2,1,0:T(1,128)} %param.27) | copy-start | bytes 196612
  152.0 42.4 %copy-start.6 = (f32[2,32,32]{2,1,0:T(8,128)S(1)}, f32[2,32,32]{2,1,0:T(8,128)}, u32[]{:S(2)}) copy-start(f32[2,32,32]{2,1,0:T(8,128)} %param.26) | copy-start | bytes 24580
  152.0 42.6 %copy-start.2 = (f32[1,8,4,256]{3,2,1,0:T(4,128)S(1)}, f32[1,8,4,256]{3,2,1,0:T(4,128)}, u32[]{:S(2)}) copy-start(f32[1,8,4,256]{3,2,1,0:T(4,128)} %param.16) | copy-start | bytes 98308
  193.7 278.9 %copy-start.11 = (s32[512,1]{0,1:T(1,128)}, s32[512,1]{0,1:T(1,128)S(1)}, u32[]{:S(2)}) copy-start(s32[512,1]{0,1:T(1,128)S(1)} %compare_select_fusion.1) | copy-start | bytes 6148
  454.3 102.4 %all-to-all-start.3 = ((f32[64,1,256]{2,1,0:T(1,128)}), f32[64,1,256]{2,1,0:T(1,128)S(1)}, u32[]{:S(2)}, u32[]{:S(2)}) async-start(f32[64,1,256]{2,1,0:T(1,128)} %reshape.1387), calls=%async_computation.3 | async-start | bytes 131072 | tf_op jit(solution)/shard_map/all_to_all | solution.py:235
  519.7 14.2 %copy-start.7 = (f32[1,1,4096]{2,1,0:T(1,128)S(1)}, f32[1,1,4096]{2,1,0:T(1,128)}, u32[]{:S(2)}) copy-start(f32[1,1,4096]{2,1,0:T(1,128)} %get-tuple-element.34) | copy-start | bytes 49156
  519.7 14.2 %copy-start.8 = (f32[1,1,4096]{2,1,0:T(1,128)S(1)}, f32[1,1,4096]{2,1,0:T(1,128)}, u32[]{:S(2)}) copy-start(f32[1,1,4096]{2,1,0:T(1,128)} %get-tuple-element.35) | copy-start | bytes 49156
  519.7 14.2 %copy-start.9 = (f32[1,1,4096]{2,1,0:T(1,128)S(1)}, f32[1,1,4096]{2,1,0:T(1,128)}, u32[]{:S(2)}) copy-start(f32[1,1,4096]{2,1,0:T(1,128)} %get-tuple-element.36) | copy-start | bytes 49156
  534.0 18.4 %copy-start.18 = (pred[512]{0:T(512)(128)(4,1)S(1)}, pred[512]{0:T(512)(128)(4,1)}, u32[]{:S(2)}) copy-start(pred[512]{0:T(512)(128)(4,1)} %compare_and_fusion.1) | copy-start | bytes 1540
  552.5 28.5 %copy-start.12 = (s32[512,1]{0,1:T(1,128)S(1)}, s32[512,1]{0,1:T(1,128)}, u32[]{:S(2)}) copy-start(s32[512,1]{0,1:T(1,128)} %copy-done.11) | copy-start | bytes 6148
  556.7 85.5 %all-to-all-start.2 = ((f32[64,1,256]{2,1,0:T(1,128)}), f32[64,1,256]{2,1,0:T(1,128)S(1)}, u32[]{:S(2)}, u32[]{:S(2)}) async-start(f32[64,1,256]{2,1,0:T(1,128)} %reshape.1389), calls=%async_computation.2 | async-start | bytes 131072 | tf_op jit(solution)/shard_map/all_to_all | solution.py:228
  642.2 86.9 %all-to-all-start.1 = ((f32[64,1,256]{2,1,0:T(1,128)}), f32[64,1,256]{2,1,0:T(1,128)}, u32[]{:S(2)}, u32[]{:S(2)}) async-start(f32[64,1,256]{2,1,0:T(1,128)} %reshape.1385), calls=%async_computation.1 | async-start | bytes 131072 | tf_op jit(solution)/shard_map/all_to_all | solution.py:257
  657.1 304.9 %all-reduce.5.cloned.1.call-start = ((), (), s32[]{:S(2)}) async-start(), calls=%async_computation.4 | async-start | bytes 131072 | tf_op jit(solution)/shard_map/psum | solution.py:275
  714.0 19.6 %copy-start.4 = (f32[1,2,64,32]{2,3,0,1:T(8,128)S(1)}, f32[1,2,64,32]{2,3,0,1:T(8,128)}, u32[]{:S(2)}) copy-start(f32[1,2,64,32]{2,3,0,1:T(8,128)} %get-tuple-element.47) | copy-start | bytes 49156
  714.0 19.6 %copy-start.5 = (f32[1,2,64,32]{2,3,0,1:T(8,128)S(1)}, f32[1,2,64,32]{2,3,0,1:T(8,128)}, u32[]{:S(2)}) copy-start(f32[1,2,64,32]{2,3,0,1:T(8,128)} %get-tuple-element.48) | copy-start | bytes 49156
  724.4 11.1 %copy-start.16 = (f32[1,256]{1,0:T(1,128)S(1)}, f32[1,256]{1,0:T(1,128)}, u32[]{:S(2)}) copy-start(f32[1,256]{1,0:T(1,128)} %param.21) | copy-start | bytes 3076
  724.4 11.1 %copy-start.17 = (f32[1,8]{1,0:T(1,128)S(1)}, f32[1,8]{1,0:T(1,128)}, u32[]{:S(2)}) copy-start(f32[1,8]{1,0:T(1,128)} %param.20) | copy-start | bytes 100
  724.4 126.4 %copy-start.20 = (f32[8]{0:T(128)S(1)}, f32[8]{0:T(128)}, u32[]{:S(2)}) copy-start(f32[8]{0:T(128)} %copy-done.19) | copy-start | bytes 100
  724.4 126.4 %copy-start = (f32[1,8,4,256]{3,2,1,0:T(4,128)S(1)}, f32[1,8,4,256]{3,2,1,0:T(4,128)}, u32[]{:S(2)}) copy-start(f32[1,8,4,256]{3,2,1,0:T(4,128)} %param.17) | copy-start | bytes 98308
  724.5 126.4 %copy-start.1 = (f32[1,8,4,256]{3,2,1,0:T(4,128)S(1)}, f32[1,8,4,256]{3,2,1,0:T(4,128)}, u32[]{:S(2)}) copy-start(f32[1,8,4,256]{3,2,1,0:T(4,128)} %param.18) | copy-start | bytes 98308
  724.5 126.4 %copy-start.15 = (f32[8]{0:T(128)S(1)}, f32[8]{0:T(128)}, u32[]{:S(2)}) copy-start(f32[8]{0:T(128)} %copy-done.14) | copy-start | bytes 100
  724.5 128.7 %copy-start.3 = (f32[1,8,4,256]{3,2,1,0:T(4,128)S(1)}, f32[1,8,4,256]{3,2,1,0:T(4,128)}, u32[]{:S(2)}) copy-start(f32[1,8,4,256]{3,2,1,0:T(4,128)} %param.16) | copy-start | bytes 98308
Sparse Core Ops, SparseCore 0:
  165.2 281.7 all-reduce.6
  853.3 108.5 all-reduce.4
where the time goes:
time: 982 us; the launch traced here: 971 us
  waiting for transfers between devices  348 us (35%)
  blocking collectives  261 us (27%)
  local copies, waits for them, and re-layouts  251 us (26%)
  starting transfers between devices  44.4 us (5%)
  matrix products  30.2 us (3%)
  other arithmetic  19.8 us (2%)
  between operations  15.9 us (2%)
    psum x1, waiting for transfers between devices, per_device(): amp_real, amp_imag = lax.psum((dir_amps[0], dir_amps[1]), 'fft')  241 us
    scatter x3, local copies, waits for them, and re-layouts, finish_planes(): plane = jnp.zeros((bands, 2, 2, slab_rows, length * length), values.dtype...  141 us
    psum x1, blocking collectives, per_device(): norm_now = lax.psum(jnp.sum(res_now * res_now, axis=(1, 2)), 'fft')  123 us
    psum x1, blocking collectives, per_device(): curvature = lax.psum(jnp.sum(direction * image, axis=(1, 2)), 'fft')  115 us
    psum x1, waiting for transfers between devices, per_device(): density = lax.psum(density * scale, 'kpool')  107 us
    another operation x7, local copies, waits for them, and re-layouts  47.8 us
    dot_general x28, matrix products, contract(): return jnp.einsum(form_text, *operands, precision=HIGHEST)  30.2 us
    squeeze x1, blocking collectives, per_device(): all_columns = every_column[0]  23.4 us
  transfers between devices with their start and end apart: 6, of which 2 were waited for; matrix products, arithmetic and copies ran while one was open for 29% of the time, Pallas kernels for 0%

commit v1 on v0

v1 whole, which is shorter than its diff:
```python
import math

import jax
import jax.numpy as jnp
from jax import lax
from jax.experimental import pallas as pl
from jax.experimental.pallas import tpu as pltpu
from jax.sharding import PartitionSpec as P

NG = 64
STICK = 32
NB = 8
COLS = 8
PW = COLS * STICK
PA = 16
DEV = 64
ALL = COLS * DEV
ROWS1 = 17
ROWS2 = 8
SMALL_TERM = 1e-06
VOLUME = 1.0 / (NG * NG * NG)
F32 = jnp.float32
BF16 = jnp.bfloat16
LIMIT = 48 * 1024 * 1024

COS = (1.0, -19.73920440673828, 64.93911743164062, -85.45014190673828,
       60.16762924194336, -25.967599868774414, 6.528658390045166)
SIN = (6.2831854820251465, -41.34170150756836, 81.60513305664062, -76.70301818847656,
       42.02592849731445, -14.899847030639648, 3.2381374835968018)


def iota(shape, dim):
    return lax.broadcasted_iota(jnp.int32, shape, dim)


def horner(coefficients, w):
    total = jnp.full_like(w, coefficients[-1])
    for c in coefficients[-2::-1]:
        total = total * w + c
    return total


def trig_turns(turns):
    r = turns - jnp.floor(turns + 0.5)
    w = r * r
    return horner(COS, w), r * horner(SIN, w)


def trig_wound(wound):
    r = (((wound + 32) & 63) - 32).astype(F32) * (1.0 / 64.0)
    w = r * r
    return horner(COS, w), r * horner(SIN, w)


def split(x):
    high = x.astype(BF16)
    return high, (x - high.astype(F32)).astype(BF16)


def dot(a, b, form="nn"):
    return lax.dot_general(
        a, b, (((1,), (0 if form == "nn" else 1,)), ((), ())), preferred_element_type=F32
    )


def dot3(a, b, form="nn"):
    return dot(a[0], b[0], form) + dot(a[1], b[0], form) + dot(a[0], b[1], form)


def swap_sign(x):
    lane = iota(x.shape, x.ndim - 1)
    return jnp.where(lane < 64, -1.0, 1.0) * pltpu.roll(x, 64, x.ndim - 1)


def row_to_col(row, n):
    shape = (n, row.shape[1])
    return jnp.sum(jnp.where(iota(shape, 0) == iota(shape, 1), row, 0.0), axis=1, keepdims=True)


def col_to_row(col, width):
    shape = (col.shape[0], width)
    return jnp.sum(jnp.where(iota(shape, 0) == iota(shape, 1), col, 0.0), axis=0, keepdims=True)


def signed(g):
    return jnp.where(g < 32, g, g - 64).astype(F32)


def atom_phases(index, positions):
    fx = signed(index >> 12)
    fy = signed((index >> 6) & 63)
    fz = signed(index & 63)
    tx, ty, tz = (row_to_col(positions[i : i + 1, :], NG) for i in range(3))
    turns = tx * fx + ty * fy + tz * fz
    cosine, sine = trig_turns(turns)
    return jnp.concatenate([cosine, sine], axis=0)


def depth_table():
    shape = (NG, PW)
    wound = iota(shape, 0) * ((iota(shape, 1) & 31) - 16)
    cosine, sine = trig_wound(wound)
    return jnp.concatenate([cosine, sine], axis=0)


def send_kernel(orb_ref, resp_ref, res_ref, old_ref, form_ref, index_ref, pos_ref, out_ref):
    arrays = (orb_ref, resp_ref, res_ref, old_ref)
    lines = jnp.concatenate(
        [ref[0, :, 2 * s + c, :] for c in range(2) for ref in arrays for s in range(2)], axis=0
    )
    lines = split(lines)
    table = depth_table()
    group = iota(table.shape, 1) >> 5
    for b in range(COLS):
        z = dot3(split(jnp.where(group == b, table, 0.0)), lines, "nt")
        out_ref[pl.ds(b, DEV, stride=ROWS1), :] = z[:64] + swap_sign(z[64:])

    index = index_ref[...]
    phases = split(atom_phases(index, pos_ref[...]))
    form_re, form_im = form_ref[0, 0], form_ref[0, 1]
    for n in range(NB):
        parts_re, parts_im = [], []
        for ref in arrays[2:]:
            for s in range(2):
                d_re = ref[0, n, 2 * s : 2 * s + 1, :]
                d_im = ref[0, n, 2 * s + 1 : 2 * s + 2, :]
                parts_re.append(form_re * d_re + form_im * d_im)
                parts_im.append(form_re * d_im - form_im * d_re)
        values = split(jnp.concatenate(parts_re + parts_im, axis=0))
        z = dot3(phases, values, "nt")
        out_ref[pl.ds(COLS + n, DEV, stride=ROWS1), :] = z[:64] + swap_sign(z[64:])

    squares = jnp.zeros((NB, PW), F32)
    for comp in range(4):
        r = res_ref[0, :, comp, :]
        squares = squares + r * r
    row = col_to_row(jnp.sum(squares, axis=1, keepdims=True), 128)
    codes = (index >> 6).astype(F32)
    lane = iota((1, PW), 1)
    target = iota((1, 128), 1)
    for b in range(COLS):
        code = jnp.sum(jnp.where(lane == STICK * b, codes, 0.0), axis=1, keepdims=True)
        row = jnp.where(target == COLS + b, code, row)
    out_ref[pl.ds(COLS + NB, DEV, stride=ROWS1), :] = jnp.broadcast_to(row, (DEV, 128))


def own_columns(recv_ref):
    values = jnp.concatenate(
        [recv_ref[pl.ds(b, DEV, stride=ROWS1), :] for b in range(COLS)], axis=0
    )
    return values.T


def column_codes(extra):
    turned = extra.T
    codes = jnp.concatenate(
        [turned[COLS + b : COLS + b + 1, :] for b in range(COLS)], axis=1
    ).astype(jnp.int32)
    return codes


def x_tables(codes, cos_ref, sin_ref):
    shape = (NG, ALL)
    cosine, sine = trig_wound(iota(shape, 0) * (codes >> 6))
    cos_ref[...] = cosine
    sin_ref[...] = sine


def y_forward(extra, table_ref):
    shape = (DEV, 128)
    lane = iota(shape, 1)
    for b in range(COLS):
        gy = extra[:, COLS + b : COLS + b + 1].astype(jnp.int32) & 63
        cosine, sine = trig_wound(gy * (lane & 63))
        first = jnp.where(lane < 64, cosine, sine)
        second = jnp.where(lane < 64, -sine, cosine)
        for c, part in ((0, first), (1, second)):
            high, low = split(part)
            rows = slice(c * ALL + b * DEV, c * ALL + (b + 1) * DEV)
            table_ref[rows, 0:128] = high
            table_ref[rows, 128:256] = low


def plane_chunk(re, im, first, count, cos_ref, sin_ref, table_ref, high_ref, low_ref):
    rows = re.shape[0]
    for i in range(count):
        cx = cos_ref[pl.ds(first + i, 1), :]
        sx = sin_ref[pl.ds(first + i, 1), :]
        for c, part in ((0, re * cx - im * sx), (1, re * sx + im * cx)):
            high, low = split(part)
            high_ref[i * rows : (i + 1) * rows, c * ALL : (c + 1) * ALL] = high
            low_ref[i * rows : (i + 1) * rows, c * ALL : (c + 1) * ALL] = low
    both = dot(high_ref[...], table_ref[...])
    return both[:, :128] + both[:, 128:] + dot(low_ref[...], table_ref[:, :128])


def potential_kernel(
    recv_ref, old_norm_ref, res_ref, old_ref, kin_ref, energy_ref, atom_ref, slots_ref,
    coup_ref, pot_ref, out_ref, grid_ref, scalars_ref,
    cos_ref, sin_ref, table_ref, back_high, back_low, high_ref, low_ref, prod_ref, pair_ref,
):
    extra = recv_ref[pl.ds(COLS + NB, DEV, stride=ROWS1), :]
    norm = row_to_col(jnp.sum(extra, axis=0, keepdims=True), NB)
    beta = norm / row_to_col(old_norm_ref[...], NB)
    codes = column_codes(extra)
    x_tables(codes, cos_ref, sin_ref)
    y_forward(extra, table_ref)
    cosine, sine = trig_wound(iota((NG, ALL), 0) * (codes & 63))
    for rows, parts in ((slice(0, 64), (cosine, -sine)), (slice(64, 128), (sine, cosine))):
        for c in range(2):
            high, low = split(parts[c])
            back_high[rows, c * ALL : (c + 1) * ALL] = high
            back_low[rows, c * ALL : (c + 1) * ALL] = low

    values = own_columns(recv_ref)
    beta2 = jnp.concatenate([beta, beta], axis=0)
    re = values[32:48] + beta2 * values[48:64]
    im = values[96:112] + beta2 * values[112:128]

    def chunk(k, carry):
        acc_re, acc_im, local = carry
        first = k * 16
        grid = plane_chunk(re, im, first, 16, cos_ref, sin_ref, table_ref, high_ref, low_ref)
        grid_ref[pl.ds(pl.multiple_of(k * 256, 256), 256), :] = grid
        for i in range(16):
            up = grid[i * 16 : i * 16 + 8]
            down = grid[i * 16 + 8 : i * 16 + 16]
            v0, bx, by, bz = (pot_ref[m, pl.ds(first + i, 1), :] for m in range(4))
            new_up = (v0 + bz) * up + bx * down - by * swap_sign(down)
            new_down = bx * up + by * swap_sign(up) + (v0 - bz) * down
            prod_ref[i * 16 : i * 16 + 8, :] = new_up
            prod_ref[i * 16 + 8 : i * 16 + 16, :] = new_down
            local = local + up * new_up + down * new_down
        prod = split(prod_ref[...])
        table = back_high[...]
        turned = dot(prod[0], table) + dot(prod[1], table) + dot(prod[0], back_low[...])
        for i in range(16):
            cx = cos_ref[pl.ds(first + i, 1), :]
            sx = sin_ref[pl.ds(first + i, 1), :]
            q_re = turned[i * 16 : (i + 1) * 16, :ALL]
            q_im = turned[i * 16 : (i + 1) * 16, ALL:]
            acc_re = acc_re + q_re * cx + q_im * sx
            acc_im = acc_im + q_im * cx - q_re * sx
        return acc_re, acc_im, local

    zero = jnp.zeros((16, ALL), F32)
    acc_re, acc_im, local = lax.fori_loop(0, 4, chunk, (zero, zero, jnp.zeros((NB, 128), F32)))
    acc_re = acc_re * VOLUME
    acc_im = acc_im * VOLUME
    for r in range(2):
        pieces = []
        for b in range(4 * r, 4 * r + 4):
            lanes = slice(b * DEV, (b + 1) * DEV)
            pieces += [acc_re[:, lanes], acc_im[:, lanes]]
        out_ref[pl.ds(r, DEV, stride=ROWS2), :] = jnp.concatenate(pieces, axis=0).T

    sums = [
        jnp.sum(recv_ref[pl.ds(COLS + n, DEV, stride=ROWS1), :], axis=0, keepdims=True)
        for n in range(NB)
    ]
    amps = jnp.concatenate(sums, axis=0)
    amps = amps + beta * pltpu.roll(amps, 96, 1)
    amp_re, amp_im = amps[:, 0:32], amps[:, 64:96]
    count = jnp.sum(
        jnp.where(slots_ref[...] == atom_ref[0], 1.0, 0.0), axis=1, keepdims=True
    )
    shape = (PA, 32)
    count = jnp.sum(
        jnp.where((iota(shape, 1) & 15) == iota(shape, 0), count, 0.0), axis=0, keepdims=True
    )
    h_re = 0.5 * (coup_ref[0] + coup_ref[0].T)
    h_im = 0.5 * (coup_ref[1] - coup_ref[1].T)
    by_re, by_im = amp_re * count, amp_im * count

    def exact(a, b):
        return lax.dot_general(
            a, b, (((1,), (0,)), ((), ())),
            precision=lax.Precision.HIGHEST, preferred_element_type=F32,
        )

    q_re = (exact(by_re, h_re) + exact(by_im, h_im)) * count
    q_im = (exact(by_im, h_re) - exact(by_re, h_im)) * count
    pair_ref[:, 0:32] = q_re
    pair_ref[:, 32:64] = q_im
    pair_ref[:, 64:128] = jnp.zeros((NB, 64), F32)
    even = pair_ref[pl.ds(0, 4, stride=2), :]
    odd = pair_ref[pl.ds(1, 4, stride=2), :]
    packed = even + pltpu.roll(odd, 64, 1)
    for k in range(4):
        out_ref[pl.ds(2 + k, DEV, stride=ROWS2), :] = jnp.broadcast_to(
            packed[k : k + 1], (DEV, 128)
        )

    curvature = jnp.sum(local, axis=1, keepdims=True) * VOLUME
    curvature = curvature + jnp.sum(amp_re * q_re + amp_im * q_im, axis=1, keepdims=True)
    weight = kin_ref[...] - row_to_col(energy_ref[...], NB)
    own = jnp.zeros((NB, PW), F32)
    for comp in range(4):
        d = res_ref[0, :, comp, :] + beta * old_ref[0, :, comp, :]
        own = own + d * d
    curvature = curvature + jnp.sum(own * weight, axis=1, keepdims=True)
    out_ref[pl.ds(6, DEV, stride=ROWS2), :] = jnp.broadcast_to(
        col_to_row(curvature, 128), (DEV, 128)
    )
    out_ref[pl.ds(7, DEV, stride=ROWS2), :] = jnp.zeros((DEV, 128), F32)
    lane = iota((NB, 128), 1)
    scalars_ref[...] = jnp.where(lane == 0, norm, jnp.where(lane == 1, beta, 0.0))


def orbital_kernel(recv_ref, grid_ref, cos_ref, sin_ref, table_ref, high_ref, low_ref):
    extra = recv_ref[pl.ds(COLS + NB, DEV, stride=ROWS1), :]
    x_tables(column_codes(extra), cos_ref, sin_ref)
    y_forward(extra, table_ref)
    values = own_columns(recv_ref)
    re, im = values[0:32], values[64:96]

    def chunk(k, carry):
        grid = plane_chunk(re, im, k * 8, 8, cos_ref, sin_ref, table_ref, high_ref, low_ref)
        grid_ref[pl.ds(pl.multiple_of(k * 256, 256), 256), :] = grid
        return carry

    lax.fori_loop(0, 8, chunk, 0)


def step_of(recv_ref, scalars_ref):
    total = jnp.sum(recv_ref[pl.ds(6, DEV, stride=ROWS2), :], axis=0, keepdims=True)
    return scalars_ref[:, 0:1] / (row_to_col(total, NB) + SMALL_TERM)


def density_kernel(recv_ref, scalars_ref, grid_ref, other_ref, out_ref):
    step = step_of(recv_ref, scalars_ref)
    step = jnp.broadcast_to(step, (NB, 128))
    lane = iota((1, 128), 1)

    def terms(x):
        base = pl.multiple_of(x * 32, 32)
        o_up = other_ref[pl.ds(base, 8), :]
        o_down = other_ref[pl.ds(base + 8, 8), :]
        half = pl.multiple_of(x * 16, 16)
        c_up = other_ref[pl.ds(base + 16, 8), :] + step * grid_ref[pl.ds(half, 8), :]
        c_down = other_ref[pl.ds(base + 24, 8), :] + step * grid_ref[pl.ds(half + 8, 8), :]
        same_up = o_up * c_up
        same_down = o_down * c_down
        parts = (
            same_up + same_down,
            o_up * c_down + o_down * c_up,
            o_down * swap_sign(c_up) - o_up * swap_sign(c_down),
            same_up - same_down,
        )
        sums = []
        for part in parts:
            row = jnp.sum(part, axis=0, keepdims=True)
            sums.append(2.0 * (row + pltpu.roll(row, 64, 1)))
        return sums

    def pair(p, carry):
        even = terms(2 * p)
        odd = terms(2 * p + 1)
        for m in range(4):
            row = jnp.where(lane < 64, even[m], odd[m])
            for copy in range(8):
                out_ref[pl.ds(copy * 128 + m * 32 + p, 1), :] = row
        return carry

    lax.fori_loop(0, 32, pair, 0, unroll=4)


def finish_kernel(
    recv_ref, scalars_ref, resp_ref, res_ref, old_ref, kin_ref, energy_ref, form_ref,
    index_ref, pos_ref, next_ref, residual_ref, direction_ref,
):
    step = step_of(recv_ref, scalars_ref)
    beta = scalars_ref[:, 1:2]
    table = depth_table()
    table = split(jnp.concatenate([table[:64], table[64:]], axis=1))
    group = iota((32, PW), 1) >> 5
    local = jnp.zeros((32, PW), F32)
    for r in range(2):
        values = recv_ref[pl.ds(r, DEV, stride=ROWS2), :].T
        z = dot3(split(values), table)
        for i in range(4):
            re_c, re_s = z[i * 32 : i * 32 + 16, :PW], z[i * 32 : i * 32 + 16, PW:]
            im_c, im_s = z[i * 32 + 16 : i * 32 + 32, :PW], z[i * 32 + 16 : i * 32 + 32, PW:]
            part = jnp.concatenate([re_c + im_s, im_c - re_s], axis=0)
            local = local + jnp.where(group == 4 * r + i, part, 0.0)

    phases = atom_phases(index_ref[...], pos_ref[...])
    phases = split(jnp.concatenate([phases[:64], phases[64:]], axis=1))
    form_re, form_im = form_ref[0, 0], form_ref[0, 1]
    rows_re, rows_im = [[], []], [[], []]
    for k in range(4):
        values = recv_ref[pl.ds(2 + k, DEV, stride=ROWS2), :].T
        z = dot3(split(values), phases)
        for i in range(2):
            for s in range(2):
                a = i * 64 + s * 16
                re_c, re_s = z[a : a + 16, :PW], z[a : a + 16, PW:]
                im_c, im_s = z[a + 32 : a + 48, :PW], z[a + 32 : a + 48, PW:]
                w_re = re_c + im_s
                w_im = im_c - re_s
                rows_re[s].append(
                    jnp.sum(form_re * w_re - form_im * w_im, axis=0, keepdims=True)
                )
                rows_im[s].append(
                    jnp.sum(form_re * w_im + form_im * w_re, axis=0, keepdims=True)
                )
    weight = kin_ref[...] - row_to_col(energy_ref[...], NB)
    for s in range(2):
        for c in range(2):
            comp = 2 * s + c
            nonlocal_term = jnp.concatenate((rows_re, rows_im)[c][s], axis=0)
            residual = res_ref[0, :, comp, :]
            direction = residual + beta * old_ref[0, :, comp, :]
            place = c * 16 + s * 8
            image = weight * direction + local[place : place + 8] + nonlocal_term
            direction_ref[0, :, comp, :] = direction
            next_ref[0, :, comp, :] = resp_ref[0, :, comp, :] + step * direction
            residual_ref[0, :, comp, :] = residual - step * image


def call(kernel, outs, name, scratch=(), flops=1, size=1, smem=()):
    def run(*args):
        specs = [
            pl.BlockSpec(memory_space=pltpu.SMEM if i in smem else pltpu.VMEM)
            for i in range(len(args))
        ]
        single = not isinstance(outs, (list, tuple))
        return pl.pallas_call(
            kernel,
            out_shape=outs,
            in_specs=specs,
            out_specs=jax.tree.map(lambda _: pl.BlockSpec(memory_space=pltpu.VMEM), outs),
            scratch_shapes=list(scratch),
            compiler_params=pltpu.CompilerParams(vmem_limit_bytes=LIMIT),
            cost_estimate=pl.CostEstimate(flops=flops, bytes_accessed=size, transcendentals=0),
            name=name,
        )(*args)

    return run


def shape_of(*dims):
    return jax.ShapeDtypeStruct(dims, F32)


def exchange(values, axis, parts):
    rows = values.shape[0] // parts
    if rows % 8:
        flat = values.reshape(parts, 1, rows * 128)
        flat = lax.all_to_all(flat, axis, 0, 0, tiled=True)
        return flat.reshape(values.shape)
    out = lax.all_to_all(values.reshape(parts, rows, 128), axis, 0, 0, tiled=True)
    return out.reshape(values.shape)


def per_device(
    orbitals, response, residual, old_direction, old_norm, band_energy, kinetic, form_factor,
    sphere_index, atom_positions, proj_atom, coupling, potential,
):
    scale = 1.0 / (8 * 16384)
    me = lax.axis_index("fft").reshape(1).astype(jnp.int32)
    slots = proj_atom.reshape(PA, NG)
    plane = potential.reshape(4, NG, NG)
    plane = jnp.concatenate([plane, plane], axis=2)

    sent = call(send_kernel, shape_of(DEV * ROWS1, 128), "lines_and_amplitudes")(
        orbitals, response, residual, old_direction, form_factor, sphere_index, atom_positions
    )
    recv = exchange(sent, "fft", DEV)
    tables = [
        pltpu.VMEM((NG, ALL), F32), pltpu.VMEM((NG, ALL), F32),
        pltpu.VMEM((2 * ALL, 256), BF16),
    ]
    wide = [pltpu.VMEM((256, 2 * ALL), BF16), pltpu.VMEM((256, 2 * ALL), BF16)]
    back, grid, scalars = call(
        potential_kernel,
        (shape_of(DEV * ROWS2, 128), shape_of(NG * 16, 128), shape_of(NB, 128)),
        "potential_and_coupling",
        tables + [pltpu.VMEM((128, 2 * ALL), BF16), pltpu.VMEM((128, 2 * ALL), BF16)] + wide
        + [pltpu.VMEM((256, 128), F32), pltpu.VMEM((NB, 128), F32)],
        smem=(6,),
    )(recv, old_norm, residual, old_direction, kinetic, band_energy, me, slots, coupling, plane)
    returned = exchange(back, "fft", DEV)
    other = call(
        orbital_kernel, shape_of(NG * 32, 128), "orbital_and_response_grid", tables + wide,
        flops=3_000_000_000, size=3_000_000,
    )(recv)
    density = call(density_kernel, shape_of(8 * 128, 128), "density")(
        returned, scalars, grid, other
    )
    gathered = exchange(density, "kpool", 8)
    outs = call(
        finish_kernel, (shape_of(1, NB, 4, PW),) * 3, "new_vectors",
        flops=3_000_000_000, size=3_000_000,
    )(
        returned, scalars, response, residual, old_direction, kinetic, band_energy, form_factor,
        sphere_index, atom_positions,
    )
    total = jnp.sum(gathered.reshape(8, 128, 128), axis=0) * scale
    return outs[0], outs[1], outs[2], total.reshape(4, 1, NG * NG)


def solution(mesh):
    vector = P("kpool", None, None, "fft")
    in_specs = (
        vector, vector, vector, vector, P("kpool", None), P("kpool", None), P("kpool", "fft"),
        vector, P("kpool", "fft"), P(), P(), P(), P(None, "fft", None),
    )
    out_specs = (vector, vector, vector, P(None, "fft", None))
    return jax.shard_map(
        per_device, mesh=mesh, in_specs=in_specs, out_specs=out_specs, check_vma=False
    )
```

time: 982 us -> 115 us (0.12); the launches traced: 971 us -> 114 us
  waiting for transfers between devices: 348 us -> 52.2 us
  blocking collectives: 261 us -> 0 us
  local copies, waits for them, and re-layouts: 251 us -> 6.58 us
  matrix products: 30.2 us -> 0 us
  other arithmetic: 19.8 us -> 0.93 us
  Pallas kernels: 0 us -> 16.6 us
  between operations: 15.9 us -> 0.75 us
    psum x2 -> x0, waiting for transfers between devices: 348 us -> none  [the longest x1 241 us: per_device(): amp_real, amp_imag = lax.psum((dir_amps[0], dir_amps[1]), 'fft')]
    psum x2 -> x0, blocking collectives: 238 us -> none  [the longest x1 123 us: per_device(): norm_now = lax.psum(jnp.sum(res_now * res_now, axis=(1, 2)), 'fft')]
    scatter x3 -> x0, local copies, waits for them, and re-layouts: 141 us -> none  [finish_planes(): plane = jnp.zeros((bands, 2, 2, slab_rows, length * length), values.dtype...]
    all_to_all x4 -> x3, waiting for transfers between devices: 0.01 us -> 52.2 us  [the longest x1 30.2 us: exchange(): flat = lax.all_to_all(flat, axis, 0, 0, tiled=True)]
    another operation x11 -> x0, local copies, waits for them, and re-layouts: 49.1 us -> none
    dot_general x28 -> x0, matrix products: 30.2 us -> none  [contract(): return jnp.einsum(form_text, *operands, precision=HIGHEST)]
    squeeze x1 -> x0, blocking collectives: 23.4 us -> none  [per_device(): all_columns = every_column[0]]
    pallas_call x0 -> x5, Pallas kernels: none -> 16.6 us  [run(): pl.pallas_call(kernel, out_shape=outs, in_specs=specs, out_specs=jax.tree...]
  transfers between devices with their start and end apart: 6 -> 3, of which waited for: 2 -> 3; matrix products, arithmetic and copies ran while one was open for 29% -> 0% of each run, Pallas kernels for 0% -> 5%
where the time goes in v1:
time: 115 us; the launch traced here: 114 us
  waiting for transfers between devices  52.2 us (45%)
  starting transfers between devices  37.2 us (32%)
  Pallas kernels  16.6 us (14%)
  local copies, waits for them, and re-layouts  6.58 us (6%)
    all_to_all x1, waiting for transfers between devices, exchange(): flat = lax.all_to_all(flat, axis, 0, 0, tiled=True)  30.2 us
    all_to_all x2, waiting for transfers between devices, exchange(): lax.all_to_all(values.reshape(parts, rows, 128), axis, 0, 0, tiled=True)  22.1 us
    all_to_all x1, starting transfers between devices, exchange(): flat = lax.all_to_all(flat, axis, 0, 0, tiled=True)  19.4 us
    all_to_all x2, starting transfers between devices, exchange(): lax.all_to_all(values.reshape(parts, rows, 128), axis, 0, 0, tiled=True)  17.8 us
    pallas_call x5, Pallas kernels, run(): pl.pallas_call(kernel, out_shape=outs, in_specs=specs, out_specs=jax.tree...  16.6 us
    unnamed x38, local copies, waits for them, and re-layouts  6.38 us
  transfers between devices with their start and end apart: 3, of which 3 were waited for; matrix products, arithmetic and copies ran while one was open for 0% of the time, Pallas kernels for 5%

profile of v1, /device:TPU:1, one launch (start us, length us, event | category | flops | bytes accessed | tf_op | source)
XLA Modules:
  0.0 114.3 jit_solution(1367793195138202162)
XLA Ops:
  0.6 0.0 copy-start
  0.6 0.7 copy-done
  1.4 0.0 copy-start.2
  1.4 0.8 copy-done.2
  2.1 0.0 copy-start.4
  2.2 0.8 copy-done.4
  2.9 0.0 copy-start.6
  2.9 0.8 copy-done.6
  3.7 0.0 copy-start.8
  3.7 0.8 copy-done.8
  4.4 0.7 copy-done.10
  5.1 0.0 copy-start.12
  5.1 0.7 copy-done.12
  5.8 2.0 %lines_and_amplitudes.1 = f32[1088,128]{1,0:T(8,128)} custom-call(f32[1,8,4,256]{3,2,1,0:T(4,128)S(1)} %copy-done.4, f32[1,8,4,256]{3,2,1,0:T(4,128)S(1)} %copy-done.6, f32[1,8,4,256]{3,2,1,0:T(4,128)S(1)} %copy-done, f32[1,8,4,256]{3,2,1,0:T(4,128)S(1)} %copy-done.2, f32[1,2,16,256]{3,2,1,0:T(8,128)S(1)} %copy-done.8, s32[1,256]{1,0:T(1,128)S(1)} %copy-done.12, ...), custom_call_target="tpu_custom_call" | custom-call | flops 1 | bytes 1 | tf_op jit(solution)/shard_map/lines_and_amplitudes/pallas_call | solution.py:428
  7.8 0.0 copy-start.17
  7.8 19.4 %all-to-all-start = ((f32[64,1,2176]{2,1,0:T(1,128)}), f32[64,1,2176]{2,1,0:T(1,128)S(1)}, u32[]{:S(2)}, u32[]{:S(2)}) async-start(f32[64,1,2176]{2,1,0:T(1,128)} %bitcast), calls=%async_computation | async-start | bytes 1114112 | tf_op jit(solution)/shard_map/all_to_all | solution.py:450
  27.2 0.0 copy-done.17
  27.2 0.2 reduce
  27.4 0.0 copy-start.18
  27.4 0.1 reshape.49
  27.6 0.6 copy-done.18
  28.1 0.1 reshape.48.slots_ref
  28.2 0.0 copy-start.1
  28.2 0.0 copy-start.3
  28.2 0.0 copy-start.5
  28.2 0.0 copy-start.16
  28.2 0.1 pad_maximum_fusion.pot_ref
  28.3 30.2 %all-to-all-done = f32[64,1,2176]{2,1,0:T(1,128)S(1)} async-done(((f32[64,1,2176]{2,1,0:T(1,128)}), f32[64,1,2176]{2,1,0:T(1,128)S(1)}, u32[]{:S(2)}, u32[]{:S(2)}) %all-to-all-start) | async-done | bytes 557088 | tf_op jit(solution)/shard_map/all_to_all | solution.py:450
  58.4 0.0 copy-start.14
  58.5 0.0 copy-done.1
  58.5 0.0 copy-done.3
  58.5 0.0 copy-done.5
  58.5 0.0 copy-done.16
  58.5 0.6 copy-done.14
  59.1 0.0 copy-done.15
  59.1 6.5 %potential_and_coupling.1 = (f32[512,128]{1,0:T(8,128)}, f32[1024,128]{1,0:T(8,128)S(1)}, f32[8,128]{1,0:T(8,128)S(1)}) custom-call(f32[1088,128]{1,0:T(8,128)S(1)} %bitcast.7, f32[1,8]{1,0:T(1,128)S(1)} %copy-done.15, f32[1,8,4,256]{3,2,1,0:T(4,128)S(1)} %copy-done.1, f32[1,8,4,256]{3,2,1,0:T(4,128)S(1)} %copy-done.3, f32[1,256]{1,0:T(1,128)S(1)} %copy-done.14, ...), custom_call_target="tpu_custom_call" | custom-call | flops 1 | bytes 1 | tf_op jit(solution)/shard_map/potential_and_coupling/pallas_call | solution.py:428
  65.7 8.0 %all-to-all-start.1 = ((f32[64,8,128]{2,1,0:T(8,128)}), f32[64,8,128]{2,1,0:T(8,128)S(1)}, u32[]{:S(2)}, u32[]{:S(2)}) async-start(f32[64,8,128]{2,1,0:T(8,128)} %bitcast.3), calls=%async_computation.1 | async-start | bytes 524288 | tf_op jit(solution)/shard_map/all_to_all | solution.py:452
  73.7 4.1 %orbital_and_response_grid.1.other_ref = f32[2048,128]{1,0:T(8,128)S(1)} custom-call(f32[1088,128]{1,0:T(8,128)S(1)} %bitcast.8), custom_call_target="tpu_custom_call" | custom-call | flops 3000000000 | bytes 3000000 | tf_op jit(solution)/shard_map/orbital_and_response_grid/pallas_call | solution.py:428
  77.8 14.2 %all-to-all-done.1 = f32[64,8,128]{2,1,0:T(8,128)S(1)} async-done(((f32[64,8,128]{2,1,0:T(8,128)}), f32[64,8,128]{2,1,0:T(8,128)S(1)}, u32[]{:S(2)}, u32[]{:S(2)}) %all-to-all-start.1) | async-done | bytes 262176 | tf_op jit(solution)/shard_map/all_to_all | solution.py:452
  92.0 2.4 %density.1 = f32[1024,128]{1,0:T(8,128)} custom-call(f32[512,128]{1,0:T(8,128)S(1)} %bitcast.9, f32[8,128]{1,0:T(8,128)S(1)} %get-tuple-element.11.scalars_ref, f32[1024,128]{1,0:T(8,128)S(1)} %get-tuple-element.15.grid_ref, f32[2048,128]{1,0:T(8,128)S(1)} %orbital_and_response_grid.1.other_ref), custom_call_target="tpu_custom_call" | custom-call | flops 1 | bytes 1 | tf_op jit(solution)/shard_map/density/pallas_call | solution.py:428
  94.4 9.8 %all-to-all-start.2 = ((f32[8,128,128]{2,1,0:T(8,128)}), f32[8,128,128]{2,1,0:T(8,128)S(1)}, u32[]{:S(2)}, u32[]{:S(2)}) async-start(f32[8,128,128]{2,1,0:T(8,128)} %bitcast.5), calls=%async_computation.2 | async-start | bytes 1048576 | tf_op jit(solution)/shard_map/all_to_all | solution.py:452
  104.2 0.0 copy-done.7
  104.2 0.0 copy-done.9
  104.2 0.0 copy-done.11
  104.2 0.0 copy-done.13
  104.2 1.6 %new_vectors.1 = (f32[1,8,4,256]{3,2,1,0:T(4,128)}, f32[1,8,4,256]{3,2,1,0:T(4,128)}, f32[1,8,4,256]{3,2,1,0:T(4,128)}) custom-call(f32[512,128]{1,0:T(8,128)S(1)} %bitcast.10, f32[8,128]{1,0:T(8,128)S(1)} %get-tuple-element.11.scalars_ref, f32[1,8,4,256]{3,2,1,0:T(4,128)S(1)} %copy-done.7, f32[1,8,4,256]{3,2,1,0:T(4,128)S(1)} %copy-done.1, ...), custom_call_target="tpu_custom_call" | custom-call | flops 3000000000 | bytes 3000000 | tf_op jit(solution)/shard_map/new_vectors/pallas_call | solution.py:428
  105.8 7.9 %all-to-all-done.2 = f32[8,128,128]{2,1,0:T(8,128)S(1)} async-done(((f32[8,128,128]{2,1,0:T(8,128)}), f32[8,128,128]{2,1,0:T(8,128)S(1)}, u32[]{:S(2)}, u32[]{:S(2)}) %all-to-all-start.2) | async-done | bytes 524320 | tf_op jit(solution)/shard_map/all_to_all | solution.py:452
  113.7 0.6 broadcast_multiply_fusion
  (7 shorter events, 0.0 us)
Async XLA Ops:
  0.6 0.8 copy-start
  1.4 0.8 copy-start.2
  2.1 0.8 copy-start.4
  2.9 0.8 copy-start.6
  3.7 0.8 copy-start.8
  4.4 0.7 copy-start.10
  5.1 0.7 copy-start.12
  7.8 19.4 %copy-start.17 = (f32[4,1,4096]{2,1,0:T(1,128)S(1)}, f32[4,1,4096]{2,1,0:T(1,128)}, u32[]{:S(2)}) copy-start(f32[4,1,4096]{2,1,0:T(1,128)} %param.25) | copy-start | bytes 196612
  7.8 50.6 %all-to-all-start = ((f32[64,1,2176]{2,1,0:T(1,128)}), f32[64,1,2176]{2,1,0:T(1,128)S(1)}, u32[]{:S(2)}, u32[]{:S(2)}) async-start(f32[64,1,2176]{2,1,0:T(1,128)} %bitcast), calls=%async_computation | async-start | bytes 1114112 | tf_op jit(solution)/shard_map/all_to_all | solution.py:450
  27.4 0.7 copy-start.18
  28.2 30.3 %copy-start.1 = (f32[1,8,4,256]{3,2,1,0:T(4,128)S(1)}, f32[1,8,4,256]{3,2,1,0:T(4,128)}, u32[]{:S(2)}) copy-start(f32[1,8,4,256]{3,2,1,0:T(4,128)} %res_ref.5) | copy-start | bytes 98308
  28.2 30.3 %copy-start.3 = (f32[1,8,4,256]{3,2,1,0:T(4,128)S(1)}, f32[1,8,4,256]{3,2,1,0:T(4,128)}, u32[]{:S(2)}) copy-start(f32[1,8,4,256]{3,2,1,0:T(4,128)} %old_ref.5) | copy-start | bytes 98308
  28.2 30.3 %copy-start.5 = (f32[2,32,32]{2,1,0:T(8,128)S(1)}, f32[2,32,32]{2,1,0:T(8,128)}, u32[]{:S(2)}) copy-start(f32[2,32,32]{2,1,0:T(8,128)} %coup_ref.1) | copy-start | bytes 24580
  28.2 30.3 %copy-start.16 = (f32[1,8]{1,0:T(1,128)S(1)}, f32[1,8]{1,0:T(1,128)}, u32[]{:S(2)}) copy-start(f32[1,8]{1,0:T(1,128)} %energy_ref.3) | copy-start | bytes 100
  58.4 0.7 copy-start.14
  58.4 0.7 copy-start.15
  65.7 26.4 %all-to-all-start.1 = ((f32[64,8,128]{2,1,0:T(8,128)}), f32[64,8,128]{2,1,0:T(8,128)S(1)}, u32[]{:S(2)}, u32[]{:S(2)}) async-start(f32[64,8,128]{2,1,0:T(8,128)} %bitcast.3), calls=%async_computation.1 | async-start | bytes 524288 | tf_op jit(solution)/shard_map/all_to_all | solution.py:452
  94.4 9.8 %copy-start.7 = (f32[1,8,4,256]{3,2,1,0:T(4,128)S(1)}, f32[1,8,4,256]{3,2,1,0:T(4,128)}, u32[]{:S(2)}) copy-start(f32[1,8,4,256]{3,2,1,0:T(4,128)} %resp_ref.3) | copy-start | bytes 98308
  94.4 9.8 %copy-start.9 = (f32[1,2,16,256]{3,2,1,0:T(8,128)S(1)}, f32[1,2,16,256]{3,2,1,0:T(8,128)}, u32[]{:S(2)}) copy-start(f32[1,2,16,256]{3,2,1,0:T(8,128)} %form_ref.3) | copy-start | bytes 98308
  94.4 9.8 %copy-start.11 = (f32[3,64]{1,0:T(4,128)S(1)}, f32[3,64]{1,0:T(4,128)}, u32[]{:S(2)}) copy-start(f32[3,64]{1,0:T(4,128)} %pos_ref.3) | copy-start | bytes 2308
  94.4 9.8 %copy-start.13 = (s32[1,256]{1,0:T(1,128)S(1)}, s32[1,256]{1,0:T(1,128)}, u32[]{:S(2)}) copy-start(s32[1,256]{1,0:T(1,128)} %index_ref.3) | copy-start | bytes 3076
  94.4 19.2 %all-to-all-start.2 = ((f32[8,128,128]{2,1,0:T(8,128)}), f32[8,128,128]{2,1,0:T(8,128)S(1)}, u32[]{:S(2)}, u32[]{:S(2)}) async-start(f32[8,128,128]{2,1,0:T(8,128)} %bitcast.5), calls=%async_computation.2 | async-start | bytes 1048576 | tf_op jit(solution)/shard_map/all_to_all | solution.py:452

commit v2 on v1

--- a/solution.py
+++ b/solution.py
@@ -14,9 +14,12 @@
 PW = COLS * STICK
 PA = 16
 DEV = 64
+EXTRA = 16
+MIRROR = [(i, i ^ 1) for i in range(DEV)]
+HALF = NG // 2
 ALL = COLS * DEV
 ROWS1 = 17
-ROWS2 = 8
+ROWS2 = 5
 SMALL_TERM = 1e-06
 VOLUME = 1.0 / (NG * NG * NG)
 F32 = jnp.float32
@@ -103,13 +106,25 @@
     return jnp.concatenate([cosine, sine], axis=0)
 
 
-def send_kernel(orb_ref, resp_ref, res_ref, old_ref, form_ref, index_ref, pos_ref, out_ref):
+def send_kernel(
+    orb_hbm, resp_hbm, res_hbm, old_hbm, form_hbm, index_hbm, pos_hbm, out_ref,
+    orb_ref, resp_ref, res_ref, old_ref, form_ref, index_ref, pos_ref, sems,
+):
     arrays = (orb_ref, resp_ref, res_ref, old_ref)
+    copies = fetch(
+        (
+            (orb_hbm, orb_ref), (resp_hbm, resp_ref), (res_hbm, res_ref), (old_hbm, old_ref),
+            (form_hbm, form_ref), (index_hbm, index_ref), (pos_hbm, pos_ref),
+        ),
+        sems,
+    )
+    table = depth_table()
+    for copy in copies:
+        copy.wait()
     lines = jnp.concatenate(
         [ref[0, :, 2 * s + c, :] for c in range(2) for ref in arrays for s in range(2)], axis=0
     )
     lines = split(lines)
-    table = depth_table()
     group = iota(table.shape, 1) >> 5
     for b in range(COLS):
         z = dot3(split(jnp.where(group == b, table, 0.0)), lines, "nt")
@@ -141,7 +156,7 @@
     for b in range(COLS):
         code = jnp.sum(jnp.where(lane == STICK * b, codes, 0.0), axis=1, keepdims=True)
         row = jnp.where(target == COLS + b, code, row)
-    out_ref[pl.ds(COLS + NB, DEV, stride=ROWS1), :] = jnp.broadcast_to(row, (DEV, 128))
+    out_ref[pl.ds(EXTRA, DEV, stride=ROWS1), :] = jnp.broadcast_to(row, (DEV, 128))
 
 
 def own_columns(recv_ref):
@@ -160,29 +175,33 @@
 
 
 def x_tables(codes, cos_ref, sin_ref):
-    shape = (NG, ALL)
+    shape = (HALF, ALL)
     cosine, sine = trig_wound(iota(shape, 0) * (codes >> 6))
     cos_ref[...] = cosine
     sin_ref[...] = sine
 
 
-def y_forward(extra, table_ref):
+def y_tables(extra, high_ref, low_ref):
     shape = (DEV, 128)
     lane = iota(shape, 1)
     for b in range(COLS):
-        gy = extra[:, COLS + b : COLS + b + 1].astype(jnp.int32) & 63
-        cosine, sine = trig_wound(gy * (lane & 63))
+        code = extra[:, COLS + b : COLS + b + 1].astype(jnp.int32)
+        wound = (code & 63) * (lane & 63)
+        cosine, sine = trig_wound(wound)
+        odd = jnp.broadcast_to(((code >> 6) & 1) == 1, shape)
         first = jnp.where(lane < 64, cosine, sine)
         second = jnp.where(lane < 64, -sine, cosine)
         for c, part in ((0, first), (1, second)):
-            high, low = split(part)
             rows = slice(c * ALL + b * DEV, c * ALL + (b + 1) * DEV)
-            table_ref[rows, 0:128] = high
-            table_ref[rows, 128:256] = low
-
-
-def plane_chunk(re, im, first, count, cos_ref, sin_ref, table_ref, high_ref, low_ref):
+            for parity, mine in ((0, jnp.where(odd, 0.0, part)), (1, jnp.where(odd, part, 0.0))):
+                high, low = split(mine)
+                high_ref[rows, parity * 128 : (parity + 1) * 128] = high
+                low_ref[rows, parity * 128 : (parity + 1) * 128] = low
+
+
+def plane_chunk(re, im, first, count, cos_ref, sin_ref, tables, scratch):
     rows = re.shape[0]
+    high_ref, low_ref = scratch
     for i in range(count):
         cx = cos_ref[pl.ds(first + i, 1), :]
         sx = sin_ref[pl.ds(first + i, 1), :]
@@ -190,61 +209,82 @@
             high, low = split(part)
             high_ref[i * rows : (i + 1) * rows, c * ALL : (c + 1) * ALL] = high
             low_ref[i * rows : (i + 1) * rows, c * ALL : (c + 1) * ALL] = low
-    both = dot(high_ref[...], table_ref[...])
-    return both[:, :128] + both[:, 128:] + dot(low_ref[...], table_ref[:, :128])
+    high = high_ref[...]
+    table = tables[0][...]
+    both = dot(high, table) + dot(low_ref[...], table) + dot(high, tables[1][...])
+    return both[:, :128] + both[:, 128:], both[:, :128] - both[:, 128:]
+
+
+def fetch(pairs, sems):
+    copies = [
+        pltpu.make_async_copy(source, target, sems.at[i])
+        for i, (source, target) in enumerate(pairs)
+    ]
+    for copy in copies:
+        copy.start()
+    return copies
 
 
 def potential_kernel(
-    recv_ref, old_norm_ref, res_ref, old_ref, kin_ref, energy_ref, atom_ref, slots_ref,
-    coup_ref, pot_ref, out_ref, grid_ref, scalars_ref,
-    cos_ref, sin_ref, table_ref, back_high, back_low, high_ref, low_ref, prod_ref, pair_ref,
+    recv_ref, atom_ref, slots_ref, pot_ref, old_norm_hbm, res_hbm, old_hbm, kin_hbm,
+    energy_hbm, coup_hbm,
+    out_ref, grid_ref, scalars_ref,
+    old_norm_ref, res_ref, old_ref, kin_ref, energy_ref, coup_ref, sems,
+    cos_ref, sin_ref, table_high, table_low, high_ref, low_ref, prod_ref, pair_ref,
 ):
-    extra = recv_ref[pl.ds(COLS + NB, DEV, stride=ROWS1), :]
+    copies = fetch(
+        (
+            (old_norm_hbm, old_norm_ref), (res_hbm, res_ref), (old_hbm, old_ref),
+            (kin_hbm, kin_ref), (energy_hbm, energy_ref), (coup_hbm, coup_ref),
+        ),
+        sems,
+    )
+    extra = recv_ref[pl.ds(EXTRA, DEV, stride=ROWS1), :]
+    codes = column_codes(extra)
+    x_tables(codes, cos_ref, sin_ref)
+    y_tables(extra, table_high, table_low)
+    tables = (table_high, table_low)
+    for copy in copies:
+        copy.wait()
     norm = row_to_col(jnp.sum(extra, axis=0, keepdims=True), NB)
     beta = norm / row_to_col(old_norm_ref[...], NB)
-    codes = column_codes(extra)
-    x_tables(codes, cos_ref, sin_ref)
-    y_forward(extra, table_ref)
-    cosine, sine = trig_wound(iota((NG, ALL), 0) * (codes & 63))
-    for rows, parts in ((slice(0, 64), (cosine, -sine)), (slice(64, 128), (sine, cosine))):
-        for c in range(2):
-            high, low = split(parts[c])
-            back_high[rows, c * ALL : (c + 1) * ALL] = high
-            back_low[rows, c * ALL : (c + 1) * ALL] = low
-
     values = own_columns(recv_ref)
     beta2 = jnp.concatenate([beta, beta], axis=0)
     re = values[32:48] + beta2 * values[48:64]
     im = values[96:112] + beta2 * values[112:128]
 
-    def chunk(k, carry):
-        acc_re, acc_im, local = carry
+    acc_re = jnp.zeros((16, ALL), F32)
+    acc_im = jnp.zeros((16, ALL), F32)
+    local = jnp.zeros((NB, 128), F32)
+    for k in range(2):
         first = k * 16
-        grid = plane_chunk(re, im, first, 16, cos_ref, sin_ref, table_ref, high_ref, low_ref)
-        grid_ref[pl.ds(pl.multiple_of(k * 256, 256), 256), :] = grid
+        grids = plane_chunk(re, im, first, 16, cos_ref, sin_ref, tables, (high_ref.at[k], low_ref.at[k]))
         for i in range(16):
-            up = grid[i * 16 : i * 16 + 8]
-            down = grid[i * 16 + 8 : i * 16 + 16]
-            v0, bx, by, bz = (pot_ref[m, pl.ds(first + i, 1), :] for m in range(4))
-            new_up = (v0 + bz) * up + bx * down - by * swap_sign(down)
-            new_down = bx * up + by * swap_sign(up) + (v0 - bz) * down
-            prod_ref[i * 16 : i * 16 + 8, :] = new_up
-            prod_ref[i * 16 + 8 : i * 16 + 16, :] = new_down
-            local = local + up * new_up + down * new_down
-        prod = split(prod_ref[...])
-        table = back_high[...]
-        turned = dot(prod[0], table) + dot(prod[1], table) + dot(prod[0], back_low[...])
+            products = []
+            for half in range(2):
+                grid = grids[half]
+                x = first + i + 32 * half
+                up = grid[i * 16 : i * 16 + 8]
+                down = grid[i * 16 + 8 : i * 16 + 16]
+                grid_ref[x * 16 : x * 16 + 8, :] = up
+                grid_ref[x * 16 + 8 : x * 16 + 16, :] = down
+                v0, bx, by, bz = (pot_ref[m, x : x + 1, :] for m in range(4))
+                new_up = (v0 + bz) * up + bx * down - by * swap_sign(down)
+                new_down = bx * up + by * swap_sign(up) + (v0 - bz) * down
+                local = local + up * new_up + down * new_down
+                products.append((new_up, new_down))
+            for j in range(2):
+                rows = slice(i * 16 + 8 * j, i * 16 + 8 * j + 8)
+                prod_ref[k, rows, 0:128] = products[0][j] + products[1][j]
+                prod_ref[k, rows, 128:256] = products[0][j] - products[1][j]
+        turned = dot3(split(prod_ref[k]), (table_high[...], table_low[...]), "nt")
         for i in range(16):
-            cx = cos_ref[pl.ds(first + i, 1), :]
-            sx = sin_ref[pl.ds(first + i, 1), :]
+            cx = cos_ref[first + i : first + i + 1, :]
+            sx = sin_ref[first + i : first + i + 1, :]
             q_re = turned[i * 16 : (i + 1) * 16, :ALL]
             q_im = turned[i * 16 : (i + 1) * 16, ALL:]
             acc_re = acc_re + q_re * cx + q_im * sx
             acc_im = acc_im + q_im * cx - q_re * sx
-        return acc_re, acc_im, local
-
-    zero = jnp.zeros((16, ALL), F32)
-    acc_re, acc_im, local = lax.fori_loop(0, 4, chunk, (zero, zero, jnp.zeros((NB, 128), F32)))
     acc_re = acc_re * VOLUME
     acc_im = acc_im * VOLUME
     for r in range(2):
@@ -283,12 +323,13 @@
     pair_ref[:, 0:32] = q_re
     pair_ref[:, 32:64] = q_im
     pair_ref[:, 64:128] = jnp.zeros((NB, 64), F32)
-    even = pair_ref[pl.ds(0, 4, stride=2), :]
-    odd = pair_ref[pl.ds(1, 4, stride=2), :]
-    packed = even + pltpu.roll(odd, 64, 1)
-    for k in range(4):
-        out_ref[pl.ds(2 + k, DEV, stride=ROWS2), :] = jnp.broadcast_to(
-            packed[k : k + 1], (DEV, 128)
+    first_half = pair_ref[pl.ds(0, 4, stride=2), :]
+    second_half = pair_ref[pl.ds(1, 4, stride=2), :]
+    packed = first_half + pltpu.roll(second_half, 64, 1)
+    odd = (iota((DEV, 128), 0) & 1) == 1
+    for k in range(2):
+        out_ref[pl.ds(2 + k, DEV, stride=ROWS2), :] = jnp.where(
+            odd, packed[2 + k : 3 + k], packed[k : k + 1]
         )
 
     curvature = jnp.sum(local, axis=1, keepdims=True) * VOLUME
@@ -299,38 +340,44 @@
         d = res_ref[0, :, comp, :] + beta * old_ref[0, :, comp, :]
         own = own + d * d
     curvature = curvature + jnp.sum(own * weight, axis=1, keepdims=True)
-    out_ref[pl.ds(6, DEV, stride=ROWS2), :] = jnp.broadcast_to(
+    out_ref[pl.ds(4, DEV, stride=ROWS2), :] = jnp.broadcast_to(
         col_to_row(curvature, 128), (DEV, 128)
     )
-    out_ref[pl.ds(7, DEV, stride=ROWS2), :] = jnp.zeros((DEV, 128), F32)
     lane = iota((NB, 128), 1)
     scalars_ref[...] = jnp.where(lane == 0, norm, jnp.where(lane == 1, beta, 0.0))
 
 
-def orbital_kernel(recv_ref, grid_ref, cos_ref, sin_ref, table_ref, high_ref, low_ref):
-    extra = recv_ref[pl.ds(COLS + NB, DEV, stride=ROWS1), :]
+def orbital_kernel(
+    recv_ref, grid_ref, cos_ref, sin_ref, table_high, table_low, high_ref, low_ref
+):
+    extra = recv_ref[pl.ds(EXTRA, DEV, stride=ROWS1), :]
     x_tables(column_codes(extra), cos_ref, sin_ref)
-    y_forward(extra, table_ref)
+    y_tables(extra, table_high, table_low)
     values = own_columns(recv_ref)
     re, im = values[0:32], values[64:96]
 
     def chunk(k, carry):
-        grid = plane_chunk(re, im, k * 8, 8, cos_ref, sin_ref, table_ref, high_ref, low_ref)
-        grid_ref[pl.ds(pl.multiple_of(k * 256, 256), 256), :] = grid
+        grids = plane_chunk(
+            re, im, k * 8, 8, cos_ref, sin_ref, (table_high, table_low), (high_ref, low_ref)
+        )
+        for half in range(2):
+            place = pl.multiple_of(k * 256 + half * 1024, 256)
+            grid_ref[pl.ds(place, 256), :] = grids[half]
         return carry
 
-    lax.fori_loop(0, 8, chunk, 0)
+    lax.fori_loop(0, 4, chunk, 0)
 
 
 def step_of(recv_ref, scalars_ref):
-    total = jnp.sum(recv_ref[pl.ds(6, DEV, stride=ROWS2), :], axis=0, keepdims=True)
+    total = jnp.sum(recv_ref[pl.ds(4, DEV, stride=ROWS2), :], axis=0, keepdims=True)
     return scalars_ref[:, 0:1] / (row_to_col(total, NB) + SMALL_TERM)
 
 
-def density_kernel(recv_ref, scalars_ref, grid_ref, other_ref, out_ref):
-    step = step_of(recv_ref, scalars_ref)
-    step = jnp.broadcast_to(step, (NB, 128))
-    lane = iota((1, 128), 1)
+def density_kernel(
+    recv_ref, scalars_ref, grid_ref, other_ref, out_ref, half_ref, sum_ref
+):
+    step = jnp.broadcast_to(step_of(recv_ref, scalars_ref), (NB, 128))
+    lane = iota((NB, 128), 1)
 
     def terms(x):
         base = pl.multiple_of(x * 32, 32)
@@ -341,32 +388,33 @@
         c_down = other_ref[pl.ds(base + 24, 8), :] + step * grid_ref[pl.ds(half + 8, 8), :]
         same_up = o_up * c_up
         same_down = o_down * c_down
-        parts = (
+        return (
             same_up + same_down,
             o_up * c_down + o_down * c_up,
             o_down * swap_sign(c_up) - o_up * swap_sign(c_down),
             same_up - same_down,
         )
-        sums = []
-        for part in parts:
-            row = jnp.sum(part, axis=0, keepdims=True)
-            sums.append(2.0 * (row + pltpu.roll(row, 64, 1)))
-        return sums
 
     def pair(p, carry):
         even = terms(2 * p)
         odd = terms(2 * p + 1)
         for m in range(4):
-            row = jnp.where(lane < 64, even[m], odd[m])
-            for copy in range(8):
-                out_ref[pl.ds(copy * 128 + m * 32 + p, 1), :] = row
+            both = jnp.where(lane < 64, even[m], odd[m]) + pltpu.roll(
+                jnp.where(lane < 64, odd[m], even[m]), 64, 1
+            )
+            sum_ref[pl.ds(m * 32 + p, 1), :] = 2.0 * jnp.sum(both, axis=0, keepdims=True)
         return carry
 
-    lax.fori_loop(0, 32, pair, 0, unroll=4)
+    lax.fori_loop(0, 32, pair, 0, unroll=8)
+    total = sum_ref[...]
+    for copy in range(8):
+        out_ref[copy * 128 : (copy + 1) * 128, :] = total
+    for k in range(2):
+        half_ref[k * DEV : (k + 1) * DEV, :] = recv_ref[pl.ds(2 + k, DEV, stride=ROWS2), :]
 
 
 def finish_kernel(
-    recv_ref, scalars_ref, resp_ref, res_ref, old_ref, kin_ref, energy_ref, form_ref,
+    parity_ref, half_ref, other_ref, recv_ref, scalars_ref, resp_ref, res_ref, old_ref, kin_ref, energy_ref, form_ref,
     index_ref, pos_ref, next_ref, residual_ref, direction_ref,
 ):
     step = step_of(recv_ref, scalars_ref)
@@ -389,7 +437,9 @@
     form_re, form_im = form_ref[0, 0], form_ref[0, 1]
     rows_re, rows_im = [[], []], [[], []]
     for k in range(4):
-        values = recv_ref[pl.ds(2 + k, DEV, stride=ROWS2), :].T
+        rows = slice((k & 1) * DEV, (k & 1) * DEV + DEV)
+        mine = parity_ref[0] == (k >> 1)
+        values = jnp.where(mine, half_ref[rows, :], other_ref[rows, :]).T
         z = dot3(split(values), phases)
         for i in range(2):
             for s in range(2):
@@ -418,13 +468,16 @@
             residual_ref[0, :, comp, :] = residual - step * image
 
 
-def call(kernel, outs, name, scratch=(), flops=1, size=1, smem=()):
+def call(kernel, outs, name, scratch=(), flops=1, size=1, smem=(), hbm=()):
+    def space(i):
+        return pltpu.SMEM if i in smem else pltpu.HBM if i in hbm else pltpu.VMEM
+
     def run(*args):
-        specs = [
-            pl.BlockSpec(memory_space=pltpu.SMEM if i in smem else pltpu.VMEM)
-            for i in range(len(args))
+        specs = [pl.BlockSpec(memory_space=space(i)) for i in range(len(args))]
+        args = [
+            pltpu.with_memory_space_constraint(a, pltpu.HBM) if i in hbm else a
+            for i, a in enumerate(args)
         ]
-        single = not isinstance(outs, (list, tuple))
         return pl.pallas_call(
             kernel,
             out_shape=outs,
@@ -463,37 +516,52 @@
     plane = potential.reshape(4, NG, NG)
     plane = jnp.concatenate([plane, plane], axis=2)
 
-    sent = call(send_kernel, shape_of(DEV * ROWS1, 128), "lines_and_amplitudes")(
-        orbitals, response, residual, old_direction, form_factor, sphere_index, atom_positions
-    )
+    parity = me & 1
+    vector = pltpu.VMEM((1, NB, 4, PW), F32)
+    sent = call(
+        send_kernel, shape_of(DEV * ROWS1, 128), "lines_and_amplitudes",
+        [vector] * 4 + [
+            pltpu.VMEM((1, 2, PA, PW), F32), pltpu.VMEM((1, PW), jnp.int32),
+            pltpu.VMEM((3, NG), F32), pltpu.SemaphoreType.DMA((7,)),
+        ],
+        hbm=range(7),
+    )(orbitals, response, residual, old_direction, form_factor, sphere_index, atom_positions)
     recv = exchange(sent, "fft", DEV)
     tables = [
-        pltpu.VMEM((NG, ALL), F32), pltpu.VMEM((NG, ALL), F32),
-        pltpu.VMEM((2 * ALL, 256), BF16),
+        pltpu.VMEM((HALF, ALL), F32), pltpu.VMEM((HALF, ALL), F32),
+        pltpu.VMEM((2 * ALL, 256), BF16), pltpu.VMEM((2 * ALL, 256), BF16),
     ]
-    wide = [pltpu.VMEM((256, 2 * ALL), BF16), pltpu.VMEM((256, 2 * ALL), BF16)]
     back, grid, scalars = call(
         potential_kernel,
         (shape_of(DEV * ROWS2, 128), shape_of(NG * 16, 128), shape_of(NB, 128)),
         "potential_and_coupling",
-        tables + [pltpu.VMEM((128, 2 * ALL), BF16), pltpu.VMEM((128, 2 * ALL), BF16)] + wide
-        + [pltpu.VMEM((256, 128), F32), pltpu.VMEM((NB, 128), F32)],
-        smem=(6,),
-    )(recv, old_norm, residual, old_direction, kinetic, band_energy, me, slots, coupling, plane)
+        [
+            pltpu.VMEM((1, NB), F32), vector, vector, pltpu.VMEM((1, PW), F32),
+            pltpu.VMEM((1, NB), F32), pltpu.VMEM((2, 32, 32), F32),
+            pltpu.SemaphoreType.DMA((6,)),
+        ]
+        + tables
+        + [pltpu.VMEM((2, 256, 2 * ALL), BF16), pltpu.VMEM((2, 256, 2 * ALL), BF16)]
+        + [pltpu.VMEM((2, 256, 256), F32), pltpu.VMEM((NB, 128), F32)],
+        smem=(1,), hbm=range(4, 10),
+    )(recv, me, slots, plane, old_norm, residual, old_direction, kinetic, band_energy, coupling)
     returned = exchange(back, "fft", DEV)
     other = call(
-        orbital_kernel, shape_of(NG * 32, 128), "orbital_and_response_grid", tables + wide,
+        orbital_kernel, shape_of(NG * 32, 128), "orbital_and_response_grid",
+        tables + [pltpu.VMEM((256, 2 * ALL), BF16), pltpu.VMEM((256, 2 * ALL), BF16)],
         flops=3_000_000_000, size=3_000_000,
     )(recv)
-    density = call(density_kernel, shape_of(8 * 128, 128), "density")(
-        returned, scalars, grid, other
-    )
+    density, half = call(
+        density_kernel, (shape_of(8 * 128, 128), shape_of(2 * DEV, 128)), "density",
+        [pltpu.VMEM((128, 128), F32)],
+    )(returned, scalars, grid, other)
     gathered = exchange(density, "kpool", 8)
+    other_half = lax.ppermute(half, "fft", MIRROR)
     outs = call(
         finish_kernel, (shape_of(1, NB, 4, PW),) * 3, "new_vectors",
-        flops=3_000_000_000, size=3_000_000,
+        flops=3_000_000_000, size=3_000_000, smem=(0,),
     )(
-        returned, scalars, response, residual, old_direction, kinetic, band_energy, form_factor,
+        parity, half, other_half, returned, scalars, response, residual, old_direction, kinetic, band_energy, form_factor,
         sphere_index, atom_positions,
     )
     total = jnp.sum(gathered.reshape(8, 128, 128), axis=0) * scale

time: 115 us -> 104 us (0.904)
  local copies, waits for them, and re-layouts: 6.58 us -> 0.91 us
  waiting for transfers between devices: 52.2 us -> 48.4 us
  Pallas kernels: 16.6 us -> 14.2 us
    all_to_all x2 -> x1, waiting for transfers between devices: 22.1 us -> 2.1 us  [exchange(): lax.all_to_all(values.reshape(parts, rows, 128), axis, 0, 0, tiled=True)]
    all_to_all x1 -> x2, waiting for transfers between devices: 30.2 us -> 42.8 us  [exchange(): flat = lax.all_to_all(flat, axis, 0, 0, tiled=True)]
    all_to_all x2 -> x1, starting transfers between devices: 17.8 us -> 8.47 us  [exchange(): lax.all_to_all(values.reshape(parts, rows, 128), axis, 0, 0, tiled=True)]
    all_to_all x1 -> x2, starting transfers between devices: 19.4 us -> 27.5 us  [exchange(): flat = lax.all_to_all(flat, axis, 0, 0, tiled=True)]
    unnamed x38 -> x20, local copies, waits for them, and re-layouts: 6.38 us -> 0.72 us
    ppermute x0 -> x1, waiting for transfers between devices: none -> 3.47 us  [per_device(): other_half = lax.ppermute(half, 'fft', MIRROR)]
    pallas_call x5, Pallas kernels: 16.6 us -> 14.2 us  [run(): pl.pallas_call(kernel, out_shape=outs, in_specs=specs, out_specs=jax.tree...]
    ppermute x0 -> x1, starting transfers between devices: none -> 2.25 us  [per_device(): other_half = lax.ppermute(half, 'fft', MIRROR)]
  transfers between devices with their start and end apart: 3 -> 4, of which waited for: 3 -> 4; matrix products, arithmetic and copies ran while one was open for 0% -> 0% of each run, Pallas kernels for 5% -> 5%
where the time goes in v2:
time: 104 us; the launch traced here: 103 us
  waiting for transfers between devices  48.4 us (47%)
  starting transfers between devices  38.2 us (37%)
  Pallas kernels  14.2 us (14%)
    all_to_all x2, waiting for transfers between devices, exchange(): flat = lax.all_to_all(flat, axis, 0, 0, tiled=True)  42.8 us
    all_to_all x2, starting transfers between devices, exchange(): flat = lax.all_to_all(flat, axis, 0, 0, tiled=True)  27.5 us
    pallas_call x5, Pallas kernels, run(): pl.pallas_call(kernel, out_shape=outs, in_specs=specs, out_specs=jax.tree...  14.2 us
    all_to_all x1, starting transfers between devices, exchange(): lax.all_to_all(values.reshape(parts, rows, 128), axis, 0, 0, tiled=True)  8.47 us
    ppermute x1, waiting for transfers between devices, per_device(): other_half = lax.ppermute(half, 'fft', MIRROR)  3.47 us
    ppermute x1, starting transfers between devices, per_device(): other_half = lax.ppermute(half, 'fft', MIRROR)  2.25 us
    all_to_all x1, waiting for transfers between devices, exchange(): lax.all_to_all(values.reshape(parts, rows, 128), axis, 0, 0, tiled=True)  2.1 us
  transfers between devices with their start and end apart: 4, of which 4 were waited for; matrix products, arithmetic and copies ran while one was open for 0% of the time, Pallas kernels for 5%

profile of v2, /device:TPU:1, one launch (start us, length us, event | category | flops | bytes accessed | tf_op | source)
XLA Modules:
  0.0 103.4 jit_solution(12776185629082321508)
XLA Ops:
  0.6 2.8 %lines_and_amplitudes.1 = f32[1088,128]{1,0:T(8,128)} custom-call(f32[1,8,4,256]{3,2,1,0:T(4,128)} %orb_hbm.1, f32[1,8,4,256]{3,2,1,0:T(4,128)} %resp_ref.1, f32[1,8,4,256]{3,2,1,0:T(4,128)} %res_ref.1, f32[1,8,4,256]{3,2,1,0:T(4,128)} %old_ref.1, f32[1,2,16,256]{3,2,1,0:T(8,128)} %form_ref.1, s32[1,256]{1,0:T(1,128)} %index_ref.1, f32[3,64]{1,0:T(4,128)} %pos_ref.1), custom_call_target="tpu_custom_call" | custom-call | flops 1 | bytes 1 | tf_op jit(solution)/shard_map/lines_and_amplitudes/pallas_call | solution.py:481
  3.5 0.0 copy-start.8
  3.5 19.4 %all-to-all-start = ((f32[64,1,2176]{2,1,0:T(1,128)}), f32[64,1,2176]{2,1,0:T(1,128)S(1)}, u32[]{:S(2)}, u32[]{:S(2)}) async-start(f32[64,1,2176]{2,1,0:T(1,128)} %bitcast.1), calls=%async_computation | async-start | bytes 1114112 | tf_op jit(solution)/shard_map/all_to_all | solution.py:503
  22.9 0.0 copy-start.9
  22.9 0.7 copy-done.9
  23.6 0.1 reshape.48.slots_ref
  23.7 0.0 copy-done.8
  23.7 0.2 reduce
  23.8 0.1 reshape.49
  24.0 0.1 pad_maximum_fusion.pot_ref
  24.1 30.1 %all-to-all-done = f32[64,1,2176]{2,1,0:T(1,128)S(1)} async-done(((f32[64,1,2176]{2,1,0:T(1,128)}), f32[64,1,2176]{2,1,0:T(1,128)S(1)}, u32[]{:S(2)}, u32[]{:S(2)}) %all-to-all-start) | async-done | bytes 557088 | tf_op jit(solution)/shard_map/all_to_all | solution.py:503
  54.1 4.9 %potential_and_coupling.1 = (f32[320,128]{1,0:T(8,128)}, f32[1024,128]{1,0:T(8,128)S(1)}, f32[8,128]{1,0:T(8,128)S(1)}) custom-call(f32[1088,128]{1,0:T(8,128)S(1)} %bitcast.7, s32[1]{0:T(128)} %bitcast.atom_ref, s32[16,64]{1,0:T(8,128)S(1)} %reshape.48.slots_ref, f32[4,64,128]{2,1,0:T(8,128)S(1)} %pad_maximum_fusion.pot_ref, f32[1,8]{1,0:T(1,128)} %old_norm_hbm.1, ...), custom_call_target="tpu_custom_call" | custom-call | flops 1 | bytes 1 | tf_op jit(solution)/shard_map/potential_and_coupling/pallas_call | solution.py:481
  59.0 8.0 %all-to-all-start.1 = ((f32[64,1,640]{2,1,0:T(1,128)}), f32[64,1,640]{2,1,0:T(1,128)S(1)}, u32[]{:S(2)}, u32[]{:S(2)}) async-start(f32[64,1,640]{2,1,0:T(1,128)} %bitcast.3), calls=%async_computation.1 | async-start | bytes 327680 | tf_op jit(solution)/shard_map/all_to_all | solution.py:503
  67.1 3.1 %orbital_and_response_grid.1.other_ref = f32[2048,128]{1,0:T(8,128)S(1)} custom-call(f32[1088,128]{1,0:T(8,128)S(1)} %bitcast.8), custom_call_target="tpu_custom_call" | custom-call | flops 3000000000 | bytes 3000000 | tf_op jit(solution)/shard_map/orbital_and_response_grid/pallas_call | solution.py:481
  70.2 12.8 %all-to-all-done.1 = f32[64,1,640]{2,1,0:T(1,128)S(1)} async-done(((f32[64,1,640]{2,1,0:T(1,128)}), f32[64,1,640]{2,1,0:T(1,128)S(1)}, u32[]{:S(2)}, u32[]{:S(2)}) %all-to-all-start.1) | async-done | bytes 163872 | tf_op jit(solution)/shard_map/all_to_all | solution.py:503
  83.0 1.7 %density.1 = (f32[1024,128]{1,0:T(8,128)}, f32[128,128]{1,0:T(8,128)S(1)}) custom-call(f32[320,128]{1,0:T(8,128)S(1)} %bitcast.9, f32[8,128]{1,0:T(8,128)S(1)} %get-tuple-element.13.scalars_ref, f32[1024,128]{1,0:T(8,128)S(1)} %get-tuple-element.14.grid_ref, f32[2048,128]{1,0:T(8,128)S(1)} %orbital_and_response_grid.1.other_ref), custom_call_target="tpu_custom_call" | custom-call | flops 1 | bytes 1 | tf_op jit(solution)/shard_map/density/pallas_call | solution.py:481
  84.7 0.0 copy-start
  84.7 0.0 copy-start.1
  84.7 0.0 copy-start.2
  84.7 0.0 copy-start.3
  84.7 0.0 copy-start.6
  84.8 8.5 %all-to-all-start.2 = ((f32[8,128,128]{2,1,0:T(8,128)}), f32[8,128,128]{2,1,0:T(8,128)S(1)}, u32[]{:S(2)}, u32[]{:S(2)}) async-start(f32[8,128,128]{2,1,0:T(8,128)} %bitcast.5), calls=%async_computation.2 | async-start | bytes 1048576 | tf_op jit(solution)/shard_map/all_to_all | solution.py:505
  93.2 0.0 copy-start.4
  93.2 0.0 copy-start.5
  93.2 0.0 copy-start.7
  93.2 2.2 %collective-permute-start = (f32[128,128]{1,0:T(8,128)S(1)}, f32[128,128]{1,0:T(8,128)S(1)}, u32[]{:S(2)}, u32[]{:S(2)}) collective-permute-start(f32[128,128]{1,0:T(8,128)S(1)} %get-tuple-element.15.half_ref), channel_id=1, source_target_pairs={{0,1},{1,0},{2,3},{3,2},{4,5},{5,4},{6,7},{7,6},{8,9},{9,8},{10,11... | collective-permute-start | bytes 196616 | tf_op jit(solution)/shard_map/ppermute | solution.py:559
  95.5 3.5 %collective-permute-done.other_ref = f32[128,128]{1,0:T(8,128)S(1)} collective-permute-done((f32[128,128]{1,0:T(8,128)S(1)}, f32[128,128]{1,0:T(8,128)S(1)}, u32[]{:S(2)}, u32[]{:S(2)}) %collective-permute-start) | collective-permute-done | bytes 65568 | tf_op jit(solution)/shard_map/ppermute | solution.py:559
  99.0 0.0 copy-done
  99.0 0.0 copy-done.1
  99.0 0.0 copy-done.2
  99.0 0.0 copy-done.3
  99.0 0.0 copy-done.6
  99.0 0.0 copy-done.4
  99.0 0.0 copy-done.5
  99.0 0.0 copy-done.7
  99.0 1.6 %new_vectors.1 = (f32[1,8,4,256]{3,2,1,0:T(4,128)}, f32[1,8,4,256]{3,2,1,0:T(4,128)}, f32[1,8,4,256]{3,2,1,0:T(4,128)}) custom-call(s32[1]{0:T(128)S(6)} %and.4.parity_ref, f32[128,128]{1,0:T(8,128)S(1)} %get-tuple-element.15.half_ref, f32[128,128]{1,0:T(8,128)S(1)} %collective-permute-done.other_ref, f32[320,128]{1,0:T(8,128)S(1)} %bitcast.10, ...), custom_call_target="tpu_custom_call" | custom-call | flops 3000000000 | bytes 3000000 | tf_op jit(solution)/shard_map/new_vectors/pallas_call | solution.py:481
  100.6 2.1 %all-to-all-done.2 = f32[8,128,128]{2,1,0:T(8,128)S(1)} async-done(((f32[8,128,128]{2,1,0:T(8,128)}), f32[8,128,128]{2,1,0:T(8,128)S(1)}, u32[]{:S(2)}, u32[]{:S(2)}) %all-to-all-start.2) | async-done | bytes 524320 | tf_op jit(solution)/shard_map/all_to_all | solution.py:505
  102.7 0.6 broadcast_multiply_fusion
  (1 shorter events, 0.0 us)
Async XLA Ops:
  3.5 20.2 %copy-start.8 = (f32[4,1,4096]{2,1,0:T(1,128)S(1)}, f32[4,1,4096]{2,1,0:T(1,128)}, u32[]{:S(2)}) copy-start(f32[4,1,4096]{2,1,0:T(1,128)} %param.25) | copy-start | bytes 196612
  3.5 50.6 %all-to-all-start = ((f32[64,1,2176]{2,1,0:T(1,128)}), f32[64,1,2176]{2,1,0:T(1,128)S(1)}, u32[]{:S(2)}, u32[]{:S(2)}) async-start(f32[64,1,2176]{2,1,0:T(1,128)} %bitcast.1), calls=%async_computation | async-start | bytes 1114112 | tf_op jit(solution)/shard_map/all_to_all | solution.py:503
  22.9 0.7 copy-start.9
  59.0 24.0 %all-to-all-start.1 = ((f32[64,1,640]{2,1,0:T(1,128)}), f32[64,1,640]{2,1,0:T(1,128)S(1)}, u32[]{:S(2)}, u32[]{:S(2)}) async-start(f32[64,1,640]{2,1,0:T(1,128)} %bitcast.3), calls=%async_computation.1 | async-start | bytes 327680 | tf_op jit(solution)/shard_map/all_to_all | solution.py:503
  84.7 14.2 %copy-start = (f32[1,8,4,256]{3,2,1,0:T(4,128)S(1)}, f32[1,8,4,256]{3,2,1,0:T(4,128)}, u32[]{:S(2)}) copy-start(f32[1,8,4,256]{3,2,1,0:T(4,128)} %res_ref.1) | copy-start | bytes 98308
  84.7 14.2 %copy-start.1 = (f32[1,8,4,256]{3,2,1,0:T(4,128)S(1)}, f32[1,8,4,256]{3,2,1,0:T(4,128)}, u32[]{:S(2)}) copy-start(f32[1,8,4,256]{3,2,1,0:T(4,128)} %old_ref.1) | copy-start | bytes 98308
  84.7 14.2 %copy-start.2 = (f32[1,8,4,256]{3,2,1,0:T(4,128)S(1)}, f32[1,8,4,256]{3,2,1,0:T(4,128)}, u32[]{:S(2)}) copy-start(f32[1,8,4,256]{3,2,1,0:T(4,128)} %resp_ref.1) | copy-start | bytes 98308
  84.7 14.2 %copy-start.3 = (f32[1,2,16,256]{3,2,1,0:T(8,128)S(1)}, f32[1,2,16,256]{3,2,1,0:T(8,128)}, u32[]{:S(2)}) copy-start(f32[1,2,16,256]{3,2,1,0:T(8,128)} %form_ref.1) | copy-start | bytes 98308
  84.7 14.2 %copy-start.6 = (f32[1,256]{1,0:T(1,128)S(1)}, f32[1,256]{1,0:T(1,128)}, u32[]{:S(2)}) copy-start(f32[1,256]{1,0:T(1,128)} %kin_ref.1) | copy-start | bytes 3076
  84.8 18.0 %all-to-all-start.2 = ((f32[8,128,128]{2,1,0:T(8,128)}), f32[8,128,128]{2,1,0:T(8,128)S(1)}, u32[]{:S(2)}, u32[]{:S(2)}) async-start(f32[8,128,128]{2,1,0:T(8,128)} %bitcast.5), calls=%async_computation.2 | async-start | bytes 1048576 | tf_op jit(solution)/shard_map/all_to_all | solution.py:505
  93.2 5.8 %copy-start.4 = (f32[3,64]{1,0:T(4,128)S(1)}, f32[3,64]{1,0:T(4,128)}, u32[]{:S(2)}) copy-start(f32[3,64]{1,0:T(4,128)} %pos_ref.1) | copy-start | bytes 2308
  93.2 5.8 %copy-start.5 = (s32[1,256]{1,0:T(1,128)S(1)}, s32[1,256]{1,0:T(1,128)}, u32[]{:S(2)}) copy-start(s32[1,256]{1,0:T(1,128)} %index_ref.1) | copy-start | bytes 3076
  93.2 5.8 %copy-start.7 = (f32[1,8]{1,0:T(1,128)S(1)}, f32[1,8]{1,0:T(1,128)}, u32[]{:S(2)}) copy-start(f32[1,8]{1,0:T(1,128)} %energy_ref.1) | copy-start | bytes 100
  93.2 5.7 %collective-permute-start = (f32[128,128]{1,0:T(8,128)S(1)}, f32[128,128]{1,0:T(8,128)S(1)}, u32[]{:S(2)}, u32[]{:S(2)}) collective-permute-start(f32[128,128]{1,0:T(8,128)S(1)} %get-tuple-element.15.half_ref), channel_id=1, source_target_pairs={{0,1},{1,0},{2,3},{3,2},{4,5},{5,4},{6,7},{7,6},{8,9},{9,8},{10,11... | collective-permute-start | bytes 196616 | tf_op jit(solution)/shard_map/ppermute | solution.py:559

commit v3 on v2

--- a/solution.py
+++ b/solution.py
@@ -17,6 +17,8 @@
 EXTRA = 16
 MIRROR = [(i, i ^ 1) for i in range(DEV)]
 HALF = NG // 2
+CH = 2
+CX = HALF // CH
 ALL = COLS * DEV
 ROWS1 = 17
 ROWS2 = 5
@@ -113,13 +115,17 @@
     arrays = (orb_ref, resp_ref, res_ref, old_ref)
     copies = fetch(
         (
-            (orb_hbm, orb_ref), (resp_hbm, resp_ref), (res_hbm, res_ref), (old_hbm, old_ref),
-            (form_hbm, form_ref), (index_hbm, index_ref), (pos_hbm, pos_ref),
+            (index_hbm, index_ref), (pos_hbm, pos_ref), (orb_hbm, orb_ref), (resp_hbm, resp_ref),
+            (res_hbm, res_ref), (old_hbm, old_ref), (form_hbm, form_ref),
         ),
         sems,
     )
     table = depth_table()
-    for copy in copies:
+    for copy in copies[:2]:
+        copy.wait()
+    index = index_ref[...]
+    phases = split(atom_phases(index, pos_ref[...]))
+    for copy in copies[2:]:
         copy.wait()
     lines = jnp.concatenate(
         [ref[0, :, 2 * s + c, :] for c in range(2) for ref in arrays for s in range(2)], axis=0
@@ -130,8 +136,6 @@
         z = dot3(split(jnp.where(group == b, table, 0.0)), lines, "nt")
         out_ref[pl.ds(b, DEV, stride=ROWS1), :] = z[:64] + swap_sign(z[64:])
 
-    index = index_ref[...]
-    phases = split(atom_phases(index, pos_ref[...]))
     form_re, form_im = form_ref[0, 0], form_ref[0, 1]
     for n in range(NB):
         parts_re, parts_im = [], []
@@ -256,10 +260,16 @@
     acc_re = jnp.zeros((16, ALL), F32)
     acc_im = jnp.zeros((16, ALL), F32)
     local = jnp.zeros((NB, 128), F32)
-    for k in range(2):
-        first = k * 16
-        grids = plane_chunk(re, im, first, 16, cos_ref, sin_ref, tables, (high_ref.at[k], low_ref.at[k]))
-        for i in range(16):
+    chunks = []
+    for k in range(CH):
+        chunks.append(plane_chunk(
+            re, im, k * CX, CX, cos_ref, sin_ref, tables, (high_ref.at[k], low_ref.at[k])
+        ))
+    turns = []
+    for k in range(CH):
+        first = k * CX
+        grids = chunks[k]
+        for i in range(CX):
             products = []
             for half in range(2):
                 grid = grids[half]
@@ -277,12 +287,14 @@
                 rows = slice(i * 16 + 8 * j, i * 16 + 8 * j + 8)
                 prod_ref[k, rows, 0:128] = products[0][j] + products[1][j]
                 prod_ref[k, rows, 128:256] = products[0][j] - products[1][j]
-        turned = dot3(split(prod_ref[k]), (table_high[...], table_low[...]), "nt")
-        for i in range(16):
-            cx = cos_ref[first + i : first + i + 1, :]
-            sx = sin_ref[first + i : first + i + 1, :]
-            q_re = turned[i * 16 : (i + 1) * 16, :ALL]
-            q_im = turned[i * 16 : (i + 1) * 16, ALL:]
+        turns.append(dot3(split(prod_ref[k]), (table_high[...], table_low[...]), "nt"))
+    for k in range(CH):
+        for i in range(CX):
+            x = k * CX + i
+            cx = cos_ref[x : x + 1, :]
+            sx = sin_ref[x : x + 1, :]
+            q_re = turns[k][i * 16 : (i + 1) * 16, :ALL]
+            q_im = turns[k][i * 16 : (i + 1) * 16, ALL:]
             acc_re = acc_re + q_re * cx + q_im * sx
             acc_im = acc_im + q_im * cx - q_re * sx
     acc_re = acc_re * VOLUME
@@ -348,44 +360,17 @@
 
 
 def orbital_kernel(
-    recv_ref, grid_ref, cos_ref, sin_ref, table_high, table_low, high_ref, low_ref
+    recv_ref, grid_ref, base_ref, slope_ref, cos_ref, sin_ref, table_high, table_low, high_ref,
+    low_ref,
 ):
     extra = recv_ref[pl.ds(EXTRA, DEV, stride=ROWS1), :]
     x_tables(column_codes(extra), cos_ref, sin_ref)
     y_tables(extra, table_high, table_low)
     values = own_columns(recv_ref)
     re, im = values[0:32], values[64:96]
-
-    def chunk(k, carry):
-        grids = plane_chunk(
-            re, im, k * 8, 8, cos_ref, sin_ref, (table_high, table_low), (high_ref, low_ref)
-        )
-        for half in range(2):
-            place = pl.multiple_of(k * 256 + half * 1024, 256)
-            grid_ref[pl.ds(place, 256), :] = grids[half]
-        return carry
-
-    lax.fori_loop(0, 4, chunk, 0)
-
-
-def step_of(recv_ref, scalars_ref):
-    total = jnp.sum(recv_ref[pl.ds(4, DEV, stride=ROWS2), :], axis=0, keepdims=True)
-    return scalars_ref[:, 0:1] / (row_to_col(total, NB) + SMALL_TERM)
-
-
-def density_kernel(
-    recv_ref, scalars_ref, grid_ref, other_ref, out_ref, half_ref, sum_ref
-):
-    step = jnp.broadcast_to(step_of(recv_ref, scalars_ref), (NB, 128))
     lane = iota((NB, 128), 1)
 
-    def terms(x):
-        base = pl.multiple_of(x * 32, 32)
-        o_up = other_ref[pl.ds(base, 8), :]
-        o_down = other_ref[pl.ds(base + 8, 8), :]
-        half = pl.multiple_of(x * 16, 16)
-        c_up = other_ref[pl.ds(base + 16, 8), :] + step * grid_ref[pl.ds(half, 8), :]
-        c_down = other_ref[pl.ds(base + 24, 8), :] + step * grid_ref[pl.ds(half + 8, 8), :]
+    def terms(o_up, o_down, c_up, c_down):
         same_up = o_up * c_up
         same_down = o_down * c_down
         return (
@@ -395,18 +380,51 @@
             same_up - same_down,
         )
 
-    def pair(p, carry):
-        even = terms(2 * p)
-        odd = terms(2 * p + 1)
-        for m in range(4):
-            both = jnp.where(lane < 64, even[m], odd[m]) + pltpu.roll(
-                jnp.where(lane < 64, odd[m], even[m]), 64, 1
-            )
-            sum_ref[pl.ds(m * 32 + p, 1), :] = 2.0 * jnp.sum(both, axis=0, keepdims=True)
+    def fold(even, odd):
+        return 2.0 * (
+            jnp.where(lane < 64, even, odd)
+            + pltpu.roll(jnp.where(lane < 64, odd, even), 64, 1)
+        )
+
+    def chunk(k, carry):
+        grids = plane_chunk(
+            re, im, k * 8, 8, cos_ref, sin_ref, (table_high, table_low), (high_ref, low_ref)
+        )
+        for half in range(2):
+            for j in range(4):
+                with_response, with_direction = [], []
+                for i in (2 * j, 2 * j + 1):
+                    o_up, o_down, r_up, r_down = (
+                        grids[half][i * 32 + 8 * q : i * 32 + 8 * q + 8] for q in range(4)
+                    )
+                    place = pl.multiple_of((k * 8 + i + 32 * half) * 16, 16)
+                    d_up = grid_ref[pl.ds(place, 8), :]
+                    d_down = grid_ref[pl.ds(place + 8, 8), :]
+                    with_response.append(terms(o_up, o_down, r_up, r_down))
+                    with_direction.append(terms(o_up, o_down, d_up, d_down))
+                for m in range(4):
+                    row = m * 32 + 16 * half + j + 4 * k
+                    base_ref[pl.ds(row, 1), :] = jnp.sum(
+                        fold(with_response[0][m], with_response[1][m]), axis=0, keepdims=True
+                    )
+                    slope_ref[pl.ds(row, NB, stride=128), :] = fold(
+                        with_direction[0][m], with_direction[1][m]
+                    )
         return carry
 
-    lax.fori_loop(0, 32, pair, 0, unroll=8)
-    total = sum_ref[...]
+    lax.fori_loop(0, 4, chunk, 0)
+
+
+def step_of(recv_ref, scalars_ref):
+    total = jnp.sum(recv_ref[pl.ds(4, DEV, stride=ROWS2), :], axis=0, keepdims=True)
+    return scalars_ref[:, 0:1] / (row_to_col(total, NB) + SMALL_TERM)
+
+
+def density_kernel(recv_ref, scalars_ref, base_ref, slope_ref, out_ref, half_ref):
+    step = step_of(recv_ref, scalars_ref)
+    total = base_ref[...]
+    for n in range(NB):
+        total = total + step[n : n + 1, :] * slope_ref[n * 128 : (n + 1) * 128, :]
     for copy in range(8):
         out_ref[copy * 128 : (copy + 1) * 128, :] = total
     for k in range(2):
@@ -541,20 +559,19 @@
             pltpu.SemaphoreType.DMA((6,)),
         ]
         + tables
-        + [pltpu.VMEM((2, 256, 2 * ALL), BF16), pltpu.VMEM((2, 256, 2 * ALL), BF16)]
-        + [pltpu.VMEM((2, 256, 256), F32), pltpu.VMEM((NB, 128), F32)],
+        + [pltpu.VMEM((CH, 512 // CH, 2 * ALL), BF16), pltpu.VMEM((CH, 512 // CH, 2 * ALL), BF16)]
+        + [pltpu.VMEM((CH, 512 // CH, 256), F32), pltpu.VMEM((NB, 128), F32)],
         smem=(1,), hbm=range(4, 10),
     )(recv, me, slots, plane, old_norm, residual, old_direction, kinetic, band_energy, coupling)
     returned = exchange(back, "fft", DEV)
-    other = call(
-        orbital_kernel, shape_of(NG * 32, 128), "orbital_and_response_grid",
+    base, slope = call(
+        orbital_kernel, (shape_of(128, 128), shape_of(NB * 128, 128)), "density_terms",
         tables + [pltpu.VMEM((256, 2 * ALL), BF16), pltpu.VMEM((256, 2 * ALL), BF16)],
         flops=3_000_000_000, size=3_000_000,
-    )(recv)
+    )(recv, grid)
     density, half = call(
-        density_kernel, (shape_of(8 * 128, 128), shape_of(2 * DEV, 128)), "density",
-        [pltpu.VMEM((128, 128), F32)],
-    )(returned, scalars, grid, other)
+        density_kernel, (shape_of(8 * 128, 128), shape_of(2 * DEV, 128)), "density"
+    )(returned, scalars, base, slope)
     gathered = exchange(density, "kpool", 8)
     other_half = lax.ppermute(half, "fft", MIRROR)
     outs = call(

time: 104 us -> 103 us (level)
  no operation moved by 1% of the time
where the time goes in v3:
time: 103 us; the launch traced here: 102 us
  waiting for transfers between devices  47.6 us (46%)
  starting transfers between devices  38.2 us (37%)
  Pallas kernels  13.6 us (13%)
    all_to_all x2, waiting for transfers between devices, exchange(): flat = lax.all_to_all(flat, axis, 0, 0, tiled=True)  42 us
    all_to_all x2, starting transfers between devices, exchange(): flat = lax.all_to_all(flat, axis, 0, 0, tiled=True)  27.5 us
    pallas_call x5, Pallas kernels, run(): pl.pallas_call(kernel, out_shape=outs, in_specs=specs, out_specs=jax.tree...  13.6 us
    all_to_all x1, starting transfers between devices, exchange(): lax.all_to_all(values.reshape(parts, rows, 128), axis, 0, 0, tiled=True)  8.49 us
    ppermute x1, waiting for transfers between devices, per_device(): other_half = lax.ppermute(half, 'fft', MIRROR)  3.47 us
    ppermute x1, starting transfers between devices, per_device(): other_half = lax.ppermute(half, 'fft', MIRROR)  2.25 us
    all_to_all x1, waiting for transfers between devices, exchange(): lax.all_to_all(values.reshape(parts, rows, 128), axis, 0, 0, tiled=True)  2.1 us
  transfers between devices with their start and end apart: 4, of which 4 were waited for; matrix products, arithmetic and copies ran while one was open for 0% of the time, Pallas kernels for 5%

profile of v3, /device:TPU:1, one launch (start us, length us, event | category | flops | bytes accessed | tf_op | source)
XLA Modules:
  0.0 102.0 jit_solution(6862886773842221972)
XLA Ops:
  0.6 2.9 %lines_and_amplitudes.1 = f32[1088,128]{1,0:T(8,128)} custom-call(f32[1,8,4,256]{3,2,1,0:T(4,128)} %orb_hbm.1, f32[1,8,4,256]{3,2,1,0:T(4,128)} %resp_ref.1, f32[1,8,4,256]{3,2,1,0:T(4,128)} %res_ref.1, f32[1,8,4,256]{3,2,1,0:T(4,128)} %old_ref.1, f32[1,2,16,256]{3,2,1,0:T(8,128)} %form_ref.1, s32[1,256]{1,0:T(1,128)} %index_ref.1, f32[3,64]{1,0:T(4,128)} %pos_ref.1), custom_call_target="tpu_custom_call" | custom-call | flops 1 | bytes 1 | tf_op jit(solution)/shard_map/lines_and_amplitudes/pallas_call | solution.py:499
  3.5 0.0 copy-start.8
  3.5 19.4 %all-to-all-start = ((f32[64,1,2176]{2,1,0:T(1,128)}), f32[64,1,2176]{2,1,0:T(1,128)S(1)}, u32[]{:S(2)}, u32[]{:S(2)}) async-start(f32[64,1,2176]{2,1,0:T(1,128)} %bitcast.1), calls=%async_computation | async-start | bytes 1114112 | tf_op jit(solution)/shard_map/all_to_all | solution.py:521
  22.9 0.0 copy-start.9
  23.0 0.7 copy-done.9
  23.6 0.1 reshape.48.slots_ref
  23.7 0.0 copy-done.8
  23.7 0.2 reduce
  23.9 0.1 reshape.49
  24.0 0.1 pad_maximum_fusion.pot_ref
  24.1 30.0 %all-to-all-done = f32[64,1,2176]{2,1,0:T(1,128)S(1)} async-done(((f32[64,1,2176]{2,1,0:T(1,128)}), f32[64,1,2176]{2,1,0:T(1,128)S(1)}, u32[]{:S(2)}, u32[]{:S(2)}) %all-to-all-start) | async-done | bytes 557088 | tf_op jit(solution)/shard_map/all_to_all | solution.py:521
  54.2 4.2 %potential_and_coupling.1 = (f32[320,128]{1,0:T(8,128)}, f32[1024,128]{1,0:T(8,128)S(1)}, f32[8,128]{1,0:T(8,128)S(1)}) custom-call(f32[1088,128]{1,0:T(8,128)S(1)} %bitcast.7, s32[1]{0:T(128)} %bitcast.atom_ref, s32[16,64]{1,0:T(8,128)S(1)} %reshape.48.slots_ref, f32[4,64,128]{2,1,0:T(8,128)S(1)} %pad_maximum_fusion.pot_ref, f32[1,8]{1,0:T(1,128)} %old_norm_hbm.1, ...), custom_call_target="tpu_custom_call" | custom-call | flops 1 | bytes 1 | tf_op jit(solution)/shard_map/potential_and_coupling/pallas_call | solution.py:499
  58.4 8.0 %all-to-all-start.1 = ((f32[64,1,640]{2,1,0:T(1,128)}), f32[64,1,640]{2,1,0:T(1,128)S(1)}, u32[]{:S(2)}, u32[]{:S(2)}) async-start(f32[64,1,640]{2,1,0:T(1,128)} %bitcast.3), calls=%async_computation.1 | async-start | bytes 327680 | tf_op jit(solution)/shard_map/all_to_all | solution.py:521
  66.5 3.9 %density_terms.1 = (f32[128,128]{1,0:T(8,128)S(1)}, f32[1024,128]{1,0:T(8,128)S(1)}) custom-call(f32[1088,128]{1,0:T(8,128)S(1)} %bitcast.8, f32[1024,128]{1,0:T(8,128)S(1)} %get-tuple-element.16.grid_ref), custom_call_target="tpu_custom_call" | custom-call | flops 3000000000 | bytes 3000000 | tf_op jit(solution)/shard_map/density_terms/pallas_call | solution.py:499
  70.4 12.0 %all-to-all-done.1 = f32[64,1,640]{2,1,0:T(1,128)S(1)} async-done(((f32[64,1,640]{2,1,0:T(1,128)}), f32[64,1,640]{2,1,0:T(1,128)S(1)}, u32[]{:S(2)}, u32[]{:S(2)}) %all-to-all-start.1) | async-done | bytes 163872 | tf_op jit(solution)/shard_map/all_to_all | solution.py:521
  82.4 1.0 density.1
  83.4 0.0 copy-start
  83.4 0.0 copy-start.1
  83.4 0.0 copy-start.2
  83.4 0.0 copy-start.3
  83.4 0.0 copy-start.6
  83.4 8.5 %all-to-all-start.2 = ((f32[8,128,128]{2,1,0:T(8,128)}), f32[8,128,128]{2,1,0:T(8,128)S(1)}, u32[]{:S(2)}, u32[]{:S(2)}) async-start(f32[8,128,128]{2,1,0:T(8,128)} %bitcast.5), calls=%async_computation.2 | async-start | bytes 1048576 | tf_op jit(solution)/shard_map/all_to_all | solution.py:523
  91.9 0.0 copy-start.4
  91.9 0.0 copy-start.5
  91.9 0.0 copy-start.7
  91.9 2.2 %collective-permute-start = (f32[128,128]{1,0:T(8,128)S(1)}, f32[128,128]{1,0:T(8,128)S(1)}, u32[]{:S(2)}, u32[]{:S(2)}) collective-permute-start(f32[128,128]{1,0:T(8,128)S(1)} %get-tuple-element.19.half_ref), channel_id=1, source_target_pairs={{0,1},{1,0},{2,3},{3,2},{4,5},{5,4},{6,7},{7,6},{8,9},{9,8},{10,11... | collective-permute-start | bytes 196616 | tf_op jit(solution)/shard_map/ppermute | solution.py:576
  94.1 3.5 %collective-permute-done.other_ref = f32[128,128]{1,0:T(8,128)S(1)} collective-permute-done((f32[128,128]{1,0:T(8,128)S(1)}, f32[128,128]{1,0:T(8,128)S(1)}, u32[]{:S(2)}, u32[]{:S(2)}) %collective-permute-start) | collective-permute-done | bytes 65568 | tf_op jit(solution)/shard_map/ppermute | solution.py:576
  97.6 0.0 copy-done
  97.6 0.0 copy-done.1
  97.6 0.0 copy-done.2
  97.6 0.0 copy-done.3
  97.6 0.0 copy-done.6
  97.6 0.0 copy-done.4
  97.7 0.0 copy-done.5
  97.7 0.0 copy-done.7
  97.7 1.6 %new_vectors.1 = (f32[1,8,4,256]{3,2,1,0:T(4,128)}, f32[1,8,4,256]{3,2,1,0:T(4,128)}, f32[1,8,4,256]{3,2,1,0:T(4,128)}) custom-call(s32[1]{0:T(128)S(6)} %and.4.parity_ref, f32[128,128]{1,0:T(8,128)S(1)} %get-tuple-element.19.half_ref, f32[128,128]{1,0:T(8,128)S(1)} %collective-permute-done.other_ref, f32[320,128]{1,0:T(8,128)S(1)} %bitcast.10, ...), custom_call_target="tpu_custom_call" | custom-call | flops 3000000000 | bytes 3000000 | tf_op jit(solution)/shard_map/new_vectors/pallas_call | solution.py:499
  99.2 2.1 %all-to-all-done.2 = f32[8,128,128]{2,1,0:T(8,128)S(1)} async-done(((f32[8,128,128]{2,1,0:T(8,128)}), f32[8,128,128]{2,1,0:T(8,128)S(1)}, u32[]{:S(2)}, u32[]{:S(2)}) %all-to-all-start.2) | async-done | bytes 524320 | tf_op jit(solution)/shard_map/all_to_all | solution.py:523
  101.4 0.6 broadcast_multiply_fusion
  (1 shorter events, 0.0 us)
Async XLA Ops:
  3.5 20.2 %copy-start.8 = (f32[4,1,4096]{2,1,0:T(1,128)S(1)}, f32[4,1,4096]{2,1,0:T(1,128)}, u32[]{:S(2)}) copy-start(f32[4,1,4096]{2,1,0:T(1,128)} %param.25) | copy-start | bytes 196612
  3.5 50.6 %all-to-all-start = ((f32[64,1,2176]{2,1,0:T(1,128)}), f32[64,1,2176]{2,1,0:T(1,128)S(1)}, u32[]{:S(2)}, u32[]{:S(2)}) async-start(f32[64,1,2176]{2,1,0:T(1,128)} %bitcast.1), calls=%async_computation | async-start | bytes 1114112 | tf_op jit(solution)/shard_map/all_to_all | solution.py:521
  22.9 0.7 copy-start.9
  58.4 24.0 %all-to-all-start.1 = ((f32[64,1,640]{2,1,0:T(1,128)}), f32[64,1,640]{2,1,0:T(1,128)S(1)}, u32[]{:S(2)}, u32[]{:S(2)}) async-start(f32[64,1,640]{2,1,0:T(1,128)} %bitcast.3), calls=%async_computation.1 | async-start | bytes 327680 | tf_op jit(solution)/shard_map/all_to_all | solution.py:521
  83.4 14.3 %copy-start = (f32[1,8,4,256]{3,2,1,0:T(4,128)S(1)}, f32[1,8,4,256]{3,2,1,0:T(4,128)}, u32[]{:S(2)}) copy-start(f32[1,8,4,256]{3,2,1,0:T(4,128)} %res_ref.1) | copy-start | bytes 98308
  83.4 14.3 %copy-start.1 = (f32[1,8,4,256]{3,2,1,0:T(4,128)S(1)}, f32[1,8,4,256]{3,2,1,0:T(4,128)}, u32[]{:S(2)}) copy-start(f32[1,8,4,256]{3,2,1,0:T(4,128)} %old_ref.1) | copy-start | bytes 98308
  83.4 14.3 %copy-start.2 = (f32[1,8,4,256]{3,2,1,0:T(4,128)S(1)}, f32[1,8,4,256]{3,2,1,0:T(4,128)}, u32[]{:S(2)}) copy-start(f32[1,8,4,256]{3,2,1,0:T(4,128)} %resp_ref.1) | copy-start | bytes 98308
  83.4 14.3 %copy-start.3 = (f32[1,2,16,256]{3,2,1,0:T(8,128)S(1)}, f32[1,2,16,256]{3,2,1,0:T(8,128)}, u32[]{:S(2)}) copy-start(f32[1,2,16,256]{3,2,1,0:T(8,128)} %form_ref.1) | copy-start | bytes 98308
  83.4 14.3 %copy-start.6 = (f32[1,256]{1,0:T(1,128)S(1)}, f32[1,256]{1,0:T(1,128)}, u32[]{:S(2)}) copy-start(f32[1,256]{1,0:T(1,128)} %kin_ref.1) | copy-start | bytes 3076
  83.4 18.0 %all-to-all-start.2 = ((f32[8,128,128]{2,1,0:T(8,128)}), f32[8,128,128]{2,1,0:T(8,128)S(1)}, u32[]{:S(2)}, u32[]{:S(2)}) async-start(f32[8,128,128]{2,1,0:T(8,128)} %bitcast.5), calls=%async_computation.2 | async-start | bytes 1048576 | tf_op jit(solution)/shard_map/all_to_all | solution.py:523
  91.9 5.8 %copy-start.4 = (f32[3,64]{1,0:T(4,128)S(1)}, f32[3,64]{1,0:T(4,128)}, u32[]{:S(2)}) copy-start(f32[3,64]{1,0:T(4,128)} %pos_ref.1) | copy-start | bytes 2308
  91.9 5.8 %copy-start.5 = (s32[1,256]{1,0:T(1,128)S(1)}, s32[1,256]{1,0:T(1,128)}, u32[]{:S(2)}) copy-start(s32[1,256]{1,0:T(1,128)} %index_ref.1) | copy-start | bytes 3076
  91.9 5.8 %copy-start.7 = (f32[1,8]{1,0:T(1,128)S(1)}, f32[1,8]{1,0:T(1,128)}, u32[]{:S(2)}) copy-start(f32[1,8]{1,0:T(1,128)} %energy_ref.1) | copy-start | bytes 100
  91.9 5.7 %collective-permute-start = (f32[128,128]{1,0:T(8,128)S(1)}, f32[128,128]{1,0:T(8,128)S(1)}, u32[]{:S(2)}, u32[]{:S(2)}) collective-permute-start(f32[128,128]{1,0:T(8,128)S(1)} %get-tuple-element.19.half_ref), channel_id=1, source_target_pairs={{0,1},{1,0},{2,3},{3,2},{4,5},{5,4},{6,7},{7,6},{8,9},{9,8},{10,11... | collective-permute-start | bytes 196616 | tf_op jit(solution)/shard_map/ppermute | solution.py:576

commit v4 on v3

--- a/solution.py
+++ b/solution.py
@@ -14,13 +14,18 @@
 PW = COLS * STICK
 PA = 16
 DEV = 64
-EXTRA = 16
+ZS = 16
+YS = 4
+EXTRA = 40
+SAME_Z = [[z * YS + y for y in range(YS)] for z in range(ZS)]
+SAME_Y = [[z * YS + y for z in range(ZS)] for y in range(YS)]
 MIRROR = [(i, i ^ 1) for i in range(DEV)]
 HALF = NG // 2
 CH = 2
 CX = HALF // CH
 ALL = COLS * DEV
-ROWS1 = 17
+STAGE1 = 16 * ZS + 8
+STAGE2 = 41
 ROWS2 = 5
 SMALL_TERM = 1e-06
 VOLUME = 1.0 / (NG * NG * NG)
@@ -91,19 +96,27 @@
     return jnp.where(g < 32, g, g - 64).astype(F32)
 
 
-def atom_phases(index, positions):
+def device_order(i):
+    return ((i & 15) << 2) | (i >> 4)
+
+
+def atom_phases(index, positions, order=lambda i: i):
     fx = signed(index >> 12)
     fy = signed((index >> 6) & 63)
     fz = signed(index & 63)
-    tx, ty, tz = (row_to_col(positions[i : i + 1, :], NG) for i in range(3))
+    mine = iota((NG, NG), 1) == order(iota((NG, NG), 0))
+    tx, ty, tz = (
+        jnp.sum(jnp.where(mine, positions[i : i + 1, :], 0.0), axis=1, keepdims=True)
+        for i in range(3)
+    )
     turns = tx * fx + ty * fy + tz * fz
     cosine, sine = trig_turns(turns)
     return jnp.concatenate([cosine, sine], axis=0)
 
 
-def depth_table():
+def depth_table(order=lambda i: i):
     shape = (NG, PW)
-    wound = iota(shape, 0) * ((iota(shape, 1) & 31) - 16)
+    wound = order(iota(shape, 0)) * ((iota(shape, 1) & 31) - 16)
     cosine, sine = trig_wound(wound)
     return jnp.concatenate([cosine, sine], axis=0)
 
@@ -112,6 +125,10 @@
     orb_hbm, resp_hbm, res_hbm, old_hbm, form_hbm, index_hbm, pos_hbm, out_ref,
     orb_ref, resp_ref, res_ref, old_ref, form_ref, index_ref, pos_ref, sems,
 ):
+    def store(r, value):
+        for y in range(YS):
+            out_ref[pl.ds(y * STAGE1 + r, ZS, stride=16), :] = value[y * ZS : (y + 1) * ZS]
+
     arrays = (orb_ref, resp_ref, res_ref, old_ref)
     copies = fetch(
         (
@@ -120,11 +137,11 @@
         ),
         sems,
     )
-    table = depth_table()
+    table = depth_table(device_order)
     for copy in copies[:2]:
         copy.wait()
     index = index_ref[...]
-    phases = split(atom_phases(index, pos_ref[...]))
+    phases = split(atom_phases(index, pos_ref[...], device_order))
     for copy in copies[2:]:
         copy.wait()
     lines = jnp.concatenate(
@@ -134,7 +151,7 @@
     group = iota(table.shape, 1) >> 5
     for b in range(COLS):
         z = dot3(split(jnp.where(group == b, table, 0.0)), lines, "nt")
-        out_ref[pl.ds(b, DEV, stride=ROWS1), :] = z[:64] + swap_sign(z[64:])
+        store(b, z[:64] + swap_sign(z[64:]))
 
     form_re, form_im = form_ref[0, 0], form_ref[0, 1]
     for n in range(NB):
@@ -147,7 +164,7 @@
                 parts_im.append(form_re * d_im - form_im * d_re)
         values = split(jnp.concatenate(parts_re + parts_im, axis=0))
         z = dot3(phases, values, "nt")
-        out_ref[pl.ds(COLS + n, DEV, stride=ROWS1), :] = z[:64] + swap_sign(z[64:])
+        store(COLS + n, z[:64] + swap_sign(z[64:]))
 
     squares = jnp.zeros((NB, PW), F32)
     for comp in range(4):
@@ -160,27 +177,64 @@
     for b in range(COLS):
         code = jnp.sum(jnp.where(lane == STICK * b, codes, 0.0), axis=1, keepdims=True)
         row = jnp.where(target == COLS + b, code, row)
-    out_ref[pl.ds(EXTRA, DEV, stride=ROWS1), :] = jnp.broadcast_to(row, (DEV, 128))
+    for y in range(YS):
+        out_ref[(y + 1) * STAGE1 - 8 : (y + 1) * STAGE1, :] = jnp.broadcast_to(row, (8, 128))
+
+
+def regroup_kernel(in_ref, out_ref):
+    for y in range(YS):
+        for b in range(COLS):
+            out_ref[pl.ds(y * COLS + b, ZS, stride=STAGE2), :] = in_ref[
+                pl.ds(y * STAGE1 + b, ZS, stride=16), :
+            ]
+    for n in range(NB):
+        parts = [in_ref[pl.ds(y * STAGE1 + COLS + n, ZS, stride=16), :] for y in range(YS)]
+        out_ref[pl.ds(YS * COLS + n, ZS, stride=STAGE2), :] = (
+            (parts[0] + parts[1]) + (parts[2] + parts[3])
+        )
+    lane = iota((8, 128), 1)
+    row = jnp.zeros((8, 128), F32)
+    for y in range(YS):
+        extra = in_ref[(y + 1) * STAGE1 - 8 : (y + 1) * STAGE1, :]
+        row = row + jnp.where(lane < NB, extra, 0.0)
+        first = NB + y * COLS
+        moved = extra if y == 0 else pltpu.roll(extra, y * COLS, 1)
+        row = row + jnp.where((lane >= first) & (lane < first + COLS), moved, 0.0)
+    out_ref[pl.ds(EXTRA, ZS, stride=STAGE2), :] = jnp.concatenate([row, row], axis=0)
 
 
 def own_columns(recv_ref):
     values = jnp.concatenate(
-        [recv_ref[pl.ds(b, DEV, stride=ROWS1), :] for b in range(COLS)], axis=0
+        [
+            recv_ref[pl.ds(y * COLS + b, ZS, stride=STAGE2), :]
+            for b in range(COLS)
+            for y in range(YS)
+        ],
+        axis=0,
     )
     return values.T
 
 
 def column_codes(extra):
-    turned = extra.T
-    codes = jnp.concatenate(
-        [turned[COLS + b : COLS + b + 1, :] for b in range(COLS)], axis=1
-    ).astype(jnp.int32)
-    return codes
+    codes = extra.astype(jnp.int32)
+    shape = (128, ALL)
+    lane = iota(shape, 1)
+    pick = jnp.where(iota(shape, 0) == NB + ((lane >> 4) & 3) * COLS + (lane >> 6), 1.0, 0.0)
+    mine = (iota((ZS, ALL), 1) & 15) == iota((ZS, ALL), 0)
+    used = iota((ZS, 128), 1) >= NB
+    parts = []
+    for value in (codes >> 6, codes & 63):
+        value = jnp.where(used, value, 0).astype(F32).astype(BF16)
+        spread = dot(value, pick.astype(BF16))
+        parts.append(
+            jnp.sum(jnp.where(mine, spread, 0.0), axis=0, keepdims=True).astype(jnp.int32)
+        )
+    return parts
 
 
 def x_tables(codes, cos_ref, sin_ref):
     shape = (HALF, ALL)
-    cosine, sine = trig_wound(iota(shape, 0) * (codes >> 6))
+    cosine, sine = trig_wound(iota(shape, 0) * codes[0])
     cos_ref[...] = cosine
     sin_ref[...] = sine
 
@@ -189,7 +243,8 @@
     shape = (DEV, 128)
     lane = iota(shape, 1)
     for b in range(COLS):
-        code = extra[:, COLS + b : COLS + b + 1].astype(jnp.int32)
+        lanes = [NB + y * COLS + b for y in range(YS)]
+        code = jnp.concatenate([extra[:, i : i + 1] for i in lanes], axis=0).astype(jnp.int32)
         wound = (code & 63) * (lane & 63)
         cosine, sine = trig_wound(wound)
         odd = jnp.broadcast_to(((code >> 6) & 1) == 1, shape)
@@ -243,7 +298,13 @@
         ),
         sems,
     )
-    extra = recv_ref[pl.ds(EXTRA, DEV, stride=ROWS1), :]
+    def store(r, value):
+        for y in range(YS):
+            out_ref[pl.ds(y * ROWS2 + r, ZS, stride=YS * ROWS2), :] = value[
+                y * ZS : (y + 1) * ZS
+            ]
+
+    extra = recv_ref[pl.ds(EXTRA, ZS, stride=STAGE2), :]
     codes = column_codes(extra)
     x_tables(codes, cos_ref, sin_ref)
     y_tables(extra, table_high, table_low)
@@ -304,10 +365,10 @@
         for b in range(4 * r, 4 * r + 4):
             lanes = slice(b * DEV, (b + 1) * DEV)
             pieces += [acc_re[:, lanes], acc_im[:, lanes]]
-        out_ref[pl.ds(r, DEV, stride=ROWS2), :] = jnp.concatenate(pieces, axis=0).T
+        store(r, jnp.concatenate(pieces, axis=0).T)
 
     sums = [
-        jnp.sum(recv_ref[pl.ds(COLS + n, DEV, stride=ROWS1), :], axis=0, keepdims=True)
+        jnp.sum(recv_ref[pl.ds(YS * COLS + n, ZS, stride=STAGE2), :], axis=0, keepdims=True)
         for n in range(NB)
     ]
     amps = jnp.concatenate(sums, axis=0)
@@ -338,11 +399,9 @@
     first_half = pair_ref[pl.ds(0, 4, stride=2), :]
     second_half = pair_ref[pl.ds(1, 4, stride=2), :]
     packed = first_half + pltpu.roll(second_half, 64, 1)
-    odd = (iota((DEV, 128), 0) & 1) == 1
+    odd = ((iota((DEV, 128), 0) >> 4) & 1) == 1
     for k in range(2):
-        out_ref[pl.ds(2 + k, DEV, stride=ROWS2), :] = jnp.where(
-            odd, packed[2 + k : 3 + k], packed[k : k + 1]
-        )
+        store(2 + k, jnp.where(odd, packed[2 + k : 3 + k], packed[k : k + 1]))
 
     curvature = jnp.sum(local, axis=1, keepdims=True) * VOLUME
     curvature = curvature + jnp.sum(amp_re * q_re + amp_im * q_im, axis=1, keepdims=True)
@@ -352,9 +411,7 @@
         d = res_ref[0, :, comp, :] + beta * old_ref[0, :, comp, :]
         own = own + d * d
     curvature = curvature + jnp.sum(own * weight, axis=1, keepdims=True)
-    out_ref[pl.ds(4, DEV, stride=ROWS2), :] = jnp.broadcast_to(
-        col_to_row(curvature, 128), (DEV, 128)
-    )
+    store(4, jnp.broadcast_to(col_to_row(curvature, 128), (DEV, 128)))
     lane = iota((NB, 128), 1)
     scalars_ref[...] = jnp.where(lane == 0, norm, jnp.where(lane == 1, beta, 0.0))
 
@@ -363,7 +420,7 @@
     recv_ref, grid_ref, base_ref, slope_ref, cos_ref, sin_ref, table_high, table_low, high_ref,
     low_ref,
 ):
-    extra = recv_ref[pl.ds(EXTRA, DEV, stride=ROWS1), :]
+    extra = recv_ref[pl.ds(EXTRA, ZS, stride=STAGE2), :]
     x_tables(column_codes(extra), cos_ref, sin_ref)
     y_tables(extra, table_high, table_low)
     values = own_columns(recv_ref)
@@ -514,13 +571,15 @@
     return jax.ShapeDtypeStruct(dims, F32)
 
 
-def exchange(values, axis, parts):
+def exchange(values, axis, parts, groups=None):
     rows = values.shape[0] // parts
     if rows % 8:
         flat = values.reshape(parts, 1, rows * 128)
-        flat = lax.all_to_all(flat, axis, 0, 0, tiled=True)
+        flat = lax.all_to_all(flat, axis, 0, 0, tiled=True, axis_index_groups=groups)
         return flat.reshape(values.shape)
-    out = lax.all_to_all(values.reshape(parts, rows, 128), axis, 0, 0, tiled=True)
+    out = lax.all_to_all(
+        values.reshape(parts, rows, 128), axis, 0, 0, tiled=True, axis_index_groups=groups
+    )
     return out.reshape(values.shape)
 
 
@@ -537,14 +596,16 @@
     parity = me & 1
     vector = pltpu.VMEM((1, NB, 4, PW), F32)
     sent = call(
-        send_kernel, shape_of(DEV * ROWS1, 128), "lines_and_amplitudes",
+        send_kernel, shape_of(YS * STAGE1, 128), "lines_and_amplitudes",
         [vector] * 4 + [
             pltpu.VMEM((1, 2, PA, PW), F32), pltpu.VMEM((1, PW), jnp.int32),
             pltpu.VMEM((3, NG), F32), pltpu.SemaphoreType.DMA((7,)),
         ],
         hbm=range(7),
     )(orbitals, response, residual, old_direction, form_factor, sphere_index, atom_positions)
-    recv = exchange(sent, "fft", DEV)
+    near = exchange(sent, "fft", YS, SAME_Z)
+    joined = call(regroup_kernel, shape_of(ZS * STAGE2, 128), "regroup")(near)
+    recv = exchange(joined, "fft", ZS, SAME_Y)
     tables = [
         pltpu.VMEM((HALF, ALL), F32), pltpu.VMEM((HALF, ALL), F32),
         pltpu.VMEM((2 * ALL, 256), BF16), pltpu.VMEM((2 * ALL, 256), BF16),

time: 103 us -> 101 us (0.981)
  waiting for transfers between devices: 47.6 us -> 30.2 us
  blocking collectives: 0 us -> 11.8 us
  starting transfers between devices: 38.2 us -> 41.7 us
    all_to_all x3, waiting for transfers between devices: 44.1 us -> 26.7 us  [the longest x2 24.6 us: exchange(): lax.all_to_all(flat, axis, 0, 0, tiled=True, axis_index_groups=groups)]
    all_to_all x0 -> x1, blocking collectives: none -> 11.8 us  [exchange(): lax.all_to_all(values.reshape(parts, rows, 128), axis, 0, 0, tiled=True,...]
    all_to_all x3, starting transfers between devices: 36 us -> 39.4 us  [the longest x2 30.9 us: exchange(): lax.all_to_all(flat, axis, 0, 0, tiled=True, axis_index_groups=groups)]
    pallas_call x5 -> x6, Pallas kernels: 13.6 us -> 13.8 us  [run(): pl.pallas_call(kernel, out_shape=outs, in_specs=specs, out_specs=jax.tree...]
  transfers between devices with their start and end apart: 4 -> 4, of which waited for: 4 -> 4; matrix products, arithmetic and copies ran while one was open for 0% -> 0% of each run, Pallas kernels for 5% -> 6%
where the time goes in v4:
time: 101 us; the launch traced here: 100 us
  starting transfers between devices  41.7 us (41%)
  waiting for transfers between devices  30.2 us (30%)
  Pallas kernels  13.8 us (14%)
  blocking collectives  11.8 us (12%)
    all_to_all x2, starting transfers between devices, exchange(): lax.all_to_all(flat, axis, 0, 0, tiled=True, axis_index_groups=groups)  30.9 us
    all_to_all x2, waiting for transfers between devices, exchange(): lax.all_to_all(flat, axis, 0, 0, tiled=True, axis_index_groups=groups)  24.6 us
    pallas_call x6, Pallas kernels, run(): pl.pallas_call(kernel, out_shape=outs, in_specs=specs, out_specs=jax.tree...  13.8 us
    all_to_all x1, blocking collectives, exchange(): lax.all_to_all(values.reshape(parts, rows, 128), axis, 0, 0, tiled=True,...  11.8 us
    all_to_all x1, starting transfers between devices, exchange(): lax.all_to_all(values.reshape(parts, rows, 128), axis, 0, 0, tiled=True,...  8.52 us
    ppermute x1, waiting for transfers between devices, per_device(): other_half = lax.ppermute(half, 'fft', MIRROR)  3.47 us
    ppermute x1, starting transfers between devices, per_device(): other_half = lax.ppermute(half, 'fft', MIRROR)  2.25 us
    all_to_all x1, waiting for transfers between devices, exchange(): lax.all_to_all(values.reshape(parts, rows, 128), axis, 0, 0, tiled=True,...  2.1 us
  transfers between devices with their start and end apart: 4, of which 4 were waited for; matrix products, arithmetic and copies ran while one was open for 0% of the time, Pallas kernels for 6%

profile of v4, /device:TPU:1, one launch (start us, length us, event | category | flops | bytes accessed | tf_op | source)
XLA Modules:
  0.0 100.1 jit_solution(9221747607937551957)
XLA Ops:
  0.6 2.1 %lines_and_amplitudes.1 = f32[1056,128]{1,0:T(8,128)S(1)} custom-call(f32[1,8,4,256]{3,2,1,0:T(4,128)} %orb_hbm.1, f32[1,8,4,256]{3,2,1,0:T(4,128)} %resp_ref.1, f32[1,8,4,256]{3,2,1,0:T(4,128)} %res_ref.1, f32[1,8,4,256]{3,2,1,0:T(4,128)} %old_ref.1, f32[1,2,16,256]{3,2,1,0:T(8,128)} %form_ref.1, s32[1,256]{1,0:T(1,128)} %index_ref.1, f32[3,64]{1,0:T(4,128)} %pos_ref.1), custom_call_target="tpu_custom_call" | custom-call | flops 1 | bytes 1 | tf_op jit(solution)/shard_map/lines_and_amplitudes/pallas_call | solution.py:556
  2.8 11.8 %all_to_all.20 = f32[4,264,128]{2,1,0:T(8,128)S(1)} all-to-all(f32[4,264,128]{2,1,0:T(8,128)S(1)} %bitcast.10), channel_id=1, replica_groups={{0,1,2,3},{4,5,6,7},{8,9,10,11},{12,13,14,15},{16,17,18,19},{20,21,22,2..., dimensions={0} | all-to-all | bytes 1081344 | tf_op jit(solution)/shard_map/all_to_all | solution.py:580
  14.6 0.9 regroup.1
  15.5 0.0 copy-start.8
  15.5 16.7 %all-to-all-start.1 = ((f32[16,1,5248]{2,1,0:T(1,128)}), f32[16,1,5248]{2,1,0:T(1,128)S(1)}, u32[]{:S(2)}, u32[]{:S(2)}) async-start(f32[16,1,5248]{2,1,0:T(1,128)} %bitcast.3), calls=%async_computation.1 | async-start | bytes 671744 | tf_op jit(solution)/shard_map/all_to_all | solution.py:578
  32.2 0.0 copy-start.9
  32.2 0.7 copy-done.9
  32.9 0.1 reshape.56.slots_ref
  33.0 0.0 copy-done.8
  33.0 0.2 reduce
  33.2 0.1 reshape.57
  33.3 0.1 pad_maximum_fusion.pot_ref
  33.4 12.7 %all-to-all-done.1 = f32[16,1,5248]{2,1,0:T(1,128)S(1)} async-done(((f32[16,1,5248]{2,1,0:T(1,128)}), f32[16,1,5248]{2,1,0:T(1,128)S(1)}, u32[]{:S(2)}, u32[]{:S(2)}) %all-to-all-start.1) | async-done | bytes 335904 | tf_op jit(solution)/shard_map/all_to_all | solution.py:578
  46.1 4.2 %potential_and_coupling.1 = (f32[320,128]{1,0:T(8,128)}, f32[1024,128]{1,0:T(8,128)S(1)}, f32[8,128]{1,0:T(8,128)S(1)}) custom-call(f32[656,128]{1,0:T(8,128)S(1)} %bitcast.11, s32[1]{0:T(128)} %bitcast.atom_ref, s32[16,64]{1,0:T(8,128)S(1)} %reshape.56.slots_ref, f32[4,64,128]{2,1,0:T(8,128)S(1)} %pad_maximum_fusion.pot_ref, f32[1,8]{1,0:T(1,128)} %old_norm_hbm.1, ...), custom_call_target="tpu_custom_call" | custom-call | flops 1 | bytes 1 | tf_op jit(solution)/shard_map/potential_and_coupling/pallas_call | solution.py:556
  50.3 14.2 %all-to-all-start.2 = ((f32[64,1,640]{2,1,0:T(1,128)}), f32[64,1,640]{2,1,0:T(1,128)S(1)}, u32[]{:S(2)}, u32[]{:S(2)}) async-start(f32[64,1,640]{2,1,0:T(1,128)} %bitcast.5), calls=%async_computation.2 | async-start | bytes 327680 | tf_op jit(solution)/shard_map/all_to_all | solution.py:578
  64.5 3.9 %density_terms.1 = (f32[128,128]{1,0:T(8,128)S(1)}, f32[1024,128]{1,0:T(8,128)S(1)}) custom-call(f32[656,128]{1,0:T(8,128)S(1)} %bitcast.12, f32[1024,128]{1,0:T(8,128)S(1)} %get-tuple-element.16.grid_ref), custom_call_target="tpu_custom_call" | custom-call | flops 3000000000 | bytes 3000000 | tf_op jit(solution)/shard_map/density_terms/pallas_call | solution.py:556
  68.5 11.9 %all-to-all-done.2 = f32[64,1,640]{2,1,0:T(1,128)S(1)} async-done(((f32[64,1,640]{2,1,0:T(1,128)}), f32[64,1,640]{2,1,0:T(1,128)S(1)}, u32[]{:S(2)}, u32[]{:S(2)}) %all-to-all-start.2) | async-done | bytes 163872 | tf_op jit(solution)/shard_map/all_to_all | solution.py:578
  80.4 1.0 density.1
  81.4 0.0 copy-start
  81.4 0.0 copy-start.1
  81.4 0.0 copy-start.2
  81.4 0.0 copy-start.3
  81.4 0.0 copy-start.6
  81.4 8.5 %all-to-all-start.3 = ((f32[8,128,128]{2,1,0:T(8,128)}), f32[8,128,128]{2,1,0:T(8,128)S(1)}, u32[]{:S(2)}, u32[]{:S(2)}) async-start(f32[8,128,128]{2,1,0:T(8,128)} %bitcast.7), calls=%async_computation.3 | async-start | bytes 1048576 | tf_op jit(solution)/shard_map/all_to_all | solution.py:580
  89.9 0.0 copy-start.4
  89.9 0.0 copy-start.5
  89.9 0.0 copy-start.7
  89.9 2.3 %collective-permute-start = (f32[128,128]{1,0:T(8,128)S(1)}, f32[128,128]{1,0:T(8,128)S(1)}, u32[]{:S(2)}, u32[]{:S(2)}) collective-permute-start(f32[128,128]{1,0:T(8,128)S(1)} %get-tuple-element.19.half_ref), channel_id=1, source_target_pairs={{0,1},{1,0},{2,3},{3,2},{4,5},{5,4},{6,7},{7,6},{8,9},{9,8},{10,11... | collective-permute-start | bytes 196616 | tf_op jit(solution)/shard_map/ppermute | solution.py:637
  92.2 3.5 %collective-permute-done.other_ref = f32[128,128]{1,0:T(8,128)S(1)} collective-permute-done((f32[128,128]{1,0:T(8,128)S(1)}, f32[128,128]{1,0:T(8,128)S(1)}, u32[]{:S(2)}, u32[]{:S(2)}) %collective-permute-start) | collective-permute-done | bytes 65568 | tf_op jit(solution)/shard_map/ppermute | solution.py:637
  95.7 0.0 copy-done
  95.7 0.0 copy-done.1
  95.7 0.0 copy-done.2
  95.7 0.0 copy-done.3
  95.7 0.0 copy-done.6
  95.7 0.0 copy-done.4
  95.7 0.0 copy-done.5
  95.7 0.0 copy-done.7
  95.7 1.6 %new_vectors.1 = (f32[1,8,4,256]{3,2,1,0:T(4,128)}, f32[1,8,4,256]{3,2,1,0:T(4,128)}, f32[1,8,4,256]{3,2,1,0:T(4,128)}) custom-call(s32[1]{0:T(128)S(6)} %and.4.parity_ref, f32[128,128]{1,0:T(8,128)S(1)} %get-tuple-element.19.half_ref, f32[128,128]{1,0:T(8,128)S(1)} %collective-permute-done.other_ref, f32[320,128]{1,0:T(8,128)S(1)} %bitcast.14, ...), custom_call_target="tpu_custom_call" | custom-call | flops 3000000000 | bytes 3000000 | tf_op jit(solution)/shard_map/new_vectors/pallas_call | solution.py:556
  97.3 2.1 %all-to-all-done.3 = f32[8,128,128]{2,1,0:T(8,128)S(1)} async-done(((f32[8,128,128]{2,1,0:T(8,128)}), f32[8,128,128]{2,1,0:T(8,128)S(1)}, u32[]{:S(2)}, u32[]{:S(2)}) %all-to-all-start.3) | async-done | bytes 524320 | tf_op jit(solution)/shard_map/all_to_all | solution.py:580
  99.4 0.6 broadcast_multiply_fusion
  (1 shorter events, 0.0 us)
Async XLA Ops:
  15.5 17.5 %copy-start.8 = (f32[4,1,4096]{2,1,0:T(1,128)S(1)}, f32[4,1,4096]{2,1,0:T(1,128)}, u32[]{:S(2)}) copy-start(f32[4,1,4096]{2,1,0:T(1,128)} %param.25) | copy-start | bytes 196612
  15.5 30.6 %all-to-all-start.1 = ((f32[16,1,5248]{2,1,0:T(1,128)}), f32[16,1,5248]{2,1,0:T(1,128)S(1)}, u32[]{:S(2)}, u32[]{:S(2)}) async-start(f32[16,1,5248]{2,1,0:T(1,128)} %bitcast.3), calls=%async_computation.1 | async-start | bytes 671744 | tf_op jit(solution)/shard_map/all_to_all | solution.py:578
  32.2 0.7 copy-start.9
  50.3 30.1 %all-to-all-start.2 = ((f32[64,1,640]{2,1,0:T(1,128)}), f32[64,1,640]{2,1,0:T(1,128)S(1)}, u32[]{:S(2)}, u32[]{:S(2)}) async-start(f32[64,1,640]{2,1,0:T(1,128)} %bitcast.5), calls=%async_computation.2 | async-start | bytes 327680 | tf_op jit(solution)/shard_map/all_to_all | solution.py:578
  81.4 14.3 %copy-start = (f32[1,8,4,256]{3,2,1,0:T(4,128)S(1)}, f32[1,8,4,256]{3,2,1,0:T(4,128)}, u32[]{:S(2)}) copy-start(f32[1,8,4,256]{3,2,1,0:T(4,128)} %res_ref.1) | copy-start | bytes 98308
  81.4 14.3 %copy-start.1 = (f32[1,8,4,256]{3,2,1,0:T(4,128)S(1)}, f32[1,8,4,256]{3,2,1,0:T(4,128)}, u32[]{:S(2)}) copy-start(f32[1,8,4,256]{3,2,1,0:T(4,128)} %old_ref.1) | copy-start | bytes 98308
  81.4 14.3 %copy-start.2 = (f32[1,8,4,256]{3,2,1,0:T(4,128)S(1)}, f32[1,8,4,256]{3,2,1,0:T(4,128)}, u32[]{:S(2)}) copy-start(f32[1,8,4,256]{3,2,1,0:T(4,128)} %resp_ref.1) | copy-start | bytes 98308
  81.4 14.3 %copy-start.3 = (f32[1,2,16,256]{3,2,1,0:T(8,128)S(1)}, f32[1,2,16,256]{3,2,1,0:T(8,128)}, u32[]{:S(2)}) copy-start(f32[1,2,16,256]{3,2,1,0:T(8,128)} %form_ref.1) | copy-start | bytes 98308
  81.4 14.3 %copy-start.6 = (f32[1,256]{1,0:T(1,128)S(1)}, f32[1,256]{1,0:T(1,128)}, u32[]{:S(2)}) copy-start(f32[1,256]{1,0:T(1,128)} %kin_ref.1) | copy-start | bytes 3076
  81.4 18.0 %all-to-all-start.3 = ((f32[8,128,128]{2,1,0:T(8,128)}), f32[8,128,128]{2,1,0:T(8,128)S(1)}, u32[]{:S(2)}, u32[]{:S(2)}) async-start(f32[8,128,128]{2,1,0:T(8,128)} %bitcast.7), calls=%async_computation.3 | async-start | bytes 1048576 | tf_op jit(solution)/shard_map/all_to_all | solution.py:580
  89.9 5.8 %copy-start.4 = (f32[3,64]{1,0:T(4,128)S(1)}, f32[3,64]{1,0:T(4,128)}, u32[]{:S(2)}) copy-start(f32[3,64]{1,0:T(4,128)} %pos_ref.1) | copy-start | bytes 2308
  89.9 5.8 %copy-start.5 = (s32[1,256]{1,0:T(1,128)S(1)}, s32[1,256]{1,0:T(1,128)}, u32[]{:S(2)}) copy-start(s32[1,256]{1,0:T(1,128)} %index_ref.1) | copy-start | bytes 3076
  89.9 5.8 %copy-start.7 = (f32[1,8]{1,0:T(1,128)S(1)}, f32[1,8]{1,0:T(1,128)}, u32[]{:S(2)}) copy-start(f32[1,8]{1,0:T(1,128)} %energy_ref.1) | copy-start | bytes 100
  89.9 5.7 %collective-permute-start = (f32[128,128]{1,0:T(8,128)S(1)}, f32[128,128]{1,0:T(8,128)S(1)}, u32[]{:S(2)}, u32[]{:S(2)}) collective-permute-start(f32[128,128]{1,0:T(8,128)S(1)} %get-tuple-element.19.half_ref), channel_id=1, source_target_pairs={{0,1},{1,0},{2,3},{3,2},{4,5},{5,4},{6,7},{7,6},{8,9},{9,8},{10,11... | collective-permute-start | bytes 196616 | tf_op jit(solution)/shard_map/ppermute | solution.py:637

commit v5 on v4

--- a/solution.py
+++ b/solution.py
@@ -284,17 +284,22 @@
     return copies
 
 
+def twice(row, half):
+    lane = iota(row.shape, 1)
+    return jnp.where((lane >= 64) == (half == 1), row, pltpu.roll(row, 64, 1))
+
+
 def potential_kernel(
-    recv_ref, atom_ref, slots_ref, pot_ref, old_norm_hbm, res_hbm, old_hbm, kin_hbm,
+    recv_ref, atom_ref, slots_hbm, pot_hbm, old_norm_hbm, res_hbm, old_hbm, kin_hbm,
     energy_hbm, coup_hbm,
     out_ref, grid_ref, scalars_ref,
-    old_norm_ref, res_ref, old_ref, kin_ref, energy_ref, coup_ref, sems,
+    slots_ref, pot_ref, old_norm_ref, res_ref, old_ref, kin_ref, energy_ref, coup_ref, sems,
     cos_ref, sin_ref, table_high, table_low, high_ref, low_ref, prod_ref, pair_ref,
 ):
     copies = fetch(
         (
-            (old_norm_hbm, old_norm_ref), (res_hbm, res_ref), (old_hbm, old_ref),
-            (kin_hbm, kin_ref), (energy_hbm, energy_ref), (coup_hbm, coup_ref),
+            (pot_hbm, pot_ref), (old_norm_hbm, old_norm_ref), (res_hbm, res_ref),
+            (old_hbm, old_ref), (slots_hbm, slots_ref), (kin_hbm, kin_ref), (energy_hbm, energy_ref), (coup_hbm, coup_ref),
         ),
         sems,
     )
@@ -339,7 +344,10 @@
                 down = grid[i * 16 + 8 : i * 16 + 16]
                 grid_ref[x * 16 : x * 16 + 8, :] = up
                 grid_ref[x * 16 + 8 : x * 16 + 16, :] = down
-                v0, bx, by, bz = (pot_ref[m, x : x + 1, :] for m in range(4))
+                v0, bx, by, bz = (
+                    twice(pot_ref[m, :, x // 2 * 128 : x // 2 * 128 + 128], x % 2)
+                    for m in range(4)
+                )
                 new_up = (v0 + bz) * up + bx * down - by * swap_sign(down)
                 new_down = bx * up + by * swap_sign(up) + (v0 - bz) * down
                 local = local + up * new_up + down * new_down
@@ -374,13 +382,15 @@
     amps = jnp.concatenate(sums, axis=0)
     amps = amps + beta * pltpu.roll(amps, 96, 1)
     amp_re, amp_im = amps[:, 0:32], amps[:, 64:96]
-    count = jnp.sum(
-        jnp.where(slots_ref[...] == atom_ref[0], 1.0, 0.0), axis=1, keepdims=True
-    )
-    shape = (PA, 32)
-    count = jnp.sum(
-        jnp.where((iota(shape, 1) & 15) == iota(shape, 0), count, 0.0), axis=0, keepdims=True
-    )
+    here = jnp.where(slots_ref[...] == atom_ref[0], 1.0, 0.0)
+    lane = iota(here.shape, 1)
+    count = jnp.zeros((1, 32), F32)
+    for half in range(2):
+        mine = jnp.sum(jnp.where((lane >= 64) == (half == 1), here, 0.0), axis=1, keepdims=True)
+        place = 2 * iota((8, 32), 0) + half
+        count = count + jnp.sum(
+            jnp.where((iota((8, 32), 1) & 15) == place, mine, 0.0), axis=0, keepdims=True
+        )
     h_re = 0.5 * (coup_ref[0] + coup_ref[0].T)
     h_im = 0.5 * (coup_ref[1] - coup_ref[1].T)
     by_re, by_im = amp_re * count, amp_im * count
@@ -589,9 +599,7 @@
 ):
     scale = 1.0 / (8 * 16384)
     me = lax.axis_index("fft").reshape(1).astype(jnp.int32)
-    slots = proj_atom.reshape(PA, NG)
-    plane = potential.reshape(4, NG, NG)
-    plane = jnp.concatenate([plane, plane], axis=2)
+    slots = proj_atom.reshape(8, 128)
 
     parity = me & 1
     vector = pltpu.VMEM((1, NB, 4, PW), F32)
@@ -603,6 +611,7 @@
         ],
         hbm=range(7),
     )(orbitals, response, residual, old_direction, form_factor, sphere_index, atom_positions)
+    sent, me, parity = lax.optimization_barrier((sent, me, parity))
     near = exchange(sent, "fft", YS, SAME_Z)
     joined = call(regroup_kernel, shape_of(ZS * STAGE2, 128), "regroup")(near)
     recv = exchange(joined, "fft", ZS, SAME_Y)
@@ -615,15 +624,16 @@
         (shape_of(DEV * ROWS2, 128), shape_of(NG * 16, 128), shape_of(NB, 128)),
         "potential_and_coupling",
         [
+            pltpu.VMEM((8, 128), jnp.int32), pltpu.VMEM((4, 1, NG * NG), F32),
             pltpu.VMEM((1, NB), F32), vector, vector, pltpu.VMEM((1, PW), F32),
             pltpu.VMEM((1, NB), F32), pltpu.VMEM((2, 32, 32), F32),
-            pltpu.SemaphoreType.DMA((6,)),
+            pltpu.SemaphoreType.DMA((8,)),
         ]
         + tables
         + [pltpu.VMEM((CH, 512 // CH, 2 * ALL), BF16), pltpu.VMEM((CH, 512 // CH, 2 * ALL), BF16)]
         + [pltpu.VMEM((CH, 512 // CH, 256), F32), pltpu.VMEM((NB, 128), F32)],
-        smem=(1,), hbm=range(4, 10),
-    )(recv, me, slots, plane, old_norm, residual, old_direction, kinetic, band_energy, coupling)
+        smem=(1,), hbm=range(2, 10),
+    )(recv, me, slots, potential, old_norm, residual, old_direction, kinetic, band_energy, coupling)
     returned = exchange(back, "fft", DEV)
     base, slope = call(
         orbital_kernel, (shape_of(128, 128), shape_of(NB * 128, 128)), "density_terms",

time: 101 us -> 99.7 us (0.987)
  blocking collectives: 11.8 us -> 42.1 us
  starting transfers between devices: 41.7 us -> 25 us
  waiting for transfers between devices: 30.2 us -> 17.5 us
    all_to_all x0 -> x1, blocking collectives: none -> 30.3 us  [exchange(): lax.all_to_all(flat, axis, 0, 0, tiled=True, axis_index_groups=groups)]
    all_to_all x2 -> x1, starting transfers between devices: 30.9 us -> 14.2 us  [exchange(): lax.all_to_all(flat, axis, 0, 0, tiled=True, axis_index_groups=groups)]
    all_to_all x2 -> x1, waiting for transfers between devices: 24.6 us -> 11.9 us  [exchange(): lax.all_to_all(flat, axis, 0, 0, tiled=True, axis_index_groups=groups)]
  transfers between devices with their start and end apart: 4 -> 3, of which waited for: 4 -> 3; matrix products, arithmetic and copies ran while one was open for 0% -> 0% of each run, Pallas kernels for 6% -> 6%
where the time goes in v5:
time: 99.7 us; the launch traced here: 99.1 us
  blocking collectives  42.1 us (42%)
  starting transfers between devices  25 us (25%)
  waiting for transfers between devices  17.5 us (18%)
  Pallas kernels  13.1 us (13%)
    all_to_all x1, blocking collectives, exchange(): lax.all_to_all(flat, axis, 0, 0, tiled=True, axis_index_groups=groups)  30.3 us
    all_to_all x1, starting transfers between devices, exchange(): lax.all_to_all(flat, axis, 0, 0, tiled=True, axis_index_groups=groups)  14.2 us
    pallas_call x6, Pallas kernels, run(): pl.pallas_call(kernel, out_shape=outs, in_specs=specs, out_specs=jax.tree...  13.1 us
    all_to_all x1, waiting for transfers between devices, exchange(): lax.all_to_all(flat, axis, 0, 0, tiled=True, axis_index_groups=groups)  11.9 us
    all_to_all x1, blocking collectives, exchange(): lax.all_to_all(values.reshape(parts, rows, 128), axis, 0, 0, tiled=True,...  11.9 us
    all_to_all x1, starting transfers between devices, exchange(): lax.all_to_all(values.reshape(parts, rows, 128), axis, 0, 0, tiled=True,...  8.52 us
    ppermute x1, waiting for transfers between devices, per_device(): other_half = lax.ppermute(half, 'fft', MIRROR)  3.45 us
    ppermute x1, starting transfers between devices, per_device(): other_half = lax.ppermute(half, 'fft', MIRROR)  2.24 us
  transfers between devices with their start and end apart: 3, of which 3 were waited for; matrix products, arithmetic and copies ran while one was open for 0% of the time, Pallas kernels for 6%

profile of v5, /device:TPU:1, one launch (start us, length us, event | category | flops | bytes accessed | tf_op | source)
XLA Modules:
  0.0 99.1 jit_solution(3921132078694068482)
XLA Ops:
  0.6 2.1 %lines_and_amplitudes.1 = f32[1056,128]{1,0:T(8,128)S(1)} custom-call(f32[1,8,4,256]{3,2,1,0:T(4,128)} %orb_hbm.1, f32[1,8,4,256]{3,2,1,0:T(4,128)} %resp_ref.1, f32[1,8,4,256]{3,2,1,0:T(4,128)} %res_ref.1, f32[1,8,4,256]{3,2,1,0:T(4,128)} %old_ref.1, f32[1,2,16,256]{3,2,1,0:T(8,128)} %form_ref.1, s32[1,256]{1,0:T(1,128)} %index_ref.1, f32[3,64]{1,0:T(4,128)} %pos_ref.1), custom_call_target="tpu_custom_call" | custom-call | flops 1 | bytes 1 | tf_op jit(solution)/shard_map/lines_and_amplitudes/pallas_call | solution.py:566
  2.8 11.9 %all_to_all.20 = f32[4,264,128]{2,1,0:T(8,128)S(1)} all-to-all(f32[4,264,128]{2,1,0:T(8,128)S(1)} %bitcast.11), channel_id=1, replica_groups={{0,1,2,3},{4,5,6,7},{8,9,10,11},{12,13,14,15},{16,17,18,19},{20,21,22,2..., dimensions={0} | all-to-all | bytes 1081344 | tf_op jit(solution)/shard_map/all_to_all | solution.py:590
  14.6 0.2 regroup.1
  14.8 30.3 %all_to_all.21 = f32[16,1,5248]{2,1,0:T(1,128)S(1)} all-to-all(f32[16,1,5248]{2,1,0:T(1,128)S(1)} %bitcast.14), channel_id=1, replica_groups={{0,4,8,12,16,20,24,28,32,36,40,44,48,52,56,60},{1,5,9,13,17,21,25,29,33..., dimensions={0} | all-to-all | bytes 671744 | tf_op jit(solution)/shard_map/all_to_all | solution.py:588
  45.0 4.3 %potential_and_coupling.1 = (f32[320,128]{1,0:T(8,128)}, f32[1024,128]{1,0:T(8,128)S(1)}, f32[8,128]{1,0:T(8,128)S(1)}) custom-call(f32[656,128]{1,0:T(8,128)S(1)} %bitcast.12, s32[1]{0:T(128)} %bitcast.atom_ref, s32[8,128]{1,0:T(8,128)} %bitcast.18, f32[4,1,4096]{2,1,0:T(1,128)} %pot_hbm.1, f32[1,8]{1,0:T(1,128)} %old_norm_hbm.1, f32[1,8,4,256]{3,2,1,0:T(4,128)} %res_ref.1, ...), custom_call_target="tpu_custom_call" | custom-call | flops 1 | bytes 1 | tf_op jit(solution)/shard_map/potential_and_coupling/pallas_call | solution.py:566
  49.4 14.2 %all-to-all-start.2 = ((f32[64,1,640]{2,1,0:T(1,128)}), f32[64,1,640]{2,1,0:T(1,128)S(1)}, u32[]{:S(2)}, u32[]{:S(2)}) async-start(f32[64,1,640]{2,1,0:T(1,128)} %bitcast.6), calls=%async_computation.2 | async-start | bytes 327680 | tf_op jit(solution)/shard_map/all_to_all | solution.py:588
  63.6 3.9 %density_terms.1 = (f32[128,128]{1,0:T(8,128)S(1)}, f32[1024,128]{1,0:T(8,128)S(1)}) custom-call(f32[656,128]{1,0:T(8,128)S(1)} %bitcast.13, f32[1024,128]{1,0:T(8,128)S(1)} %get-tuple-element.22.grid_ref), custom_call_target="tpu_custom_call" | custom-call | flops 3000000000 | bytes 3000000 | tf_op jit(solution)/shard_map/density_terms/pallas_call | solution.py:566
  67.5 11.9 %all-to-all-done.2 = f32[64,1,640]{2,1,0:T(1,128)S(1)} async-done(((f32[64,1,640]{2,1,0:T(1,128)}), f32[64,1,640]{2,1,0:T(1,128)S(1)}, u32[]{:S(2)}, u32[]{:S(2)}) %all-to-all-start.2) | async-done | bytes 163872 | tf_op jit(solution)/shard_map/all_to_all | solution.py:588
  79.4 1.0 density.1
  80.4 0.0 copy-start
  80.4 0.0 copy-start.1
  80.4 0.0 copy-start.2
  80.4 0.0 copy-start.3
  80.4 0.0 copy-start.4
  80.4 0.0 copy-start.6
  80.5 8.5 %all-to-all-start.3 = ((f32[8,128,128]{2,1,0:T(8,128)}), f32[8,128,128]{2,1,0:T(8,128)S(1)}, u32[]{:S(2)}, u32[]{:S(2)}) async-start(f32[8,128,128]{2,1,0:T(8,128)} %bitcast.8), calls=%async_computation.3 | async-start | bytes 1048576 | tf_op jit(solution)/shard_map/all_to_all | solution.py:590
  89.0 0.0 copy-start.5
  89.0 0.0 copy-start.7
  89.0 2.2 %collective-permute-start = (f32[128,128]{1,0:T(8,128)S(1)}, f32[128,128]{1,0:T(8,128)S(1)}, u32[]{:S(2)}, u32[]{:S(2)}) collective-permute-start(f32[128,128]{1,0:T(8,128)S(1)} %get-tuple-element.25.half_ref), channel_id=1, source_target_pairs={{0,1},{1,0},{2,3},{3,2},{4,5},{5,4},{6,7},{7,6},{8,9},{9,8},{10,11... | collective-permute-start | bytes 196616 | tf_op jit(solution)/shard_map/ppermute | solution.py:647
  91.2 3.5 %collective-permute-done.other_ref = f32[128,128]{1,0:T(8,128)S(1)} collective-permute-done((f32[128,128]{1,0:T(8,128)S(1)}, f32[128,128]{1,0:T(8,128)S(1)}, u32[]{:S(2)}, u32[]{:S(2)}) %collective-permute-start) | collective-permute-done | bytes 65568 | tf_op jit(solution)/shard_map/ppermute | solution.py:647
  94.7 0.0 copy-done
  94.7 0.0 copy-done.1
  94.7 0.0 copy-done.2
  94.7 0.0 copy-done.3
  94.7 0.0 copy-done.4
  94.7 0.0 copy-done.6
  94.7 0.0 copy-done.5
  94.7 0.0 copy-done.7
  94.7 1.6 %new_vectors.1 = (f32[1,8,4,256]{3,2,1,0:T(4,128)}, f32[1,8,4,256]{3,2,1,0:T(4,128)}, f32[1,8,4,256]{3,2,1,0:T(4,128)}) custom-call(s32[1]{0:T(128)S(6)} %and.4.parity_ref, f32[128,128]{1,0:T(8,128)S(1)} %get-tuple-element.25.half_ref, f32[128,128]{1,0:T(8,128)S(1)} %collective-permute-done.other_ref, f32[320,128]{1,0:T(8,128)S(1)} %bitcast.16, ...), custom_call_target="tpu_custom_call" | custom-call | flops 3000000000 | bytes 3000000 | tf_op jit(solution)/shard_map/new_vectors/pallas_call | solution.py:566
  96.3 2.1 %all-to-all-done.3 = f32[8,128,128]{2,1,0:T(8,128)S(1)} async-done(((f32[8,128,128]{2,1,0:T(8,128)}), f32[8,128,128]{2,1,0:T(8,128)S(1)}, u32[]{:S(2)}, u32[]{:S(2)}) %all-to-all-start.3) | async-done | bytes 524320 | tf_op jit(solution)/shard_map/all_to_all | solution.py:590
  98.5 0.6 broadcast_multiply_fusion
  (1 shorter events, 0.0 us)
Async XLA Ops:
  49.4 30.1 %all-to-all-start.2 = ((f32[64,1,640]{2,1,0:T(1,128)}), f32[64,1,640]{2,1,0:T(1,128)S(1)}, u32[]{:S(2)}, u32[]{:S(2)}) async-start(f32[64,1,640]{2,1,0:T(1,128)} %bitcast.6), calls=%async_computation.2 | async-start | bytes 327680 | tf_op jit(solution)/shard_map/all_to_all | solution.py:588
  80.4 14.3 %copy-start = (f32[1,8,4,256]{3,2,1,0:T(4,128)S(1)}, f32[1,8,4,256]{3,2,1,0:T(4,128)}, u32[]{:S(2)}) copy-start(f32[1,8,4,256]{3,2,1,0:T(4,128)} %res_ref.1) | copy-start | bytes 98308
  80.4 14.3 %copy-start.1 = (f32[1,8,4,256]{3,2,1,0:T(4,128)S(1)}, f32[1,8,4,256]{3,2,1,0:T(4,128)}, u32[]{:S(2)}) copy-start(f32[1,8,4,256]{3,2,1,0:T(4,128)} %old_ref.1) | copy-start | bytes 98308
  80.4 14.3 %copy-start.2 = (f32[1,8,4,256]{3,2,1,0:T(4,128)S(1)}, f32[1,8,4,256]{3,2,1,0:T(4,128)}, u32[]{:S(2)}) copy-start(f32[1,8,4,256]{3,2,1,0:T(4,128)} %resp_ref.1) | copy-start | bytes 98308
  80.4 14.3 %copy-start.3 = (f32[1,2,16,256]{3,2,1,0:T(8,128)S(1)}, f32[1,2,16,256]{3,2,1,0:T(8,128)}, u32[]{:S(2)}) copy-start(f32[1,2,16,256]{3,2,1,0:T(8,128)} %form_ref.1) | copy-start | bytes 98308
  80.4 14.3 %copy-start.4 = (f32[3,64]{1,0:T(4,128)S(1)}, f32[3,64]{1,0:T(4,128)}, u32[]{:S(2)}) copy-start(f32[3,64]{1,0:T(4,128)} %pos_ref.1) | copy-start | bytes 2308
  80.4 14.3 %copy-start.6 = (f32[1,256]{1,0:T(1,128)S(1)}, f32[1,256]{1,0:T(1,128)}, u32[]{:S(2)}) copy-start(f32[1,256]{1,0:T(1,128)} %kin_ref.1) | copy-start | bytes 3076
  80.5 18.0 %all-to-all-start.3 = ((f32[8,128,128]{2,1,0:T(8,128)}), f32[8,128,128]{2,1,0:T(8,128)S(1)}, u32[]{:S(2)}, u32[]{:S(2)}) async-start(f32[8,128,128]{2,1,0:T(8,128)} %bitcast.8), calls=%async_computation.3 | async-start | bytes 1048576 | tf_op jit(solution)/shard_map/all_to_all | solution.py:590
  89.0 5.8 %copy-start.5 = (s32[1,256]{1,0:T(1,128)S(1)}, s32[1,256]{1,0:T(1,128)}, u32[]{:S(2)}) copy-start(s32[1,256]{1,0:T(1,128)} %index_ref.1) | copy-start | bytes 3076
  89.0 5.8 %copy-start.7 = (f32[1,8]{1,0:T(1,128)S(1)}, f32[1,8]{1,0:T(1,128)}, u32[]{:S(2)}) copy-start(f32[1,8]{1,0:T(1,128)} %energy_ref.1) | copy-start | bytes 100
  89.0 5.7 %collective-permute-start = (f32[128,128]{1,0:T(8,128)S(1)}, f32[128,128]{1,0:T(8,128)S(1)}, u32[]{:S(2)}, u32[]{:S(2)}) collective-permute-start(f32[128,128]{1,0:T(8,128)S(1)} %get-tuple-element.25.half_ref), channel_id=1, source_target_pairs={{0,1},{1,0},{2,3},{3,2},{4,5},{5,4},{6,7},{7,6},{8,9},{9,8},{10,11... | collective-permute-start | bytes 196616 | tf_op jit(solution)/shard_map/ppermute | solution.py:647

commit v6 on v5

--- a/solution.py
+++ b/solution.py
@@ -17,8 +17,14 @@
 ZS = 16
 YS = 4
 EXTRA = 40
-SAME_Z = [[z * YS + y for y in range(YS)] for z in range(ZS)]
-SAME_Y = [[z * YS + y for z in range(ZS)] for y in range(YS)]
+FIRST_Z = 8
+FIRST_Y = 2
+ORDER_Z = [(z + FIRST_Z) % ZS for z in range(ZS)]
+ORDER_Y = [(y + FIRST_Y) % YS for y in range(YS)]
+SAME_Z = [[z * YS + y for y in ORDER_Y] for z in range(ZS)]
+SAME_Y = [[z * YS + y for z in ORDER_Z] for y in range(YS)]
+EVERY = [[z * YS + y for z in ORDER_Z for y in ORDER_Y]]
+POINTS = [[4, 5, 6, 7, 0, 1, 2, 3]]
 MIRROR = [(i, i ^ 1) for i in range(DEV)]
 HALF = NG // 2
 CH = 2
@@ -96,8 +102,16 @@
     return jnp.where(g < 32, g, g - 64).astype(F32)
 
 
-def device_order(i):
-    return ((i & 15) << 2) | (i >> 4)
+def device_at(z, y):
+    return (((z + FIRST_Z) & 15) << 2) | ((y + FIRST_Y) & 3)
+
+
+def by_y(i):
+    return device_at(i & 15, i >> 4)
+
+
+def by_z(i):
+    return device_at(i >> 2, i & 3)
 
 
 def atom_phases(index, positions, order=lambda i: i):
@@ -137,11 +151,11 @@
         ),
         sems,
     )
-    table = depth_table(device_order)
+    table = depth_table(by_y)
     for copy in copies[:2]:
         copy.wait()
     index = index_ref[...]
-    phases = split(atom_phases(index, pos_ref[...], device_order))
+    phases = split(atom_phases(index, pos_ref[...], by_y))
     for copy in copies[2:]:
         copy.wait()
     lines = jnp.concatenate(
@@ -504,7 +518,7 @@
 ):
     step = step_of(recv_ref, scalars_ref)
     beta = scalars_ref[:, 1:2]
-    table = depth_table()
+    table = depth_table(by_z)
     table = split(jnp.concatenate([table[:64], table[64:]], axis=1))
     group = iota((32, PW), 1) >> 5
     local = jnp.zeros((32, PW), F32)
@@ -517,7 +531,7 @@
             part = jnp.concatenate([re_c + im_s, im_c - re_s], axis=0)
             local = local + jnp.where(group == 4 * r + i, part, 0.0)
 
-    phases = atom_phases(index_ref[...], pos_ref[...])
+    phases = atom_phases(index_ref[...], pos_ref[...], by_z)
     phases = split(jnp.concatenate([phases[:64], phases[64:]], axis=1))
     form_re, form_im = form_ref[0, 0], form_ref[0, 1]
     rows_re, rows_im = [[], []], [[], []]
@@ -634,7 +648,7 @@
         + [pltpu.VMEM((CH, 512 // CH, 256), F32), pltpu.VMEM((NB, 128), F32)],
         smem=(1,), hbm=range(2, 10),
     )(recv, me, slots, potential, old_norm, residual, old_direction, kinetic, band_energy, coupling)
-    returned = exchange(back, "fft", DEV)
+    returned = exchange(back, "fft", DEV, EVERY)
     base, slope = call(
         orbital_kernel, (shape_of(128, 128), shape_of(NB * 128, 128)), "density_terms",
         tables + [pltpu.VMEM((256, 2 * ALL), BF16), pltpu.VMEM((256, 2 * ALL), BF16)],
@@ -643,7 +657,7 @@
     density, half = call(
         density_kernel, (shape_of(8 * 128, 128), shape_of(2 * DEV, 128)), "density"
     )(returned, scalars, base, slope)
-    gathered = exchange(density, "kpool", 8)
+    gathered = exchange(density, "kpool", 8, POINTS)
     other_half = lax.ppermute(half, "fft", MIRROR)
     outs = call(
         finish_kernel, (shape_of(1, NB, 4, PW),) * 3, "new_vectors",

time: 99.7 us -> 92.6 us (0.929)
  waiting for transfers between devices: 17.5 us -> 5.32 us
  blocking collectives: 42.1 us -> 46 us
  starting transfers between devices: 25 us -> 26.2 us
    all_to_all x1, waiting for transfers between devices: 11.9 us -> 2.9 us  [exchange(): lax.all_to_all(flat, axis, 0, 0, tiled=True, axis_index_groups=groups)]
    all_to_all x1, blocking collectives: 30.3 us -> 35.5 us  [exchange(): lax.all_to_all(flat, axis, 0, 0, tiled=True, axis_index_groups=groups)]
    all_to_all x1, waiting for transfers between devices: 2.14 us -> 0.01 us  [exchange(): lax.all_to_all(values.reshape(parts, rows, 128), axis, 0, 0, tiled=True,...]
    all_to_all x1, blocking collectives: 11.9 us -> 10.5 us  [exchange(): lax.all_to_all(values.reshape(parts, rows, 128), axis, 0, 0, tiled=True,...]
    ppermute x1, waiting for transfers between devices: 3.45 us -> 2.41 us  [per_device(): other_half = lax.ppermute(half, 'fft', MIRROR)]
  transfers between devices with their start and end apart: 3 -> 3, of which waited for: 3 -> 2; matrix products, arithmetic and copies ran while one was open for 0% -> 0% of each run, Pallas kernels for 6% -> 6%
where the time goes in v6:
time: 92.6 us; the launch traced here: 92.1 us
  blocking collectives  46 us (50%)
  starting transfers between devices  26.2 us (28%)
  Pallas kernels  13.1 us (14%)
  waiting for transfers between devices  5.32 us (6%)
    all_to_all x1, blocking collectives, exchange(): lax.all_to_all(flat, axis, 0, 0, tiled=True, axis_index_groups=groups)  35.5 us
    all_to_all x1, starting transfers between devices, exchange(): lax.all_to_all(flat, axis, 0, 0, tiled=True, axis_index_groups=groups)  15.1 us
    pallas_call x6, Pallas kernels, run(): pl.pallas_call(kernel, out_shape=outs, in_specs=specs, out_specs=jax.tree...  13.1 us
    all_to_all x1, blocking collectives, exchange(): lax.all_to_all(values.reshape(parts, rows, 128), axis, 0, 0, tiled=True,...  10.5 us
    all_to_all x1, starting transfers between devices, exchange(): lax.all_to_all(values.reshape(parts, rows, 128), axis, 0, 0, tiled=True,...  8.13 us
    ppermute x1, starting transfers between devices, per_device(): other_half = lax.ppermute(half, 'fft', MIRROR)  3 us
    all_to_all x1, waiting for transfers between devices, exchange(): lax.all_to_all(flat, axis, 0, 0, tiled=True, axis_index_groups=groups)  2.9 us
    ppermute x1, waiting for transfers between devices, per_device(): other_half = lax.ppermute(half, 'fft', MIRROR)  2.41 us
  transfers between devices with their start and end apart: 3, of which 2 were waited for; matrix products, arithmetic and copies ran while one was open for 0% of the time, Pallas kernels for 6%

profile of v6, /device:TPU:1, one launch (start us, length us, event | category | flops | bytes accessed | tf_op | source)
XLA Modules:
  0.0 92.1 jit_solution(16724546323370000279)
XLA Ops:
  0.6 2.1 %lines_and_amplitudes.1 = f32[1056,128]{1,0:T(8,128)S(1)} custom-call(f32[1,8,4,256]{3,2,1,0:T(4,128)} %orb_hbm.1, f32[1,8,4,256]{3,2,1,0:T(4,128)} %resp_ref.1, f32[1,8,4,256]{3,2,1,0:T(4,128)} %res_ref.1, f32[1,8,4,256]{3,2,1,0:T(4,128)} %old_ref.1, f32[1,2,16,256]{3,2,1,0:T(8,128)} %form_ref.1, s32[1,256]{1,0:T(1,128)} %index_ref.1, f32[3,64]{1,0:T(4,128)} %pos_ref.1), custom_call_target="tpu_custom_call" | custom-call | flops 1 | bytes 1 | tf_op jit(solution)/shard_map/lines_and_amplitudes/pallas_call | solution.py:580
  2.8 10.5 %all_to_all.20 = f32[4,264,128]{2,1,0:T(8,128)S(1)} all-to-all(f32[4,264,128]{2,1,0:T(8,128)S(1)} %bitcast.11), channel_id=1, replica_groups={{2,3,0,1},{6,7,4,5},{10,11,8,9},{14,15,12,13},{18,19,16,17},{22,23,20,2..., dimensions={0} | all-to-all | bytes 1081344 | tf_op jit(solution)/shard_map/all_to_all | solution.py:604
  13.2 0.2 regroup.1
  13.4 35.5 %all_to_all.21 = f32[16,1,5248]{2,1,0:T(1,128)S(1)} all-to-all(f32[16,1,5248]{2,1,0:T(1,128)S(1)} %bitcast.14), channel_id=1, replica_groups={{32,36,40,44,48,52,56,60,0,4,8,12,16,20,24,28},{33,37,41,45,49,53,57,61..., dimensions={0} | all-to-all | bytes 671744 | tf_op jit(solution)/shard_map/all_to_all | solution.py:602
  48.9 4.3 %potential_and_coupling.1 = (f32[320,128]{1,0:T(8,128)}, f32[1024,128]{1,0:T(8,128)S(1)}, f32[8,128]{1,0:T(8,128)S(1)}) custom-call(f32[656,128]{1,0:T(8,128)S(1)} %bitcast.12, s32[1]{0:T(128)} %bitcast.atom_ref, s32[8,128]{1,0:T(8,128)} %bitcast.18, f32[4,1,4096]{2,1,0:T(1,128)} %pot_hbm.1, f32[1,8]{1,0:T(1,128)} %old_norm_hbm.1, f32[1,8,4,256]{3,2,1,0:T(4,128)} %res_ref.1, ...), custom_call_target="tpu_custom_call" | custom-call | flops 1 | bytes 1 | tf_op jit(solution)/shard_map/potential_and_coupling/pallas_call | solution.py:580
  53.2 15.1 %all-to-all-start.2 = ((f32[64,1,640]{2,1,0:T(1,128)}), f32[64,1,640]{2,1,0:T(1,128)S(1)}, u32[]{:S(2)}, u32[]{:S(2)}) async-start(f32[64,1,640]{2,1,0:T(1,128)} %bitcast.6), calls=%async_computation.2 | async-start | bytes 327680 | tf_op jit(solution)/shard_map/all_to_all | solution.py:602
  68.3 3.9 %density_terms.1 = (f32[128,128]{1,0:T(8,128)S(1)}, f32[1024,128]{1,0:T(8,128)S(1)}) custom-call(f32[656,128]{1,0:T(8,128)S(1)} %bitcast.13, f32[1024,128]{1,0:T(8,128)S(1)} %get-tuple-element.22.grid_ref), custom_call_target="tpu_custom_call" | custom-call | flops 3000000000 | bytes 3000000 | tf_op jit(solution)/shard_map/density_terms/pallas_call | solution.py:580
  72.3 2.9 %all-to-all-done.2 = f32[64,1,640]{2,1,0:T(1,128)S(1)} async-done(((f32[64,1,640]{2,1,0:T(1,128)}), f32[64,1,640]{2,1,0:T(1,128)S(1)}, u32[]{:S(2)}, u32[]{:S(2)}) %all-to-all-start.2) | async-done | bytes 163872 | tf_op jit(solution)/shard_map/all_to_all | solution.py:602
  75.2 1.0 %density.1 = (f32[1024,128]{1,0:T(8,128)}, f32[128,128]{1,0:T(8,128)S(1)}) custom-call(f32[320,128]{1,0:T(8,128)S(1)} %bitcast.15, f32[8,128]{1,0:T(8,128)S(1)} %get-tuple-element.21.scalars_ref, f32[128,128]{1,0:T(8,128)S(1)} %get-tuple-element.23.base_ref, f32[1024,128]{1,0:T(8,128)S(1)} %get-tuple-element.24.slope_ref), custom_call_target="tpu_custom_call" | custom-call | flops 1 | bytes 1 | tf_op jit(solution)/shard_map/density/pallas_call | solution.py:580
  76.2 0.0 copy-start
  76.2 0.0 copy-start.1
  76.2 0.0 copy-start.2
  76.2 0.0 copy-start.3
  76.2 0.0 copy-start.4
  76.2 0.0 copy-start.6
  76.2 8.1 %all-to-all-start.3 = ((f32[8,128,128]{2,1,0:T(8,128)}), f32[8,128,128]{2,1,0:T(8,128)S(1)}, u32[]{:S(2)}, u32[]{:S(2)}) async-start(f32[8,128,128]{2,1,0:T(8,128)} %bitcast.8), calls=%async_computation.3 | async-start | bytes 1048576 | tf_op jit(solution)/shard_map/all_to_all | solution.py:604
  84.3 0.0 copy-start.5
  84.3 0.0 copy-start.7
  84.4 3.0 %collective-permute-start = (f32[128,128]{1,0:T(8,128)S(1)}, f32[128,128]{1,0:T(8,128)S(1)}, u32[]{:S(2)}, u32[]{:S(2)}) collective-permute-start(f32[128,128]{1,0:T(8,128)S(1)} %get-tuple-element.25.half_ref), channel_id=1, source_target_pairs={{0,1},{1,0},{2,3},{3,2},{4,5},{5,4},{6,7},{7,6},{8,9},{9,8},{10,11... | collective-permute-start | bytes 196616 | tf_op jit(solution)/shard_map/ppermute | solution.py:661
  87.4 2.4 %collective-permute-done.other_ref = f32[128,128]{1,0:T(8,128)S(1)} collective-permute-done((f32[128,128]{1,0:T(8,128)S(1)}, f32[128,128]{1,0:T(8,128)S(1)}, u32[]{:S(2)}, u32[]{:S(2)}) %collective-permute-start) | collective-permute-done | bytes 65568 | tf_op jit(solution)/shard_map/ppermute | solution.py:661
  89.8 0.0 copy-done
  89.8 0.0 copy-done.1
  89.8 0.0 copy-done.2
  89.8 0.0 copy-done.3
  89.8 0.0 copy-done.4
  89.8 0.0 copy-done.6
  89.8 0.0 copy-done.5
  89.8 0.0 copy-done.7
  89.8 1.6 %new_vectors.1 = (f32[1,8,4,256]{3,2,1,0:T(4,128)}, f32[1,8,4,256]{3,2,1,0:T(4,128)}, f32[1,8,4,256]{3,2,1,0:T(4,128)}) custom-call(s32[1]{0:T(128)S(6)} %and.4.parity_ref, f32[128,128]{1,0:T(8,128)S(1)} %get-tuple-element.25.half_ref, f32[128,128]{1,0:T(8,128)S(1)} %collective-permute-done.other_ref, f32[320,128]{1,0:T(8,128)S(1)} %bitcast.16, ...), custom_call_target="tpu_custom_call" | custom-call | flops 3000000000 | bytes 3000000 | tf_op jit(solution)/shard_map/new_vectors/pallas_call | solution.py:580
  91.4 0.0 all-to-all-done.3
  91.5 0.6 broadcast_multiply_fusion
  (1 shorter events, 0.0 us)
Async XLA Ops:
  53.2 21.9 %all-to-all-start.2 = ((f32[64,1,640]{2,1,0:T(1,128)}), f32[64,1,640]{2,1,0:T(1,128)S(1)}, u32[]{:S(2)}, u32[]{:S(2)}) async-start(f32[64,1,640]{2,1,0:T(1,128)} %bitcast.6), calls=%async_computation.2 | async-start | bytes 327680 | tf_op jit(solution)/shard_map/all_to_all | solution.py:602
  76.2 13.6 %copy-start = (f32[1,8,4,256]{3,2,1,0:T(4,128)S(1)}, f32[1,8,4,256]{3,2,1,0:T(4,128)}, u32[]{:S(2)}) copy-start(f32[1,8,4,256]{3,2,1,0:T(4,128)} %res_ref.1) | copy-start | bytes 98308
  76.2 13.6 %copy-start.1 = (f32[1,8,4,256]{3,2,1,0:T(4,128)S(1)}, f32[1,8,4,256]{3,2,1,0:T(4,128)}, u32[]{:S(2)}) copy-start(f32[1,8,4,256]{3,2,1,0:T(4,128)} %old_ref.1) | copy-start | bytes 98308
  76.2 13.6 %copy-start.2 = (f32[1,8,4,256]{3,2,1,0:T(4,128)S(1)}, f32[1,8,4,256]{3,2,1,0:T(4,128)}, u32[]{:S(2)}) copy-start(f32[1,8,4,256]{3,2,1,0:T(4,128)} %resp_ref.1) | copy-start | bytes 98308
  76.2 13.6 %copy-start.3 = (f32[1,2,16,256]{3,2,1,0:T(8,128)S(1)}, f32[1,2,16,256]{3,2,1,0:T(8,128)}, u32[]{:S(2)}) copy-start(f32[1,2,16,256]{3,2,1,0:T(8,128)} %form_ref.1) | copy-start | bytes 98308
  76.2 13.6 %copy-start.4 = (f32[3,64]{1,0:T(4,128)S(1)}, f32[3,64]{1,0:T(4,128)}, u32[]{:S(2)}) copy-start(f32[3,64]{1,0:T(4,128)} %pos_ref.1) | copy-start | bytes 2308
  76.2 13.6 %copy-start.6 = (f32[1,256]{1,0:T(1,128)S(1)}, f32[1,256]{1,0:T(1,128)}, u32[]{:S(2)}) copy-start(f32[1,256]{1,0:T(1,128)} %kin_ref.1) | copy-start | bytes 3076
  76.2 15.2 %all-to-all-start.3 = ((f32[8,128,128]{2,1,0:T(8,128)}), f32[8,128,128]{2,1,0:T(8,128)S(1)}, u32[]{:S(2)}, u32[]{:S(2)}) async-start(f32[8,128,128]{2,1,0:T(8,128)} %bitcast.8), calls=%async_computation.3 | async-start | bytes 1048576 | tf_op jit(solution)/shard_map/all_to_all | solution.py:604
  84.3 5.5 %copy-start.5 = (s32[1,256]{1,0:T(1,128)S(1)}, s32[1,256]{1,0:T(1,128)}, u32[]{:S(2)}) copy-start(s32[1,256]{1,0:T(1,128)} %index_ref.1) | copy-start | bytes 3076
  84.3 5.5 %copy-start.7 = (f32[1,8]{1,0:T(1,128)S(1)}, f32[1,8]{1,0:T(1,128)}, u32[]{:S(2)}) copy-start(f32[1,8]{1,0:T(1,128)} %energy_ref.1) | copy-start | bytes 100
  84.4 5.4 %collective-permute-start = (f32[128,128]{1,0:T(8,128)S(1)}, f32[128,128]{1,0:T(8,128)S(1)}, u32[]{:S(2)}, u32[]{:S(2)}) collective-permute-start(f32[128,128]{1,0:T(8,128)S(1)} %get-tuple-element.25.half_ref), channel_id=1, source_target_pairs={{0,1},{1,0},{2,3},{3,2},{4,5},{5,4},{6,7},{7,6},{8,9},{9,8},{10,11... | collective-permute-start | bytes 196616 | tf_op jit(solution)/shard_map/ppermute | solution.py:661

commit v7 on v6

--- a/solution.py
+++ b/solution.py
@@ -512,11 +512,40 @@
         half_ref[k * DEV : (k + 1) * DEV, :] = recv_ref[pl.ds(2 + k, DEV, stride=ROWS2), :]
 
 
-def finish_kernel(
-    parity_ref, half_ref, other_ref, recv_ref, scalars_ref, resp_ref, res_ref, old_ref, kin_ref, energy_ref, form_ref,
-    index_ref, pos_ref, next_ref, residual_ref, direction_ref,
+def half_term(half_ref, phases, form_ref):
+    form_re, form_im = form_ref[0, 0], form_ref[0, 1]
+    rows_re, rows_im = [[], []], [[], []]
+    for k in range(2):
+        z = dot3(split(half_ref[k * DEV : (k + 1) * DEV, :].T), phases)
+        for i in range(2):
+            for s in range(2):
+                a = i * 64 + s * 16
+                re_c, re_s = z[a : a + 16, :PW], z[a : a + 16, PW:]
+                im_c, im_s = z[a + 32 : a + 48, :PW], z[a + 32 : a + 48, PW:]
+                w_re = re_c + im_s
+                w_im = im_c - re_s
+                rows_re[s].append(
+                    jnp.sum(form_re * w_re - form_im * w_im, axis=0, keepdims=True)
+                )
+                rows_im[s].append(
+                    jnp.sum(form_re * w_im + form_im * w_re, axis=0, keepdims=True)
+                )
+    return [
+        [jnp.concatenate(rows[s], axis=0) for rows in (rows_re, rows_im)] for s in range(2)
+    ]
+
+
+def in_half(part, second):
+    zero = jnp.zeros_like(part)
+    return jnp.where(
+        second, jnp.concatenate([zero, part], axis=0), jnp.concatenate([part, zero], axis=0)
+    )
+
+
+def image_kernel(
+    parity_ref, half_ref, recv_ref, scalars_ref, res_ref, old_ref, kin_ref, energy_ref,
+    form_ref, index_ref, pos_ref, image_ref, phases_ref,
 ):
-    step = step_of(recv_ref, scalars_ref)
     beta = scalars_ref[:, 1:2]
     table = depth_table(by_z)
     table = split(jnp.concatenate([table[:64], table[64:]], axis=1))
@@ -530,38 +559,35 @@
             im_c, im_s = z[i * 32 + 16 : i * 32 + 32, :PW], z[i * 32 + 16 : i * 32 + 32, PW:]
             part = jnp.concatenate([re_c + im_s, im_c - re_s], axis=0)
             local = local + jnp.where(group == 4 * r + i, part, 0.0)
-
     phases = atom_phases(index_ref[...], pos_ref[...], by_z)
-    phases = split(jnp.concatenate([phases[:64], phases[64:]], axis=1))
-    form_re, form_im = form_ref[0, 0], form_ref[0, 1]
-    rows_re, rows_im = [[], []], [[], []]
-    for k in range(4):
-        rows = slice((k & 1) * DEV, (k & 1) * DEV + DEV)
-        mine = parity_ref[0] == (k >> 1)
-        values = jnp.where(mine, half_ref[rows, :], other_ref[rows, :]).T
-        z = dot3(split(values), phases)
-        for i in range(2):
-            for s in range(2):
-                a = i * 64 + s * 16
-                re_c, re_s = z[a : a + 16, :PW], z[a : a + 16, PW:]
-                im_c, im_s = z[a + 32 : a + 48, :PW], z[a + 32 : a + 48, PW:]
-                w_re = re_c + im_s
-                w_im = im_c - re_s
-                rows_re[s].append(
-                    jnp.sum(form_re * w_re - form_im * w_im, axis=0, keepdims=True)
-                )
-                rows_im[s].append(
-                    jnp.sum(form_re * w_im + form_im * w_re, axis=0, keepdims=True)
-                )
+    phases = jnp.concatenate([phases[:64], phases[64:]], axis=1)
+    phases_ref[...] = phases
+    mine = half_term(half_ref, split(phases), form_ref)
     weight = kin_ref[...] - row_to_col(energy_ref[...], NB)
     for s in range(2):
         for c in range(2):
             comp = 2 * s + c
-            nonlocal_term = jnp.concatenate((rows_re, rows_im)[c][s], axis=0)
+            direction = res_ref[0, :, comp, :] + beta * old_ref[0, :, comp, :]
+            place = c * 16 + s * 8
+            image_ref[comp] = (
+                weight * direction + local[place : place + 8]
+                + in_half(mine[s][c], parity_ref[0] == 1)
+            )
+
+
+def finish_kernel(
+    parity_ref, other_ref, recv_ref, scalars_ref, image_ref, phases_ref, resp_ref, res_ref,
+    old_ref, form_ref, next_ref, residual_ref, direction_ref,
+):
+    step = step_of(recv_ref, scalars_ref)
+    beta = scalars_ref[:, 1:2]
+    theirs = half_term(other_ref, split(phases_ref[...]), form_ref)
+    for s in range(2):
+        for c in range(2):
+            comp = 2 * s + c
             residual = res_ref[0, :, comp, :]
             direction = residual + beta * old_ref[0, :, comp, :]
-            place = c * 16 + s * 8
-            image = weight * direction + local[place : place + 8] + nonlocal_term
+            image = image_ref[comp] + in_half(theirs[s][c], parity_ref[0] == 0)
             direction_ref[0, :, comp, :] = direction
             next_ref[0, :, comp, :] = resp_ref[0, :, comp, :] + step * direction
             residual_ref[0, :, comp, :] = residual - step * image
@@ -659,12 +685,19 @@
     )(returned, scalars, base, slope)
     gathered = exchange(density, "kpool", 8, POINTS)
     other_half = lax.ppermute(half, "fft", MIRROR)
+    image, phases = call(
+        image_kernel, (shape_of(4, NB, PW), shape_of(DEV, 2 * PW)), "image",
+        flops=3_000_000_000, size=3_000_000, smem=(0,),
+    )(
+        parity, half, returned, scalars, residual, old_direction, kinetic, band_energy,
+        form_factor, sphere_index, atom_positions,
+    )
     outs = call(
         finish_kernel, (shape_of(1, NB, 4, PW),) * 3, "new_vectors",
-        flops=3_000_000_000, size=3_000_000, smem=(0,),
+        flops=1_000_000_000, size=1_000_000, smem=(0,),
     )(
-        parity, half, other_half, returned, scalars, response, residual, old_direction, kinetic, band_energy, form_factor,
-        sphere_index, atom_positions,
+        parity, other_half, returned, scalars, image, phases, response, residual, old_direction,
+        form_factor,
     )
     total = jnp.sum(gathered.reshape(8, 128, 128), axis=0) * scale
     return outs[0], outs[1], outs[2], total.reshape(4, 1, NG * NG)

time: 92.6 us -> 92.5 us (level)
    pallas_call x6 -> x7, Pallas kernels: 13.1 us -> 13.4 us  [run(): pl.pallas_call(kernel, out_shape=outs, in_specs=specs, out_specs=jax.tree...]
  transfers between devices with their start and end apart: 3 -> 3, of which waited for: 2 -> 3; matrix products, arithmetic and copies ran while one was open for 0% -> 0% of each run, Pallas kernels for 6% -> 6%
where the time goes in v7:
time: 92.5 us; the launch traced here: 91.9 us
  blocking collectives  46 us (50%)
  starting transfers between devices  26.2 us (28%)
  Pallas kernels  13.4 us (14%)
  waiting for transfers between devices  4.83 us (5%)
    all_to_all x1, blocking collectives, exchange(): lax.all_to_all(flat, axis, 0, 0, tiled=True, axis_index_groups=groups)  35.5 us
    all_to_all x1, starting transfers between devices, exchange(): lax.all_to_all(flat, axis, 0, 0, tiled=True, axis_index_groups=groups)  15.1 us
    pallas_call x7, Pallas kernels, run(): pl.pallas_call(kernel, out_shape=outs, in_specs=specs, out_specs=jax.tree...  13.4 us
    all_to_all x1, blocking collectives, exchange(): lax.all_to_all(values.reshape(parts, rows, 128), axis, 0, 0, tiled=True,...  10.5 us
    all_to_all x1, starting transfers between devices, exchange(): lax.all_to_all(values.reshape(parts, rows, 128), axis, 0, 0, tiled=True,...  8.13 us
    ppermute x1, starting transfers between devices, per_device(): other_half = lax.ppermute(half, 'fft', MIRROR)  3.02 us
    all_to_all x1, waiting for transfers between devices, exchange(): lax.all_to_all(flat, axis, 0, 0, tiled=True, axis_index_groups=groups)  2.9 us
  transfers between devices with their start and end apart: 3, of which 3 were waited for; matrix products, arithmetic and copies ran while one was open for 0% of the time, Pallas kernels for 6%

profile of v7, /device:TPU:1, one launch (start us, length us, event | category | flops | bytes accessed | tf_op | source)
XLA Modules:
  0.0 91.9 jit_solution(5576741496950646083)
XLA Ops:
  0.6 2.1 %lines_and_amplitudes.1 = f32[1056,128]{1,0:T(8,128)S(1)} custom-call(f32[1,8,4,256]{3,2,1,0:T(4,128)} %orb_hbm.1, f32[1,8,4,256]{3,2,1,0:T(4,128)} %resp_ref.1, f32[1,8,4,256]{3,2,1,0:T(4,128)} %res_ref.3, f32[1,8,4,256]{3,2,1,0:T(4,128)} %old_ref.3, f32[1,2,16,256]{3,2,1,0:T(8,128)} %form_ref.3, s32[1,256]{1,0:T(1,128)} %index_ref.1, f32[3,64]{1,0:T(4,128)} %pos_ref.1), custom_call_target="tpu_custom_call" | custom-call | flops 1 | bytes 1 | tf_op jit(solution)/shard_map/lines_and_amplitudes/pallas_call | solution.py:606
  2.8 10.5 %all_to_all.20 = f32[4,264,128]{2,1,0:T(8,128)S(1)} all-to-all(f32[4,264,128]{2,1,0:T(8,128)S(1)} %bitcast.11), channel_id=1, replica_groups={{2,3,0,1},{6,7,4,5},{10,11,8,9},{14,15,12,13},{18,19,16,17},{22,23,20,2..., dimensions={0} | all-to-all | bytes 1081344 | tf_op jit(solution)/shard_map/all_to_all | solution.py:630
  13.2 0.2 regroup.1
  13.4 35.5 %all_to_all.21 = f32[16,1,5248]{2,1,0:T(1,128)S(1)} all-to-all(f32[16,1,5248]{2,1,0:T(1,128)S(1)} %bitcast.14), channel_id=1, replica_groups={{32,36,40,44,48,52,56,60,0,4,8,12,16,20,24,28},{33,37,41,45,49,53,57,61..., dimensions={0} | all-to-all | bytes 671744 | tf_op jit(solution)/shard_map/all_to_all | solution.py:628
  48.9 4.3 %potential_and_coupling.1 = (f32[320,128]{1,0:T(8,128)}, f32[1024,128]{1,0:T(8,128)S(1)}, f32[8,128]{1,0:T(8,128)S(1)}) custom-call(f32[656,128]{1,0:T(8,128)S(1)} %bitcast.12, s32[1]{0:T(128)} %bitcast.atom_ref, s32[8,128]{1,0:T(8,128)} %bitcast.19, f32[4,1,4096]{2,1,0:T(1,128)} %pot_hbm.1, f32[1,8]{1,0:T(1,128)} %old_norm_hbm.1, f32[1,8,4,256]{3,2,1,0:T(4,128)} %res_ref.3, ...), custom_call_target="tpu_custom_call" | custom-call | flops 1 | bytes 1 | tf_op jit(solution)/shard_map/potential_and_coupling/pallas_call | solution.py:606
  53.2 15.1 %all-to-all-start.2 = ((f32[64,1,640]{2,1,0:T(1,128)}), f32[64,1,640]{2,1,0:T(1,128)S(1)}, u32[]{:S(2)}, u32[]{:S(2)}) async-start(f32[64,1,640]{2,1,0:T(1,128)} %bitcast.6), calls=%async_computation.2 | async-start | bytes 327680 | tf_op jit(solution)/shard_map/all_to_all | solution.py:628
  68.3 3.9 %density_terms.1 = (f32[128,128]{1,0:T(8,128)S(1)}, f32[1024,128]{1,0:T(8,128)S(1)}) custom-call(f32[656,128]{1,0:T(8,128)S(1)} %bitcast.13, f32[1024,128]{1,0:T(8,128)S(1)} %get-tuple-element.24.grid_ref), custom_call_target="tpu_custom_call" | custom-call | flops 3000000000 | bytes 3000000 | tf_op jit(solution)/shard_map/density_terms/pallas_call | solution.py:606
  72.3 2.9 %all-to-all-done.2 = f32[64,1,640]{2,1,0:T(1,128)S(1)} async-done(((f32[64,1,640]{2,1,0:T(1,128)}), f32[64,1,640]{2,1,0:T(1,128)S(1)}, u32[]{:S(2)}, u32[]{:S(2)}) %all-to-all-start.2) | async-done | bytes 163872 | tf_op jit(solution)/shard_map/all_to_all | solution.py:628
  75.2 1.0 %density.1 = (f32[1024,128]{1,0:T(8,128)}, f32[128,128]{1,0:T(8,128)S(1)}) custom-call(f32[320,128]{1,0:T(8,128)S(1)} %bitcast.15, f32[8,128]{1,0:T(8,128)S(1)} %get-tuple-element.23.scalars_ref, f32[128,128]{1,0:T(8,128)S(1)} %get-tuple-element.25.base_ref, f32[1024,128]{1,0:T(8,128)S(1)} %get-tuple-element.26.slope_ref), custom_call_target="tpu_custom_call" | custom-call | flops 1 | bytes 1 | tf_op jit(solution)/shard_map/density/pallas_call | solution.py:606
  76.2 0.0 copy-start
  76.2 0.0 copy-start.1
  76.2 0.0 copy-start.3
  76.2 0.0 copy-start.4
  76.2 0.0 copy-start.6
  76.2 8.1 %all-to-all-start.3 = ((f32[8,128,128]{2,1,0:T(8,128)}), f32[8,128,128]{2,1,0:T(8,128)S(1)}, u32[]{:S(2)}, u32[]{:S(2)}) async-start(f32[8,128,128]{2,1,0:T(8,128)} %bitcast.8), calls=%async_computation.3 | async-start | bytes 1048576 | tf_op jit(solution)/shard_map/all_to_all | solution.py:630
  84.3 0.0 copy-start.5
  84.3 0.0 copy-start.7
  84.3 0.0 copy-start.2
  84.3 3.0 %collective-permute-start = (f32[128,128]{1,0:T(8,128)S(1)}, f32[128,128]{1,0:T(8,128)S(1)}, u32[]{:S(2)}, u32[]{:S(2)}) collective-permute-start(f32[128,128]{1,0:T(8,128)S(1)} %get-tuple-element.27.half_ref), channel_id=1, source_target_pairs={{0,1},{1,0},{2,3},{3,2},{4,5},{5,4},{6,7},{7,6},{8,9},{9,8},{10,11... | collective-permute-start | bytes 196616 | tf_op jit(solution)/shard_map/ppermute | solution.py:687
  87.4 0.0 copy-done
  87.4 0.0 copy-done.1
  87.4 0.0 copy-done.3
  87.4 0.0 copy-done.4
  87.4 0.0 copy-done.6
  87.4 0.0 copy-done.5
  87.4 0.0 copy-done.7
  87.4 0.7 image.1
  88.1 1.6 %collective-permute-done.other_ref = f32[128,128]{1,0:T(8,128)S(1)} collective-permute-done((f32[128,128]{1,0:T(8,128)S(1)}, f32[128,128]{1,0:T(8,128)S(1)}, u32[]{:S(2)}, u32[]{:S(2)}) %collective-permute-start) | collective-permute-done | bytes 65568 | tf_op jit(solution)/shard_map/ppermute | solution.py:687
  89.8 0.0 copy-done.2
  89.8 1.1 %new_vectors.1 = (f32[1,8,4,256]{3,2,1,0:T(4,128)}, f32[1,8,4,256]{3,2,1,0:T(4,128)}, f32[1,8,4,256]{3,2,1,0:T(4,128)}) custom-call(s32[1]{0:T(128)S(6)} %and.4.parity_ref, f32[128,128]{1,0:T(8,128)S(1)} %collective-permute-done.other_ref, f32[320,128]{1,0:T(8,128)S(1)} %bitcast.17, f32[8,128]{1,0:T(8,128)S(1)} %get-tuple-element.23.scalars_ref, ...), custom_call_target="tpu_custom_call" | custom-call | flops 1000000000 | bytes 1000000 | tf_op jit(solution)/shard_map/new_vectors/pallas_call | solution.py:606
  90.9 0.3 all-to-all-done.3
  91.2 0.6 broadcast_multiply_fusion
  (1 shorter events, 0.0 us)
Async XLA Ops:
  53.2 21.9 %all-to-all-start.2 = ((f32[64,1,640]{2,1,0:T(1,128)}), f32[64,1,640]{2,1,0:T(1,128)S(1)}, u32[]{:S(2)}, u32[]{:S(2)}) async-start(f32[64,1,640]{2,1,0:T(1,128)} %bitcast.6), calls=%async_computation.2 | async-start | bytes 327680 | tf_op jit(solution)/shard_map/all_to_all | solution.py:628
  76.2 11.2 %copy-start = (f32[1,8,4,256]{3,2,1,0:T(4,128)S(1)}, f32[1,8,4,256]{3,2,1,0:T(4,128)}, u32[]{:S(2)}) copy-start(f32[1,8,4,256]{3,2,1,0:T(4,128)} %res_ref.3) | copy-start | bytes 98308
  76.2 11.2 %copy-start.1 = (f32[1,8,4,256]{3,2,1,0:T(4,128)S(1)}, f32[1,8,4,256]{3,2,1,0:T(4,128)}, u32[]{:S(2)}) copy-start(f32[1,8,4,256]{3,2,1,0:T(4,128)} %old_ref.3) | copy-start | bytes 98308
  76.2 11.2 %copy-start.3 = (f32[1,2,16,256]{3,2,1,0:T(8,128)S(1)}, f32[1,2,16,256]{3,2,1,0:T(8,128)}, u32[]{:S(2)}) copy-start(f32[1,2,16,256]{3,2,1,0:T(8,128)} %form_ref.3) | copy-start | bytes 98308
  76.2 11.2 %copy-start.4 = (f32[3,64]{1,0:T(4,128)S(1)}, f32[3,64]{1,0:T(4,128)}, u32[]{:S(2)}) copy-start(f32[3,64]{1,0:T(4,128)} %pos_ref.1) | copy-start | bytes 2308
  76.2 11.2 %copy-start.6 = (f32[1,256]{1,0:T(1,128)S(1)}, f32[1,256]{1,0:T(1,128)}, u32[]{:S(2)}) copy-start(f32[1,256]{1,0:T(1,128)} %kin_ref.1) | copy-start | bytes 3076
  76.2 15.0 %all-to-all-start.3 = ((f32[8,128,128]{2,1,0:T(8,128)}), f32[8,128,128]{2,1,0:T(8,128)S(1)}, u32[]{:S(2)}, u32[]{:S(2)}) async-start(f32[8,128,128]{2,1,0:T(8,128)} %bitcast.8), calls=%async_computation.3 | async-start | bytes 1048576 | tf_op jit(solution)/shard_map/all_to_all | solution.py:630
  84.3 3.1 %copy-start.5 = (s32[1,256]{1,0:T(1,128)S(1)}, s32[1,256]{1,0:T(1,128)}, u32[]{:S(2)}) copy-start(s32[1,256]{1,0:T(1,128)} %index_ref.1) | copy-start | bytes 3076
  84.3 3.1 %copy-start.7 = (f32[1,8]{1,0:T(1,128)S(1)}, f32[1,8]{1,0:T(1,128)}, u32[]{:S(2)}) copy-start(f32[1,8]{1,0:T(1,128)} %energy_ref.1) | copy-start | bytes 100
  84.3 5.4 %copy-start.2 = (f32[1,8,4,256]{3,2,1,0:T(4,128)S(1)}, f32[1,8,4,256]{3,2,1,0:T(4,128)}, u32[]{:S(2)}) copy-start(f32[1,8,4,256]{3,2,1,0:T(4,128)} %resp_ref.1) | copy-start | bytes 98308
  84.3 5.4 %collective-permute-start = (f32[128,128]{1,0:T(8,128)S(1)}, f32[128,128]{1,0:T(8,128)S(1)}, u32[]{:S(2)}, u32[]{:S(2)}) collective-permute-start(f32[128,128]{1,0:T(8,128)S(1)} %get-tuple-element.27.half_ref), channel_id=1, source_target_pairs={{0,1},{1,0},{2,3},{3,2},{4,5},{5,4},{6,7},{7,6},{8,9},{9,8},{10,11... | collective-permute-start | bytes 196616 | tf_op jit(solution)/shard_map/ppermute | solution.py:687
